TPU v7x, 32 devices: a whole 2x2x4 slice. The times are simulated.
32 devices in a mesh: scan: 4 (over y, core), ybrick: 8 (over z, x).
Axes of the slice: x: 2, y: 2, z: 4, core: 2. Of those that a mesh axis runs over, the one named last changes fastest.
Arguments:
- raw: bfloat16 [16, 1024, 2048], P(None, 'ybrick', 'scan'), may hold values from 0.099609375 to 4
- row_shift: int32 [16], replicated, may hold values from 0 to 255
- frac_index: int32 [16], replicated, may hold values from 0 to 15
- psf_y: float32 [65], replicated, may hold values from 0.05 to 1
- psf_x: float32 [65], replicated, may hold values from 0.05 to 1
Outputs:
- estimate: float32 [16, 1024, 2048], P('scan', 'ybrick')
All inputs are finite; a program needn't handle non-finite values.
Results may differ from a plain program's by a relative error of at most 0.0021.
Values may be sent and summed in bfloat16 or wider, within the bound.
No kernel may reach another device: no remote copies, remote signals or barrier semaphores. Data moves between devices by JAX's collectives and lax.ppermute only.
A program may use at most 128 MiB of HBM per device.

v0:
```python
import jax
import jax.numpy as jnp
from jax import lax
from jax.sharding import PartitionSpec as P

RADIUS = 32
ITERS = 2
NFRAC = 16


background = 0.5


def shifted_2(x, axis, by):
    devices = lax.axis_size(axis)
    pairs = [(i, i + by) for i in range(devices) if 0 <= i + by < devices]
    return lax.ppermute(x, axis, pairs)


def with_halo(x, sides, width):
    for axis, dim in sides:
        devices, length = (lax.axis_size(axis), x.shape[dim])
        up = [(i, (i + 1) % devices) for i in range(devices - 1)]
        down = [(j, i) for i, j in up]
        last = lax.slice_in_dim(x, length - width, length, axis=dim)
        initial = lax.slice_in_dim(x, 0, width, axis=dim)
        before = lax.ppermute(last, axis, up)
        after = lax.ppermute(initial, axis, down)
        x = jnp.concatenate([before, x, after], axis=dim)
    return x


def band_matrix(kernel, count_in, count_out, offset):
    inputs = jnp.arange(count_in, dtype=jnp.int32)[:, None]
    outputs = jnp.arange(count_out, dtype=jnp.int32)[None, :]
    onehot = jax.nn.one_hot(inputs - outputs + offset, kernel.shape[0], dtype=jnp.float32)
    return jnp.dot(onehot, kernel, precision=lax.Precision.HIGHEST)


def along_rows(source, matrix):
    return jnp.einsum("io,pix->pox", matrix, source, precision=lax.Precision.HIGHEST)


def along_columns(source, matrix):

    def per_frame(frame_data):
        height, width = frame_data.shape
        padded = jnp.pad(frame_data, ((0, 0), (128, 128)))
        blocks = padded.reshape(height, width // 128 + 2, 128)
        windows = jnp.concatenate([blocks[:, :-2], blocks[:, 1:-1], blocks[:, 2:]], axis=-1)
        return jnp.einsum("rbi,io->rbo", windows, matrix, precision=lax.Precision.HIGHEST).reshape(
            height, width
        )

    return lax.map(per_frame, source)


def step_bricks(moved, whole_bricks, power):
    shifted = shifted_2(moved, "ybrick", 2**power)
    taken = (whole_bricks // 2**power % 2 == 1)[:, None, None]
    return jnp.where(taken, shifted, moved)


def deskew_brick(stacked, rest, fraction, brick):
    weight = fraction.astype(jnp.float32) / NFRAC
    upper = lax.dynamic_slice_in_dim(stacked, brick - rest, brick, 0)
    lower = lax.dynamic_slice_in_dim(stacked, brick - rest - 1, brick, 0)
    return ((1.0 - weight) * upper + weight * lower).astype(jnp.bfloat16)


def local(raw, row_shift, frac_index, psf_y, psf_x):
    arranged = lax.all_to_all(raw, "scan", split_axis=0, concat_axis=2, tiled=True)
    group_planes = arranged.shape[0]
    brick = arranged.shape[1]
    first_plane = lax.axis_index("scan") * group_planes
    shifts = lax.dynamic_slice_in_dim(row_shift, first_plane, group_planes)
    fractions = lax.dynamic_slice_in_dim(frac_index, first_plane, group_planes)
    whole_bricks = shifts // brick
    rests = shifts % brick
    moved = arranged
    for power in range((lax.axis_size("ybrick") // 4 - 1).bit_length()):
        moved = step_bricks(moved, whole_bricks, power)
    previous = shifted_2(moved, "ybrick", 1)
    stacked = jnp.concatenate([previous, moved], axis=1).astype(jnp.float32)
    deskewed = jax.vmap(deskew_brick, in_axes=(0, 0, 0, None))(stacked, rests, fractions, brick)
    observed = deskewed.astype(jnp.float32) + background
    kernel_y = psf_y / jnp.sum(psf_y)
    kernel_x = psf_x / jnp.sum(psf_x)
    x_forward = band_matrix(kernel_x, 384, 128, RADIUS - 128)
    x_back = band_matrix(kernel_x[::-1], 384, 128, RADIUS - 128)
    y_back = band_matrix(kernel_y[::-1], brick + 2 * RADIUS, brick, 0)
    estimate = observed
    y_forward = band_matrix(kernel_y, brick + 2 * RADIUS, brick, 0)
    for turn_index in range(ITERS):
        extended = with_halo(estimate.astype(jnp.bfloat16), (("ybrick", 1),), RADIUS).astype(
            estimate.dtype
        )
        blurred = along_columns(along_rows(extended, y_forward), x_forward)
        ratio = observed / blurred
        ratio_wide = with_halo(ratio.astype(jnp.bfloat16), (("ybrick", 1),), RADIUS).astype(
            ratio.dtype
        )
        estimate = estimate * along_rows(along_columns(ratio_wide, x_back), y_back)
    return estimate


def solution(mesh):
    return jax.shard_map(
        local,
        mesh=mesh,
        in_specs=(P(None, "ybrick", "scan"), P(), P(), P(), P()),
        out_specs=P("scan", "ybrick", None),
        check_vma=False,
    )
```

profile of v0, /device:TPU:9, one launch (start us, length us, event | category | flops | bytes accessed | tf_op | source)
XLA Modules:
  0.0 561.3 jit_solution(16846393721652823199)
XLA Ops:
  0.0 28.9 %all_to_all.18 = bf16[16,128,512]{2,1,0:T(8,128)(2,1)S(1)} all-to-all(bf16[16,128,512]{2,1,0:T(8,128)(2,1)} %param.13), channel_id=1, replica_groups=mesh['scan'=4,'ybrick'=8] {'scan'}, dimensions={0} | all-to-all | bytes 4194304 | tf_op jit(solution)/shard_map/all_to_all | solution.py:72
  28.9 2.9 copy.86
  31.9 3.3 all_to_all.16
  35.1 3.1 collective-permute-start
  40.0 44.1 %collective-permute-done = bf16[4,128,2048]{2,1,0:T(8,128)(2,1)} collective-permute-done((bf16[4,128,2048]{2,1,0:T(8,128)(2,1)S(1)}, bf16[4,128,2048]{2,1,0:T(8,128)(2,1)}, u32[]{:S(2)}, u32[]{:S(2)}) %collective-permute-start) | collective-permute-done | bytes 2097184 | tf_op jit(solution)/shard_map/ppermute | solution.py:17
  84.1 3.2 broadcast_select_fusion
  93.3 7.6 %fusion.34 = f32[1,384,128]{2,0,1:T(1,128)S(1)} fusion(pred[384,128,65]{1,0,2:T(32,128)(4,1)S(1)} %iota_compare_fusion, f32[65]{0:T(128)S(1)} %copy-done.7, f32[]{:T(128)} %reduce_sum.19), kind=kOutput, calls=%fused_computation.47 | convolution fusion | flops 38338624 | bytes 3391752 | tf_op jit(solution)/shard_map/dot_general | solution.py:37
  101.1 34.4 %collective-permute-done.1 = bf16[4,128,2048]{2,1,0:T(8,128)(2,1)S(1)} collective-permute-done((bf16[4,128,2048]{2,1,0:T(8,128)(2,1)}, bf16[4,128,2048]{2,1,0:T(8,128)(2,1)S(1)}, u32[]{:S(2)}, u32[]{:S(2)}) %collective-permute-start.1) | collective-permute-done | bytes 2097184 | tf_op jit(solution)/shard_map/ppermute | solution.py:17
  135.4 5.7 %maximum_convert_fusion = f32[4,256,2048]{2,1,0:T(8,128)} fusion(bf16[4,128,2048]{2,1,0:T(8,128)(2,1)} %broadcast_select_fusion, bf16[4,128,2048]{2,1,0:T(8,128)(2,1)S(1)} %collective-permute-done.1), kind=kLoop, calls=%fused_computation.54 | loop fusion | flops 8388608 | bytes 12582912 | tf_op jit(solution)/shard_map/convert_element_type | solution.py:84
  143.7 16.5 %while.54 = (s32[]{:T(128)}, f32[4,256,2048]{2,1,0:T(8,128)}, s32[4,3]{1,0:T(4,128)S(1)}, f32[4,128,2048]{2,1,0:T(8,128)}, s32[]{:T(128)}) while((s32[]{:T(128)}, f32[4,256,2048]{2,1,0:T(8,128)}, s32[4,3]{1,0:T(4,128)S(1)}, f32[4,128,2048]{2,1,0:T(8,128)}, s32[]{:T(128)}) %tuple.161), condition=%wide.while_cond, body=%wide.while_body.sunk | while | flops 2 | bytes 2098793 | solution.py:66
  144.3 3.5 dynamic-slice_dynamic-update-slice_fusion.4
  148.5 3.5 dynamic-slice_dynamic-update-slice_fusion.4
  152.6 3.5 dynamic-slice_dynamic-update-slice_fusion.4
  156.7 3.5 dynamic-slice_dynamic-update-slice_fusion.4
  162.7 17.2 %while.55 = (s32[]{:T(128)}, f32[4,256,2048]{2,1,0:T(8,128)}, s32[4,3]{1,0:T(4,128)S(1)}, f32[4,128,2048]{2,1,0:T(8,128)}, s32[]{:T(128)}) while((s32[]{:T(128)}, f32[4,256,2048]{2,1,0:T(8,128)}, s32[4,3]{1,0:T(4,128)S(1)}, f32[4,128,2048]{2,1,0:T(8,128)}, s32[]{:T(128)}) %tuple.176), condition=%wide.while_cond.1, body=%wide.while_body.1.sunk | while | flops 2 | bytes 2098793 | solution.py:67
  163.4 3.7 dynamic-slice_dynamic-update-slice_fusion.5
  167.7 3.7 dynamic-slice_dynamic-update-slice_fusion.5
  172.0 3.6 dynamic-slice_dynamic-update-slice_fusion.5
  176.3 3.7 dynamic-slice_dynamic-update-slice_fusion.5
  179.9 6.0 %fusion.40 = (bf16[4,128,2048]{2,1,0:T(8,128)(2,1)S(1)}, bf16[4,128,2048]{2,1,0:T(8,128)(2,1)}) fusion(f32[4,128,2048]{2,1,0:T(8,128)} %get-tuple-element.236, f32[4]{0:T(128)S(1)} %get-tuple-element.352, f32[4,128,2048]{2,1,0:T(8,128)} %get-tuple-element.228, f32[4]{0:T(128)S(1)} %get-tuple-element.351), kind=kLoop, calls=%fused_computation.60 | loop fusion | flops 7340032 | bytes 12582944 | tf_op jit(solution)/shard_map/convert_element_type | solution.py:95
  187.9 4.7 collective-permute-start.3
  194.6 3.4 fusion.38
  198.0 9.7 %collective-permute-done.2 = bf16[4,32,2048]{2,1,0:T(8,128)(2,1)S(1)} collective-permute-done((bf16[4,32,2048]{2,1,0:T(8,128)(2,1)S(1)}, bf16[4,32,2048]{2,1,0:T(8,128)(2,1)S(1)}, u32[]{:S(2)}, u32[]{:S(2)}) %collective-permute-start.2) | collective-permute-done | bytes 524320 | tf_op jit(solution)/shard_map/ppermute | solution.py:27
  207.7 6.1 %collective-permute-done.3 = bf16[4,32,2048]{2,1,0:T(8,128)(2,1)S(1)} collective-permute-done((bf16[4,32,2048]{2,1,0:T(8,128)(2,1)S(1)}, bf16[4,32,2048]{2,1,0:T(8,128)(2,1)S(1)}, u32[]{:S(2)}, u32[]{:S(2)}) %collective-permute-start.3) | collective-permute-done | bytes 524320 | tf_op jit(solution)/shard_map/ppermute | solution.py:28
  213.9 6.0 %convolution_bitcast_fusion.1 = f32[4,128,2048]{1,2,0:T(8,128)} fusion(f32[192,128,1]{1,0,2:T(8,128)S(1)} %bitcast.113, bf16[4,32,2048]{2,1,0:T(8,128)(2,1)S(1)} %collective-permute-done.3, bf16[4,128,2048]{2,1,0:T(8,128)(2,1)S(1)} %get-tuple-element.349, bf16[4,32,2048]{2,1,0:T(8,128)(2,1)S(1)} %collective-permute-done.2), kind=kOutput, calls=%fused_computation.63 | convolution fusion | flops 2425356288 | bytes 7438336 | tf_op jit(solution)/shard_map/io,pix->pox/dot_general | solution.py:41
  222.4 56.8 %while.50 = (s32[]{:T(128)}, f32[4,128,2048]{2,1,0:T(8,128)}, f32[4,128,2048]{1,2,0:T(8,128)}, f32[384,128]{0,1:T(8,128)S(1)}, s32[]{:T(128)}, /*index=5*/f32[]{:T(128)}) while((s32[]{:T(128)}, f32[4,128,2048]{2,1,0:T(8,128)}, f32[4,128,2048]{1,2,0:T(8,128)}, f32[384,128]{0,1:T(8,128)S(1)}, s32[]{:T(128)}, /*index=5*/f32[]{:T(128)}) %tuple.177), condition=%wide.region_3.4_spmd, body=%wide.region_2.3_spmd.sunk | while | flops 1209532416 | bytes 25494092 | solution.py:55
  228.4 5.6 fusion.107
  242.6 5.6 fusion.107
  256.8 5.6 fusion.107
  270.9 5.6 fusion.107
  279.2 3.7 divide_convert_fusion.1
  285.8 4.4 collective-permute-start.5
  290.3 4.1 fusion.36
  294.4 12.1 %fusion.32 = f32[1,384,128]{2,0,1:T(1,128)S(1)} fusion(pred[384,128,65]{1,0,2:T(32,128)(4,1)} %copy-done, f32[65]{0:T(128)S(1)} %reverse.6, f32[]{:T(128)} %reduce_sum.19), kind=kOutput, calls=%fused_computation.45 | convolution fusion | flops 38338624 | bytes 3391752 | tf_op jit(solution)/shard_map/dot_general | solution.py:37
  308.5 3.5 collective-permute-done.5
  312.0 3.4 maximum_convert_fusion.1
  315.4 3.4 broadcast.83.clone
  318.8 42.1 %while.51 = (s32[]{:T(128)}, f32[4,192,2048]{2,1,0:T(8,128)}, f32[4,192,2048]{2,1,0:T(8,128)}, f32[384,128]{1,0:T(8,128)S(1)}, s32[]{:T(128)}, /*index=5*/f32[]{:T(128)}) while((s32[]{:T(128)}, f32[4,192,2048]{2,1,0:T(8,128)}, f32[4,192,2048]{2,1,0:T(8,128)}, f32[384,128]{1,0:T(8,128)S(1)}, s32[]{:T(128)}, /*index=5*/f32[]{:T(128)}) %tuple.179), condition=%wide.region_5.6_spmd, body=%wide.region_4.5_spmd.sunk | while | flops 1814298624 | bytes 32244300 | solution.py:55
  323.7 4.0 fusion.111
  334.1 4.0 fusion.111
  344.5 4.0 fusion.111
  354.9 4.0 fusion.111
  360.9 11.8 %fusion.79 = (bf16[4,128,2048]{2,1,0:T(8,128)(2,1)S(1)}, f32[4,128,2048]{2,1,0:T(8,128)}) fusion(f32[4,192,2048]{2,1,0:T(8,128)} %get-tuple-element.218, f32[192,128,1]{1,0,2:T(8,128)} %bitcast.111, bf16[4,128,2048]{2,1,0:T(8,128)(2,1)} %get-tuple-element.350), kind=kOutput, calls=%fused_computation.122 | convolution fusion | flops 2420113408 | bytes 14778368 | tf_op jit(solution)/shard_map/io,pix->pox/dot_general | solution.py:41
  374.7 4.3 collective-permute-start.7
  379.0 18.1 %collective-permute-done.6 = bf16[4,32,2048]{2,1,0:T(8,128)(2,1)} collective-permute-done((bf16[4,32,2048]{2,1,0:T(8,128)(2,1)S(1)}, bf16[4,32,2048]{2,1,0:T(8,128)(2,1)}, u32[]{:S(2)}, u32[]{:S(2)}) %collective-permute-start.6) | collective-permute-done | bytes 524320 | tf_op jit(solution)/shard_map/ppermute | solution.py:27
  397.1 3.7 collective-permute-done.7
  400.8 7.7 %convolution_bitcast_fusion = f32[4,128,2048]{1,2,0:T(8,128)} fusion(f32[192,128,1]{1,0,2:T(8,128)} %bitcast.114, bf16[4,32,2048]{2,1,0:T(8,128)(2,1)} %collective-permute-done.7, bf16[4,128,2048]{2,1,0:T(8,128)(2,1)S(1)} %get-tuple-element.381, bf16[4,32,2048]{2,1,0:T(8,128)(2,1)} %collective-permute-done.6), kind=kOutput, calls=%fused_computation.62 | convolution fusion | flops 2425356288 | bytes 7438336 | tf_op jit(solution)/shard_map/io,pix->pox/dot_general | solution.py:41
  411.0 57.3 %while.52 = (s32[]{:T(128)}, f32[4,128,2048]{2,1,0:T(8,128)}, f32[4,128,2048]{1,2,0:T(8,128)}, f32[384,128]{0,1:T(8,128)S(1)}, s32[]{:T(128)}, /*index=5*/f32[]{:T(128)}) while((s32[]{:T(128)}, f32[4,128,2048]{2,1,0:T(8,128)}, f32[4,128,2048]{1,2,0:T(8,128)}, f32[384,128]{0,1:T(8,128)S(1)}, s32[]{:T(128)}, /*index=5*/f32[]{:T(128)}) %tuple.178), condition=%wide.region_7.8_spmd, body=%wide.region_6.7_spmd.sunk | while | flops 1209532416 | bytes 25494092 | solution.py:55
  417.0 5.6 fusion.115
  431.4 5.6 fusion.115
  445.7 5.6 fusion.115
  459.9 5.6 fusion.115
  468.2 3.6 divide_convert_fusion
  473.9 4.3 collective-permute-start.9
  478.1 18.1 %collective-permute-done.8 = bf16[4,32,2048]{2,1,0:T(8,128)(2,1)S(1)} collective-permute-done((bf16[4,32,2048]{2,1,0:T(8,128)(2,1)S(1)}, bf16[4,32,2048]{2,1,0:T(8,128)(2,1)S(1)}, u32[]{:S(2)}, u32[]{:S(2)}) %collective-permute-start.8) | collective-permute-done | bytes 524320 | tf_op jit(solution)/shard_map/ppermute | solution.py:27
  496.2 3.6 collective-permute-done.9
  499.8 3.4 maximum_convert_fusion.2
  503.3 3.4 broadcast.83
  506.7 41.9 %while.53 = (s32[]{:T(128)}, f32[4,192,2048]{2,1,0:T(8,128)}, f32[4,192,2048]{2,1,0:T(8,128)}, f32[384,128]{1,0:T(8,128)S(1)}, s32[]{:T(128)}, /*index=5*/f32[]{:T(128)}) while((s32[]{:T(128)}, f32[4,192,2048]{2,1,0:T(8,128)}, f32[4,192,2048]{2,1,0:T(8,128)}, f32[384,128]{1,0:T(8,128)S(1)}, s32[]{:T(128)}, /*index=5*/f32[]{:T(128)}) %tuple.180), condition=%wide.region_9.10_spmd, body=%wide.region_8.9_spmd.sunk | while | flops 1814298624 | bytes 32244300 | solution.py:55
  511.7 4.0 fusion.119
  522.1 4.0 fusion.119
  532.6 4.0 fusion.119
  543.0 4.0 fusion.119
  548.6 12.5 %bitcast_multiply_fusion = f32[4,128,2048]{2,1,0:T(8,128)} fusion(f32[4,128,2048]{2,1,0:T(8,128)} %get-tuple-element.382, f32[4,192,2048]{2,1,0:T(8,128)} %get-tuple-element.220, f32[192,128,1]{1,0,2:T(8,128)S(1)} %bitcast.112), kind=kOutput, calls=%fused_computation.55 | convolution fusion | flops 2416967680 | bytes 14778368 | tf_op jit(solution)/shard_map/io,pix->pox/dot_general | solution.py:41
  (177 shorter events, 155.9 us)
Async XLA Ops:
  28.9 9.3 %copy-start.4 = (s32[16]{0:T(128)S(1)}, s32[16]{0:T(128)}, u32[]{:S(2)}) copy-start(s32[16]{0:T(128)} %param.14) | copy-start | bytes 196
  28.9 9.7 %copy-start.6 = (f32[65]{0:T(128)S(1)}, f32[65]{0:T(128)}, u32[]{:S(2)}) copy-start(f32[65]{0:T(128)} %param.16) | copy-start | bytes 784
  28.9 10.3 %copy-start.7 = (f32[65]{0:T(128)S(1)}, f32[65]{0:T(128)}, u32[]{:S(2)}) copy-start(f32[65]{0:T(128)} %param.17) | copy-start | bytes 784
  35.1 49.0 %collective-permute-start = (bf16[4,128,2048]{2,1,0:T(8,128)(2,1)S(1)}, bf16[4,128,2048]{2,1,0:T(8,128)(2,1)}, u32[]{:S(2)}, u32[]{:S(2)}) collective-permute-start(bf16[4,128,2048]{2,1,0:T(8,128)(2,1)S(1)} %all_to_all.16), channel_id=1, source_target_pairs={{0,1},{1,2},{2,3},{3,4},{4,5},{5,6},{6,7},{8,9},{9,10},{10,11},{11... | collective-permute-start | bytes 6291464 | tf_op jit(solution)/shard_map/ppermute | solution.py:17
  87.3 48.1 %collective-permute-start.1 = (bf16[4,128,2048]{2,1,0:T(8,128)(2,1)}, bf16[4,128,2048]{2,1,0:T(8,128)(2,1)S(1)}, u32[]{:S(2)}, u32[]{:S(2)}) collective-permute-start(bf16[4,128,2048]{2,1,0:T(8,128)(2,1)} %broadcast_select_fusion), channel_id=1, source_target_pairs={{0,1},{1,2},{2,3},{3,4},{4,5},{5,6},{6,7},{8,9},{9,10},{10,11},{11... | collective-permute-start | bytes 6291464 | tf_op jit(solution)/shard_map/ppermute | solution.py:17
  91.6 1.7 copy-start
  93.3 7.7 %copy-start.5 = (s32[16]{0:T(128)S(1)}, s32[16]{0:T(128)}, u32[]{:S(2)}) copy-start(s32[16]{0:T(128)} %param.15) | copy-start | bytes 196
  186.0 21.8 %collective-permute-start.2 = (bf16[4,32,2048]{2,1,0:T(8,128)(2,1)S(1)}, bf16[4,32,2048]{2,1,0:T(8,128)(2,1)S(1)}, u32[]{:S(2)}, u32[]{:S(2)}) collective-permute-start(bf16[4,32,2048]{2,1,0:T(8,128)(2,1)S(1)} %get-tuple-element.377), channel_id=1, source_target_pairs={{0,1},{1,2},{2,3},{3,4},{4,5},{5,6},{6,7},{8,9},{9,10},{10,11},{11... | collective-permute-start | bytes 1572872 | tf_op jit(solution)/shard_map/ppermute | solution.py:27
  187.9 25.9 %collective-permute-start.3 = (bf16[4,32,2048]{2,1,0:T(8,128)(2,1)S(1)}, bf16[4,32,2048]{2,1,0:T(8,128)(2,1)S(1)}, u32[]{:S(2)}, u32[]{:S(2)}) collective-permute-start(bf16[4,32,2048]{2,1,0:T(8,128)(2,1)S(1)} %get-tuple-element.378), channel_id=1, source_target_pairs={{1,0},{2,1},{3,2},{4,3},{5,4},{6,5},{7,6},{9,8},{10,9},{11,10},{12... | collective-permute-start | bytes 1572872 | tf_op jit(solution)/shard_map/ppermute | solution.py:28
  193.4 1.2 copy-start.1
  198.0 21.8 %copy-start.8 = (f32[1,192,128]{2,0,1:T(1,128)}, f32[1,192,128]{2,0,1:T(1,128)S(1)}, u32[]{:S(2)}) copy-start(f32[1,192,128]{2,0,1:T(1,128)S(1)} %fusion.38) | copy-start | bytes 294916
  279.2 11.1 %copy-start.2 = (pred[192,128,65]{1,0,2:T(32,128)(4,1)S(1)}, pred[192,128,65]{1,0,2:T(32,128)(4,1)}, u32[]{:S(2)}) copy-start(pred[192,128,65]{1,0,2:T(32,128)(4,1)} %copy-done.1) | copy-start | bytes 4792324
  283.9 24.6 %collective-permute-start.4 = (bf16[4,32,2048]{2,1,0:T(8,128)(2,1)}, bf16[4,32,2048]{2,1,0:T(8,128)(2,1)S(1)}, u32[]{:S(2)}, u32[]{:S(2)}) collective-permute-start(bf16[4,32,2048]{2,1,0:T(8,128)(2,1)} %get-tuple-element.375), channel_id=1, source_target_pairs={{0,1},{1,2},{2,3},{3,4},{4,5},{5,6},{6,7},{8,9},{9,10},{10,11},{11... | collective-permute-start | bytes 1572872 | tf_op jit(solution)/shard_map/ppermute | solution.py:27
  285.8 26.2 %collective-permute-start.5 = (bf16[4,32,2048]{2,1,0:T(8,128)(2,1)}, bf16[4,32,2048]{2,1,0:T(8,128)(2,1)S(1)}, u32[]{:S(2)}, u32[]{:S(2)}) collective-permute-start(bf16[4,32,2048]{2,1,0:T(8,128)(2,1)} %get-tuple-element.376), channel_id=1, source_target_pairs={{1,0},{2,1},{3,2},{4,3},{5,4},{6,5},{7,6},{9,8},{10,9},{11,10},{12... | collective-permute-start | bytes 1572872 | tf_op jit(solution)/shard_map/ppermute | solution.py:28
  372.8 24.3 %collective-permute-start.6 = (bf16[4,32,2048]{2,1,0:T(8,128)(2,1)S(1)}, bf16[4,32,2048]{2,1,0:T(8,128)(2,1)}, u32[]{:S(2)}, u32[]{:S(2)}) collective-permute-start(bf16[4,32,2048]{2,1,0:T(8,128)(2,1)S(1)} %get-tuple-element.373), channel_id=1, source_target_pairs={{0,1},{1,2},{2,3},{3,4},{4,5},{5,6},{6,7},{8,9},{9,10},{10,11},{11... | collective-permute-start | bytes 1572872 | tf_op jit(solution)/shard_map/ppermute | solution.py:27
  374.7 26.1 %collective-permute-start.7 = (bf16[4,32,2048]{2,1,0:T(8,128)(2,1)S(1)}, bf16[4,32,2048]{2,1,0:T(8,128)(2,1)}, u32[]{:S(2)}, u32[]{:S(2)}) collective-permute-start(bf16[4,32,2048]{2,1,0:T(8,128)(2,1)S(1)} %get-tuple-element.374), channel_id=1, source_target_pairs={{1,0},{2,1},{3,2},{4,3},{5,4},{6,5},{7,6},{9,8},{10,9},{11,10},{12... | collective-permute-start | bytes 1572872 | tf_op jit(solution)/shard_map/ppermute | solution.py:28
  471.9 24.3 %collective-permute-start.8 = (bf16[4,32,2048]{2,1,0:T(8,128)(2,1)S(1)}, bf16[4,32,2048]{2,1,0:T(8,128)(2,1)S(1)}, u32[]{:S(2)}, u32[]{:S(2)}) collective-permute-start(bf16[4,32,2048]{2,1,0:T(8,128)(2,1)S(1)} %get-tuple-element.371), channel_id=1, source_target_pairs={{0,1},{1,2},{2,3},{3,4},{4,5},{5,6},{6,7},{8,9},{9,10},{10,11},{11... | collective-permute-start | bytes 1572872 | tf_op jit(solution)/shard_map/ppermute | solution.py:27
  473.9 26.0 %collective-permute-start.9 = (bf16[4,32,2048]{2,1,0:T(8,128)(2,1)S(1)}, bf16[4,32,2048]{2,1,0:T(8,128)(2,1)S(1)}, u32[]{:S(2)}, u32[]{:S(2)}) collective-permute-start(bf16[4,32,2048]{2,1,0:T(8,128)(2,1)S(1)} %get-tuple-element.372), channel_id=1, source_target_pairs={{1,0},{2,1},{3,2},{4,3},{5,4},{6,5},{7,6},{9,8},{10,9},{11,10},{12... | collective-permute-start | bytes 1572872 | tf_op jit(solution)/shard_map/ppermute | solution.py:28
  506.7 41.9 %copy-start.3 = (f32[1,192,128]{2,0,1:T(1,128)S(1)}, f32[1,192,128]{2,0,1:T(1,128)}, u32[]{:S(2)}) copy-start(f32[1,192,128]{2,0,1:T(1,128)} %fusion.36) | copy-start | bytes 294916
where the time goes:
time: 567 us; the launch traced here: 561 us
  local copies, waits for them, and re-layouts  181 us (32%)
  waiting for transfers between devices  143 us (25%)
  matrix products  142 us (25%)
  other arithmetic  33.4 us (6%)
  starting transfers between devices  30.8 us (5%)
  blocking collectives  28.9 us (5%)
    ppermute x2, waiting for transfers between devices, shifted_2(): return lax.ppermute(x, axis, pairs)  78.4 us
    dot_general x16, matrix products, per_frame(): jnp.einsum('rbi,io->rbo', windows, matrix, precision=lax.Precision.HIGHEST)  77 us
    ppermute x4, waiting for transfers between devices, with_halo(): before = lax.ppermute(last, axis, up)  47.8 us
    dot_general x4, matrix products, along_rows(): jnp.einsum('io,pix->pox', matrix, source, precision=lax.Precision.HIGHEST)  37.9 us
    gather x24, local copies, waits for them, and re-layouts  33.7 us
    dynamic_update_slice x24, local copies, waits for them, and re-layouts, along_columns(): return lax.map(per_frame, source)  31.3 us
    all_to_all x1, blocking collectives, local(): lax.all_to_all(raw, 'scan', split_axis=0, concat_axis=2, tiled=True)  28.9 us
    dot_general x4, matrix products, band_matrix(): return jnp.dot(onehot, kernel, precision=lax.Precision.HIGHEST)  27.2 us
  transfers between devices with their start and end apart: 10, of which 10 were waited for; matrix products, arithmetic and copies ran while one was open for 6% of the time, Pallas kernels for 0%

commit v1 on v0

--- a/solution.py
+++ b/solution.py
@@ -1,14 +1,25 @@
+import functools
+
 import jax
 import jax.numpy as jnp
 from jax import lax
+from jax.experimental import pallas as pl
+from jax.experimental.pallas import tpu as pltpu
 from jax.sharding import PartitionSpec as P
 
 RADIUS = 32
 ITERS = 2
 NFRAC = 16
-
-
-background = 0.5
+BACKGROUND = 0.5
+
+HALO = 2 * ITERS * RADIUS
+ROWS = 192
+COLS = 256
+MARGIN = 128
+ALIGN = 16
+TINY = 1e-30
+VMEM_BYTES = 40 * 2**20
+TALL = 512
 
 
 def shifted_2(x, axis, by):
@@ -68,7 +79,7 @@
     return ((1.0 - weight) * upper + weight * lower).astype(jnp.bfloat16)
 
 
-def local(raw, row_shift, frac_index, psf_y, psf_x):
+def by_bricks(raw, row_shift, frac_index, psf_y, psf_x):
     arranged = lax.all_to_all(raw, "scan", split_axis=0, concat_axis=2, tiled=True)
     group_planes = arranged.shape[0]
     brick = arranged.shape[1]
@@ -83,7 +94,7 @@
     previous = shifted_2(moved, "ybrick", 1)
     stacked = jnp.concatenate([previous, moved], axis=1).astype(jnp.float32)
     deskewed = jax.vmap(deskew_brick, in_axes=(0, 0, 0, None))(stacked, rests, fractions, brick)
-    observed = deskewed.astype(jnp.float32) + background
+    observed = deskewed.astype(jnp.float32) + BACKGROUND
     kernel_y = psf_y / jnp.sum(psf_y)
     kernel_x = psf_x / jnp.sum(psf_x)
     x_forward = band_matrix(kernel_x, 384, 128, RADIUS - 128)
@@ -104,6 +115,291 @@
     return estimate
 
 
+def column_windows(width):
+    found = []
+    for start in range(0, width, COLS):
+        count = min(COLS, width - start)
+        low, high = max(start - MARGIN, 0), min(start + count + MARGIN, width)
+        found.append((start, count, low, high, low - (start - MARGIN)))
+    return found
+
+
+def place_in_chip():
+    scan = lax.axis_index("scan")
+    return scan // 2, scan % 2, lax.axis_index("ybrick")
+
+
+def source_of(step, bricks):
+    y, _, brick = place_in_chip()
+    core = y ^ (step // bricks)
+    return core, brick ^ (step % bricks) ^ (core * (bricks // 2))
+
+
+def plane_kernel(bricks, row_shift, frac_index, *refs):
+    pieces, refs = refs[: 2 * bricks], refs[2 * bricks :]
+    side, x_forward, x_back, y_forward, y_back = refs[:5]
+    outs, refs = refs[5 : 5 + bricks], refs[5 + bricks :]
+    raw, observed, estimate, blur_in, back_in, wide, ratio, arrived = refs
+    y, core, brick_index = place_in_chip()
+    plane = y * bricks + brick_index
+    shift, fraction = row_shift[plane], frac_index[plane]
+    _, brick, own = pieces[0].shape
+    rows, width = observed.shape
+    lead = raw.shape[0] - rows
+    windows = column_windows(width)
+    tiles = [(r, min(ROWS, rows - r)) for r in range(0, rows, ROWS)]
+    begin = core * HALO
+
+    copies = []
+    for step in range(2 * bricks):
+        source_core, source_brick = source_of(step, bricks)
+        here = pl.ds(pl.multiple_of(lead + source_brick * brick, ALIGN), brick)
+        there = pl.ds(pl.multiple_of(begin + source_core * own, 128), own)
+        copies.append((pieces[step].at[0], raw.at[here, there]))
+    there = pl.ds(pl.multiple_of((1 - core) * 2 * own, 128), HALO)
+    copies.append((side, raw.at[pl.ds(lead, rows), there]))
+    copies = [
+        pltpu.make_async_copy(source, target, arrived.at[i])
+        for i, (source, target) in enumerate(copies)
+    ]
+    for copy in copies:
+        copy.start()
+    raw[:lead, :] = jnp.zeros((lead, width), raw.dtype)
+    edge = jnp.zeros((RADIUS, width), blur_in.dtype)
+    for buffer in (blur_in, back_in):
+        buffer[:RADIUS, :] = edge
+        buffer[RADIUS + rows :, :] = edge
+
+    weight = fraction.astype(jnp.float32) / NFRAC
+    first = lead - shift - 1
+    base = (first // ALIGN) * ALIGN
+    depth = ROWS + ALIGN
+    ahead = lax.broadcasted_iota(jnp.int32, (ROWS, depth), 1) - (
+        lax.broadcasted_iota(jnp.int32, (ROWS, depth), 0) + (first - base)
+    )
+    mixing = jnp.where(ahead == 0, weight, jnp.where(ahead == 1, 1.0 - weight, 0.0))
+    mixing = mixing.astype(jnp.bfloat16)
+    for copy in copies:
+        copy.wait()
+    for r, count in tiles:
+        window = raw[pl.ds(pl.multiple_of(base + r, ALIGN), count + ALIGN), :]
+        moved = jnp.dot(
+            mixing[:count, : count + ALIGN], window, preferred_element_type=jnp.float32
+        )
+        level = moved.astype(jnp.bfloat16).astype(jnp.float32) + BACKGROUND
+        observed[r : r + count, :] = level
+        blur_in[RADIUS + r : RADIUS + r + count, :] = level.astype(jnp.bfloat16)
+
+    for turn in range(ITERS):
+        for r, count in tiles:
+            wide[r : r + count, :] = jnp.dot(
+                y_forward[:count, : count + 2 * RADIUS],
+                blur_in[r : r + count + 2 * RADIUS, :],
+                preferred_element_type=jnp.float32,
+            ).astype(jnp.bfloat16)
+        for r in range(0, rows, TALL):
+            tall = slice(r, r + TALL)
+            for start, count, low, high, row in windows:
+                blurred = jnp.dot(
+                    wide[tall, low:high],
+                    x_forward[row : row + high - low, :count],
+                    preferred_element_type=jnp.float32,
+                )
+                top = observed[tall, start : start + count]
+                ratio[tall, start : start + count] = (top / jnp.maximum(blurred, TINY)).astype(
+                    jnp.bfloat16
+                )
+            for start, count, low, high, row in windows:
+                back_in[RADIUS + r : RADIUS + r + TALL, start : start + count] = jnp.dot(
+                    ratio[tall, low:high],
+                    x_back[row : row + high - low, :count],
+                    preferred_element_type=jnp.float32,
+                ).astype(jnp.bfloat16)
+        for r, count in tiles:
+            correction = jnp.dot(
+                y_back[:count, : count + 2 * RADIUS],
+                back_in[r : r + count + 2 * RADIUS, :],
+                preferred_element_type=jnp.float32,
+            )
+            before = observed if turn == 0 else estimate
+            updated = before[r : r + count, :] * correction
+            estimate[r : r + count, :] = updated
+            if turn < ITERS - 1:
+                blur_in[RADIUS + r : RADIUS + r + count, :] = updated.astype(jnp.bfloat16)
+    first_out = core * (bricks // 2) + brick_index % (bricks // 2)
+    here = pl.ds(pl.multiple_of(begin, 128), 2 * own)
+    for k in range(bricks):
+        start = pl.multiple_of((first_out ^ k) * brick, ALIGN)
+        squared = jnp.square(estimate[pl.ds(start, brick), here])
+        outs[k][...] = jnp.square(squared).astype(outs[k].dtype)
+
+
+def band_kernel(taps, x_forward, x_back, y_forward, y_back):
+    row_sets = ((2, y_forward, 0, 0), (3, y_back, 0, 0), (1, x_forward, 1, 2), (0, x_back, 1, 2))
+    for row, out, lead_blocks, spare_blocks in row_sets:
+        count, width = out.shape
+        line = taps[row : row + 1, :]
+        line = line / jnp.sum(line)
+        whole = width * (1 + lead_blocks + spare_blocks)
+        line = jnp.concatenate(
+            [line, jnp.zeros((1, whole - line.shape[1]), jnp.float32)], axis=1
+        )
+        begin = lead_blocks * width - lead_blocks * (MARGIN + RADIUS)
+        band = pltpu.roll(
+            jnp.broadcast_to(line, (count, whole)), begin, 1, stride=1, stride_axis=0
+        )
+        out[...] = band[:, lead_blocks * width : (1 + lead_blocks) * width].astype(out.dtype)
+
+
+def band_matrices(psf_y, psf_x):
+    rows = jnp.stack([psf_x, psf_x[::-1], psf_y, psf_y[::-1]])
+    rows = jnp.pad(rows, ((0, 0), (0, 128 - rows.shape[1])))
+    vmem = pl.BlockSpec(memory_space=pltpu.VMEM)
+    shapes = [(COLS + 2 * MARGIN, COLS)] * 2 + [(ROWS, ROWS + 2 * RADIUS)] * 2
+    return pl.pallas_call(
+        band_kernel,
+        out_shape=[jax.ShapeDtypeStruct(shape, jnp.bfloat16) for shape in shapes],
+        in_specs=[vmem],
+        out_specs=[vmem] * 4,
+        compiler_params=pltpu.CompilerParams(vmem_limit_bytes=VMEM_BYTES),
+        name="band_matrices",
+    )(rows)
+
+
+def deconvolve_plane(tables, pieces, side, matrices, lead):
+    bricks = len(pieces) // 2
+    _, brick, own = pieces[0].shape
+    rows, width = bricks * brick, 2 * own + HALO
+    vmem = pl.BlockSpec(memory_space=pltpu.VMEM)
+    smem = pl.BlockSpec(memory_space=pltpu.SMEM)
+    anywhere = pl.BlockSpec(memory_space=pl.ANY)
+    return pl.pallas_call(
+        functools.partial(plane_kernel, bricks),
+        out_shape=[jax.ShapeDtypeStruct((brick, 2 * own), jnp.bfloat16)] * bricks,
+        in_specs=[smem] * 2 + [anywhere] * (2 * bricks + 1) + [vmem] * 4,
+        out_specs=[vmem] * bricks,
+        scratch_shapes=[
+            pltpu.VMEM((lead + rows, width), jnp.bfloat16),
+            pltpu.VMEM((rows, width), jnp.float32),
+            pltpu.VMEM((rows, width), jnp.float32),
+            pltpu.VMEM((rows + 2 * RADIUS, width), jnp.bfloat16),
+            pltpu.VMEM((rows + 2 * RADIUS, width), jnp.bfloat16),
+            pltpu.VMEM((rows, width), jnp.bfloat16),
+            pltpu.VMEM((rows, width), jnp.bfloat16),
+            pltpu.SemaphoreType.DMA((2 * bricks + 1,)),
+        ],
+        compiler_params=pltpu.CompilerParams(vmem_limit_bytes=VMEM_BYTES),
+        name="deconvolve_plane",
+    )(*tables, *pieces, side, *matrices)
+
+
+def edges_kernel(*refs):
+    pieces, out, arrived = refs[:-2], refs[-2], refs[-1]
+    bricks = len(pieces) // 2
+    _, brick, own = pieces[0].shape
+    _, core, _ = place_in_chip()
+    column = pl.ds(pl.multiple_of((1 - core) * (own - HALO), 128), HALO)
+    for group in range(2):
+
+        @pl.when(source_of(group * bricks, bricks)[0] == 1 - core)
+        def _(group=group):
+            copies = []
+            for k in range(bricks):
+                step = group * bricks + k
+                start = pl.multiple_of(source_of(step, bricks)[1] * brick, ALIGN)
+                copies.append(
+                    pltpu.make_async_copy(
+                        pieces[step].at[0, :, column], out.at[pl.ds(start, brick), :], arrived.at[k]
+                    )
+                )
+            for copy in copies:
+                copy.start()
+            for copy in copies:
+                copy.wait()
+
+
+def edges(pieces):
+    bricks = len(pieces) // 2
+    _, brick, _ = pieces[0].shape
+    return pl.pallas_call(
+        edges_kernel,
+        out_shape=jax.ShapeDtypeStruct((bricks * brick, HALO), jnp.bfloat16),
+        in_specs=[pl.BlockSpec(memory_space=pl.ANY)] * (2 * bricks),
+        out_specs=pl.BlockSpec(memory_space=pltpu.VMEM),
+        scratch_shapes=[pltpu.SemaphoreType.DMA((bricks,))],
+        compiler_params=pltpu.CompilerParams(vmem_limit_bytes=VMEM_BYTES),
+        name="edges",
+    )(*pieces)
+
+
+def place_kernel(*refs):
+    pieces, out = refs[:-1], refs[-1]
+    width = pieces[0].shape[1]
+    group = len(pieces) // 2
+    for k, piece in enumerate(pieces):
+        source = lax.axis_index("ybrick") ^ k
+
+        @pl.when(source % group == pl.program_id(0))
+        def _(piece=piece, source=source):
+            here = pl.ds(pl.multiple_of((source // group) * width, 128), width)
+            out[0, :, here] = jnp.sqrt(jnp.sqrt(piece[...].astype(out.dtype)))
+
+
+def place_planes(pieces):
+    brick, width = pieces[0].shape
+    group = len(pieces) // 2
+    return pl.pallas_call(
+        place_kernel,
+        grid=(group,),
+        out_shape=jax.ShapeDtypeStruct((group, brick, 2 * width), jnp.float32),
+        in_specs=[pl.BlockSpec(memory_space=pltpu.VMEM)] * len(pieces),
+        out_specs=pl.BlockSpec((1, brick, 2 * width), lambda i: (i, 0, 0)),
+        compiler_params=pltpu.CompilerParams(vmem_limit_bytes=VMEM_BYTES),
+        name="place_planes",
+    )(*pieces)
+
+
+def by_planes(raw, row_shift, frac_index, psf_y, psf_x):
+    planes, brick, own = raw.shape
+    bricks = lax.axis_size("ybrick")
+    half = bricks // 2
+    lead = bricks * brick // 4
+    matrices = band_matrices(psf_y, psf_x)
+
+    _, core, b = place_in_chip()
+    devices = [(y, c, i) for y in range(2) for c in range(2) for i in range(bricks)]
+    pieces = []
+    for step in range(2 * bricks):
+        turn, k = step // bricks, step % bricks
+        plane = (core ^ turn) * bricks + (b ^ k ^ (core * half))
+        piece = lax.dynamic_slice_in_dim(raw, plane, 1, 0)
+        route = []
+        for y, c, i in devices:
+            target = (2 * (c ^ turn) + y) * bricks + (i ^ k ^ (c * half))
+            route.append(((2 * y + c) * bricks + i, target))
+        pieces.append(lax.ppermute(piece, ("scan", "ybrick"), route))
+    side = lax.ppermute(edges(pieces), "scan", [(s, s ^ 1) for s in range(4)])
+    done = deconvolve_plane((row_shift, frac_index), pieces, side, matrices, lead)
+
+    arrived = []
+    for k in range(bricks):
+        route = []
+        for y, c, i in devices:
+            target = (2 * y + i // half) * bricks + ((c * half + i % half) ^ k)
+            route.append(((2 * y + c) * bricks + i, target))
+        arrived.append(lax.ppermute(done[k], ("scan", "ybrick"), route))
+    return place_planes(arrived)
+
+
+def local(raw, row_shift, frac_index, psf_y, psf_x):
+    planes, brick, own = raw.shape
+    bricks, scans = lax.axis_size("ybrick"), lax.axis_size("scan")
+    fits = scans == 4 and planes == 2 * bricks and bricks >= 4 and bricks & (bricks - 1) == 0
+    fits = fits and brick % ALIGN == 0 and own % HALO == 0 and bricks * brick % TALL == 0
+    plan = by_planes if fits else by_bricks
+    return plan(raw, row_shift, frac_index, psf_y, psf_x)
+
+
 def solution(mesh):
     return jax.shard_map(
         local,

time: 567 us -> 123 us (0.22)
  local copies, waits for them, and re-layouts: 181 us -> 2.02 us
  matrix products: 142 us -> 0 us
  waiting for transfers between devices: 143 us -> 51.9 us
  other arithmetic: 33.4 us -> 0.01 us
  blocking collectives: 28.9 us -> 0 us
  starting transfers between devices: 30.8 us -> 53.1 us
  Pallas kernels: 0 us -> 14.8 us
    dot_general x24 -> x0, matrix products: 142 us -> none  [the longest x16 77 us: per_frame(): jnp.einsum('rbi,io->rbo', windows, matrix, precision=lax.Precision.HIGHEST)]
    ppermute x10 -> x25, waiting for transfers between devices: 143 us -> 51.9 us  [the longest x8 42.9 us: by_planes(): arrived.append(lax.ppermute(done[k], ('scan', 'ybrick'), route))]
    while x28 -> x0, local copies, waits for them, and re-layouts: 36 us -> none
    gather x24 -> x0, local copies, waits for them, and re-layouts: 33.7 us -> none
    dynamic_update_slice x24 -> x0, local copies, waits for them, and re-layouts: 31.3 us -> none  [along_columns(): return lax.map(per_frame, source)]
    all_to_all x1 -> x0, blocking collectives: 28.9 us -> none  [local(): lax.all_to_all(raw, 'scan', split_axis=0, concat_axis=2, tiled=True)]
    convert_element_type x6 -> x0, other arithmetic: 25.9 us -> none  [the longest x2 7.32 us: local(): ratio.astype(jnp.bfloat16)]
    squeeze x16 -> x0, local copies, waits for them, and re-layouts: 22.7 us -> none  [along_columns(): return lax.map(per_frame, source)]
  transfers between devices with their start and end apart: 10 -> 25, of which waited for: 10 -> 10; matrix products, arithmetic and copies ran while one was open for 6% -> 0% of each run, Pallas kernels for 0% -> 0%
where the time goes in v1:
time: 123 us; the launch traced here: 122 us
  starting transfers between devices  53.1 us (43%)
  waiting for transfers between devices  51.9 us (42%)
  Pallas kernels  14.8 us (12%)
  local copies, waits for them, and re-layouts  2.02 us (2%)
    ppermute x8, waiting for transfers between devices, by_planes(): arrived.append(lax.ppermute(done[k], ('scan', 'ybrick'), route))  42.9 us
    ppermute x16, starting transfers between devices, by_planes(): pieces.append(lax.ppermute(piece, ('scan', 'ybrick'), route))  40 us
    pallas_call x1, Pallas kernels, deconvolve_plane(): pl.pallas_call(functools.partial(plane_kernel, bricks), out_shape=[jax.Sh...  10.7 us
    ppermute x16, waiting for transfers between devices, by_planes(): pieces.append(lax.ppermute(piece, ('scan', 'ybrick'), route))  8.34 us
    ppermute x8, starting transfers between devices, by_planes(): arrived.append(lax.ppermute(done[k], ('scan', 'ybrick'), route))  7.45 us
    ppermute x1, starting transfers between devices, by_planes(): side = lax.ppermute(edges(pieces), 'scan', [(s, s ^ 1) for s in range(4)])  5.56 us
    pallas_call x1, Pallas kernels, place_planes(): pl.pallas_call(place_kernel, grid=(group,), out_shape=jax.ShapeDtypeStruc...  3.71 us
  transfers between devices with their start and end apart: 25, of which 10 were waited for; matrix products, arithmetic and copies ran while one was open for 0% of the time, Pallas kernels for 0%

profile of v1, /device:TPU:9, one launch (start us, length us, event | category | flops | bytes accessed | tf_op | source)
XLA Modules:
  0.0 121.9 jit_solution(4677340281954390646)
XLA Ops:
  0.0 1.8 %constant_dynamic-slice_fusion = (bf16[1,128,512]{2,1,0:T(8,128)(2,1)S(1)}, bf16[1,128,512]{2,1,0:T(8,128)(2,1)S(1)}, bf16[1,128,512]{2,1,0:T(8,128)(2,1)S(1)}, ...) fusion(bf16[16,128,512]{2,1,0:T(8,128)(2,1)} %param.5, ...), kind=kLoop, calls=%fused_computation | loop fusion | bytes 4194368 | tf_op jit(solution)/shard_map/dynamic_slice | solution.py:375
  1.8 0.0 copy-start.2
  1.8 0.0 copy-start.3
  1.8 0.0 copy-start
  1.8 0.0 copy-start.1
  1.9 1.7 %collective-permute-start.15 = (bf16[1,128,512]{2,1,0:T(8,128)(2,1)S(1)}, bf16[1,128,512]{2,1,0:T(8,128)(2,1)S(1)}, u32[]{:S(2)}, u32[]{:S(2)}) collective-permute-start(bf16[1,128,512]{2,1,0:T(8,128)(2,1)S(1)} %get-tuple-element.29), channel_id=1, source_target_pairs={{0,23},{1,22},{2,21},{3,20},{4,19},{5,18},{6,17},{7,16},{8,3},{9,2... | collective-permute-start | bytes 393224 | tf_op jit(solution)/shard_map/ppermute | solution.py:380
  3.6 2.6 %collective-permute-start.13 = (bf16[1,128,512]{2,1,0:T(8,128)(2,1)S(1)}, bf16[1,128,512]{2,1,0:T(8,128)(2,1)S(1)}, u32[]{:S(2)}, u32[]{:S(2)}) collective-permute-start(bf16[1,128,512]{2,1,0:T(8,128)(2,1)S(1)} %get-tuple-element.30), channel_id=1, source_target_pairs={{0,21},{1,20},{2,23},{3,22},{4,17},{5,16},{6,19},{7,18},{8,1},{9,0... | collective-permute-start | bytes 393224 | tf_op jit(solution)/shard_map/ppermute | solution.py:380
  6.2 0.9 collective-permute-start.12
  7.1 3.0 %collective-permute-start.11 = (bf16[1,128,512]{2,1,0:T(8,128)(2,1)S(1)}, bf16[1,128,512]{2,1,0:T(8,128)(2,1)S(1)}, u32[]{:S(2)}, u32[]{:S(2)}) collective-permute-start(bf16[1,128,512]{2,1,0:T(8,128)(2,1)S(1)} %get-tuple-element.32), channel_id=1, source_target_pairs={{0,19},{1,18},{2,17},{3,16},{4,23},{5,22},{6,21},{7,20},{8,7},{9,6... | collective-permute-start | bytes 393224 | tf_op jit(solution)/shard_map/ppermute | solution.py:380
  10.2 0.0 collective-permute-start.10
  10.2 0.0 collective-permute-done.15.refs_15_
  10.2 1.1 collective-permute-start.9
  11.3 0.8 collective-permute-done.13.refs_13_
  12.0 4.0 %collective-permute-start.8 = (bf16[1,128,512]{2,1,0:T(8,128)(2,1)S(1)}, bf16[1,128,512]{2,1,0:T(8,128)(2,1)S(1)}, u32[]{:S(2)}, u32[]{:S(2)}) collective-permute-start(bf16[1,128,512]{2,1,0:T(8,128)(2,1)S(1)} %get-tuple-element.35), channel_id=1, source_target_pairs={{0,16},{1,17},{2,18},{3,19},{4,20},{5,21},{6,22},{7,23},{8,4},{9,5... | collective-permute-start | bytes 393224 | tf_op jit(solution)/shard_map/ppermute | solution.py:380
  16.0 0.0 collective-permute-done.12.refs_12_
  16.0 10.9 %collective-permute-start.7 = (bf16[1,128,512]{2,1,0:T(8,128)(2,1)S(1)}, bf16[1,128,512]{2,1,0:T(8,128)(2,1)S(1)}, u32[]{:S(2)}, u32[]{:S(2)}) collective-permute-start(bf16[1,128,512]{2,1,0:T(8,128)(2,1)S(1)} %get-tuple-element.36), channel_id=1, source_target_pairs={{0,7},{1,6},{2,5},{3,4},{4,3},{5,2},{6,1},{7,0},{8,19},{9,18},{10,... | collective-permute-start | bytes 393224 | tf_op jit(solution)/shard_map/ppermute | solution.py:380
  26.9 0.0 collective-permute-done.11.refs_11_
  26.9 0.3 collective-permute-start.6
  27.2 0.0 collective-permute-done.10.refs_10_
  27.2 1.2 %collective-permute-start.5 = (bf16[1,128,512]{2,1,0:T(8,128)(2,1)S(1)}, bf16[1,128,512]{2,1,0:T(8,128)(2,1)S(1)}, u32[]{:S(2)}, u32[]{:S(2)}) collective-permute-start(bf16[1,128,512]{2,1,0:T(8,128)(2,1)S(1)} %get-tuple-element.38), channel_id=1, source_target_pairs={{0,5},{1,4},{2,7},{3,6},{4,1},{5,0},{6,3},{7,2},{8,17},{9,16},{10,... | collective-permute-start | bytes 393224 | tf_op jit(solution)/shard_map/ppermute | solution.py:380
  28.4 0.0 collective-permute-done.9.refs_9_
  28.5 2.8 %collective-permute-start.4 = (bf16[1,128,512]{2,1,0:T(8,128)(2,1)S(1)}, bf16[1,128,512]{2,1,0:T(8,128)(2,1)S(1)}, u32[]{:S(2)}, u32[]{:S(2)}) collective-permute-start(bf16[1,128,512]{2,1,0:T(8,128)(2,1)S(1)} %get-tuple-element.39), channel_id=1, source_target_pairs={{0,4},{1,5},{2,6},{3,7},{4,0},{5,1},{6,2},{7,3},{8,16},{9,17},{10,... | collective-permute-start | bytes 393224 | tf_op jit(solution)/shard_map/ppermute | solution.py:380
  31.2 0.0 collective-permute-done.8.refs_8_
  31.3 1.5 %collective-permute-start.3 = (bf16[1,128,512]{2,1,0:T(8,128)(2,1)S(1)}, bf16[1,128,512]{2,1,0:T(8,128)(2,1)S(1)}, u32[]{:S(2)}, u32[]{:S(2)}) collective-permute-start(bf16[1,128,512]{2,1,0:T(8,128)(2,1)S(1)} %get-tuple-element.40), channel_id=1, source_target_pairs={{0,3},{1,2},{2,1},{3,0},{4,7},{5,6},{6,5},{7,4},{8,23},{9,22},{10,... | collective-permute-start | bytes 393224 | tf_op jit(solution)/shard_map/ppermute | solution.py:380
  32.8 0.0 collective-permute-done.7.refs_7_
  32.8 3.4 %collective-permute-start.2 = (bf16[1,128,512]{2,1,0:T(8,128)(2,1)S(1)}, bf16[1,128,512]{2,1,0:T(8,128)(2,1)S(1)}, u32[]{:S(2)}, u32[]{:S(2)}) collective-permute-start(bf16[1,128,512]{2,1,0:T(8,128)(2,1)S(1)} %get-tuple-element.41), channel_id=1, source_target_pairs={{0,2},{1,3},{2,0},{3,1},{4,6},{5,7},{6,4},{7,5},{8,22},{9,23},{10,... | collective-permute-start | bytes 393224 | tf_op jit(solution)/shard_map/ppermute | solution.py:380
  36.2 4.4 %collective-permute-done.6.refs_6_ = bf16[1,128,512]{2,1,0:T(8,128)(2,1)S(1)} collective-permute-done((bf16[1,128,512]{2,1,0:T(8,128)(2,1)S(1)}, bf16[1,128,512]{2,1,0:T(8,128)(2,1)S(1)}, u32[]{:S(2)}, u32[]{:S(2)}) %collective-permute-start.6) | collective-permute-done | bytes 131104 | tf_op jit(solution)/shard_map/ppermute | solution.py:380
  40.6 0.0 collective-permute-start.1
  40.7 0.0 collective-permute-done.5.refs_5_
  40.7 1.9 %collective-permute-start = (bf16[1,128,512]{2,1,0:T(8,128)(2,1)S(1)}, bf16[1,128,512]{2,1,0:T(8,128)(2,1)S(1)}, u32[]{:S(2)}, u32[]{:S(2)}) collective-permute-start(bf16[1,128,512]{2,1,0:T(8,128)(2,1)S(1)} %get-tuple-element.43), channel_id=1, source_target_pairs={{0,0},{1,1},{2,2},{3,3},{4,4},{5,5},{6,6},{7,7},{8,20},{9,21},{10,... | collective-permute-start | bytes 393224 | tf_op jit(solution)/shard_map/ppermute | solution.py:380
  42.6 0.0 collective-permute-done.4.refs_4_
  42.6 4.6 %collective-permute-start.14 = (bf16[1,128,512]{2,1,0:T(8,128)(2,1)S(1)}, bf16[1,128,512]{2,1,0:T(8,128)(2,1)S(1)}, u32[]{:S(2)}, u32[]{:S(2)}) collective-permute-start(bf16[1,128,512]{2,1,0:T(8,128)(2,1)S(1)} %get-tuple-element.44), channel_id=1, source_target_pairs={{0,22},{1,23},{2,20},{3,21},{4,18},{5,19},{6,16},{7,17},{8,2},{9,3... | collective-permute-start | bytes 393224 | tf_op jit(solution)/shard_map/ppermute | solution.py:380
  47.2 0.0 collective-permute-done.3.refs_3_
  47.2 0.0 collective-permute-done.2.refs_2_
  47.2 0.0 collective-permute-done.1.refs_1_
  47.2 3.1 %collective-permute-done.refs_0_ = bf16[1,128,512]{2,1,0:T(8,128)(2,1)S(1)} collective-permute-done((bf16[1,128,512]{2,1,0:T(8,128)(2,1)S(1)}, bf16[1,128,512]{2,1,0:T(8,128)(2,1)S(1)}, u32[]{:S(2)}, u32[]{:S(2)}) %collective-permute-start) | collective-permute-done | bytes 131104 | tf_op jit(solution)/shard_map/ppermute | solution.py:380
  50.3 0.0 collective-permute-done.14.refs_14_
  50.3 0.1 edges.1
  50.4 5.6 %collective-permute-start.16 = (bf16[1024,128]{1,0:T(8,128)(2,1)S(1)}, bf16[1024,128]{1,0:T(8,128)(2,1)S(1)}, u32[]{:S(2)}, u32[]{:S(2)}) collective-permute-start(bf16[1024,128]{1,0:T(8,128)(2,1)S(1)} %edges.1), channel_id=1, source_target_pairs={{0,8},{8,0},{16,24},{24,16},{1,9},{9,1},{17,25},{25,17},{2,10},{10... | collective-permute-start | bytes 786440 | tf_op jit(solution)/shard_map/ppermute | solution.py:381
  56.0 0.0 copy-done.2
  56.0 0.1 rev.7
  56.1 0.0 copy-done.3
  56.1 0.1 rev.6
  56.2 0.2 band_matrices.1
  56.5 0.7 collective-permute-done.16.refs_16_
  57.2 0.0 copy-done
  57.2 10.7 %deconvolve_plane.1 = (bf16[128,1024]{1,0:T(8,128)(2,1)S(1)}, bf16[128,1024]{1,0:T(8,128)(2,1)S(1)}, bf16[128,1024]{1,0:T(8,128)(2,1)S(1)}, bf16[128,1024]{1,0:T...) custom-call(s32[16]{0:T(128)S(1)} %copy-done, ...), custom_call_target="tpu_custom_call" | custom-call | tf_op jit(solution)/shard_map/deconvolve_plane/pallas_call | solution.py:276
  67.9 3.5 %collective-permute-start.17 = (bf16[128,1024]{1,0:T(8,128)(2,1)S(1)}, bf16[128,1024]{1,0:T(8,128)(2,1)S(1)}, u32[]{:S(2)}, u32[]{:S(2)}) collective-permute-start(bf16[128,1024]{1,0:T(8,128)(2,1)S(1)} %get-tuple-element.21), channel_id=1, source_target_pairs={{0,0},{1,1},{2,2},{3,3},{4,8},{5,9},{6,10},{7,11},{8,4},{9,5},{10,... | collective-permute-start | bytes 786440 | tf_op jit(solution)/shard_map/ppermute | solution.py:390
  71.4 0.2 collective-permute-start.18
  71.6 1.5 %collective-permute-start.19 = (bf16[128,1024]{1,0:T(8,128)(2,1)S(1)}, bf16[128,1024]{1,0:T(8,128)(2,1)S(1)}, u32[]{:S(2)}, u32[]{:S(2)}) collective-permute-start(bf16[128,1024]{1,0:T(8,128)(2,1)S(1)} %get-tuple-element.23), channel_id=1, source_target_pairs={{0,2},{1,3},{2,0},{3,1},{4,10},{5,11},{6,8},{7,9},{8,6},{9,7},{10,... | collective-permute-start | bytes 786440 | tf_op jit(solution)/shard_map/ppermute | solution.py:390
  73.1 2.2 %collective-permute-start.20 = (bf16[128,1024]{1,0:T(8,128)(2,1)S(1)}, bf16[128,1024]{1,0:T(8,128)(2,1)S(1)}, u32[]{:S(2)}, u32[]{:S(2)}) collective-permute-start(bf16[128,1024]{1,0:T(8,128)(2,1)S(1)} %get-tuple-element.24), channel_id=1, source_target_pairs={{0,3},{1,2},{2,1},{3,0},{4,11},{5,10},{6,9},{7,8},{8,7},{9,6},{10,... | collective-permute-start | bytes 786440 | tf_op jit(solution)/shard_map/ppermute | solution.py:390
  75.3 0.0 collective-permute-start.21
  75.4 4.3 %collective-permute-done.17.refs_0_ = bf16[128,1024]{1,0:T(8,128)(2,1)S(1)} collective-permute-done((bf16[128,1024]{1,0:T(8,128)(2,1)S(1)}, bf16[128,1024]{1,0:T(8,128)(2,1)S(1)}, u32[]{:S(2)}, u32[]{:S(2)}) %collective-permute-start.17) | collective-permute-done | bytes 262176 | tf_op jit(solution)/shard_map/ppermute | solution.py:390
  79.7 0.0 collective-permute-start.22
  79.7 15.3 %collective-permute-done.18.refs_1_ = bf16[128,1024]{1,0:T(8,128)(2,1)S(1)} collective-permute-done((bf16[128,1024]{1,0:T(8,128)(2,1)S(1)}, bf16[128,1024]{1,0:T(8,128)(2,1)S(1)}, u32[]{:S(2)}, u32[]{:S(2)}) %collective-permute-start.18) | collective-permute-done | bytes 262176 | tf_op jit(solution)/shard_map/ppermute | solution.py:390
  95.0 0.0 collective-permute-start.23
  95.0 9.5 %collective-permute-done.19.refs_2_ = bf16[128,1024]{1,0:T(8,128)(2,1)S(1)} collective-permute-done((bf16[128,1024]{1,0:T(8,128)(2,1)S(1)}, bf16[128,1024]{1,0:T(8,128)(2,1)S(1)}, u32[]{:S(2)}, u32[]{:S(2)}) %collective-permute-start.19) | collective-permute-done | bytes 262176 | tf_op jit(solution)/shard_map/ppermute | solution.py:390
  104.4 0.0 collective-permute-start.24
  104.4 10.3 %collective-permute-done.20.refs_3_ = bf16[128,1024]{1,0:T(8,128)(2,1)S(1)} collective-permute-done((bf16[128,1024]{1,0:T(8,128)(2,1)S(1)}, bf16[128,1024]{1,0:T(8,128)(2,1)S(1)}, u32[]{:S(2)}, u32[]{:S(2)}) %collective-permute-start.20) | collective-permute-done | bytes 262176 | tf_op jit(solution)/shard_map/ppermute | solution.py:390
  114.8 0.0 collective-permute-done.21.refs_4_
  114.8 0.0 collective-permute-done.22.refs_5_
  114.8 0.6 collective-permute-done.23.refs_6_
  115.4 2.8 %collective-permute-done.24.refs_7_ = bf16[128,1024]{1,0:T(8,128)(2,1)S(1)} collective-permute-done((bf16[128,1024]{1,0:T(8,128)(2,1)S(1)}, bf16[128,1024]{1,0:T(8,128)(2,1)S(1)}, u32[]{:S(2)}, u32[]{:S(2)}) %collective-permute-start.24) | collective-permute-done | bytes 262176 | tf_op jit(solution)/shard_map/ppermute | solution.py:390
  118.2 3.7 %place_planes.1 = f32[4,128,2048]{2,1,0:T(8,128)} custom-call(bf16[128,1024]{1,0:T(8,128)(2,1)S(1)} %collective-permute-done.17.refs_0_, bf16[128,1024]{1,0:T(8,128)(2,1)S(1)} %collective-permute-done.18.refs_1_, bf16[128,1024]{1,0:T(8,128)(2,1)S(1)} %collective-permute-done.19.refs_2_, bf16[128,1024]{1,0:T(8,128)(2,1)S(1)} %collective-permute-done.20.refs_3_, ...), custom_call_target="tpu_custom_call" | custom-call | tf_op jit(solution)/shard_map/place_planes/pallas_call | solution.py:351
  (2 shorter events, 0.0 us)
Async XLA Ops:
  1.8 54.2 %copy-start.2 = (f32[65]{0:T(128)S(1)}, f32[65]{0:T(128)}, u32[]{:S(2)}) copy-start(f32[65]{0:T(128)} %param.8) | copy-start | bytes 784
  1.8 54.3 %copy-start.3 = (f32[65]{0:T(128)S(1)}, f32[65]{0:T(128)}, u32[]{:S(2)}) copy-start(f32[65]{0:T(128)} %param.9) | copy-start | bytes 784
  1.8 55.3 %copy-start = (s32[16]{0:T(128)S(1)}, s32[16]{0:T(128)}, u32[]{:S(2)}) copy-start(s32[16]{0:T(128)} %row_shift.1) | copy-start | bytes 196
  1.8 55.3 %copy-start.1 = (s32[16]{0:T(128)S(1)}, s32[16]{0:T(128)}, u32[]{:S(2)}) copy-start(s32[16]{0:T(128)} %frac_index.1) | copy-start | bytes 196
  1.9 8.3 %collective-permute-start.15 = (bf16[1,128,512]{2,1,0:T(8,128)(2,1)S(1)}, bf16[1,128,512]{2,1,0:T(8,128)(2,1)S(1)}, u32[]{:S(2)}, u32[]{:S(2)}) collective-permute-start(bf16[1,128,512]{2,1,0:T(8,128)(2,1)S(1)} %get-tuple-element.29), channel_id=1, source_target_pairs={{0,23},{1,22},{2,21},{3,20},{4,19},{5,18},{6,17},{7,16},{8,3},{9,2... | collective-permute-start | bytes 393224 | tf_op jit(solution)/shard_map/ppermute | solution.py:380
  3.6 8.5 %collective-permute-start.13 = (bf16[1,128,512]{2,1,0:T(8,128)(2,1)S(1)}, bf16[1,128,512]{2,1,0:T(8,128)(2,1)S(1)}, u32[]{:S(2)}, u32[]{:S(2)}) collective-permute-start(bf16[1,128,512]{2,1,0:T(8,128)(2,1)S(1)} %get-tuple-element.30), channel_id=1, source_target_pairs={{0,21},{1,20},{2,23},{3,22},{4,17},{5,16},{6,19},{7,18},{8,1},{9,0... | collective-permute-start | bytes 393224 | tf_op jit(solution)/shard_map/ppermute | solution.py:380
  6.2 9.8 %collective-permute-start.12 = (bf16[1,128,512]{2,1,0:T(8,128)(2,1)S(1)}, bf16[1,128,512]{2,1,0:T(8,128)(2,1)S(1)}, u32[]{:S(2)}, u32[]{:S(2)}) collective-permute-start(bf16[1,128,512]{2,1,0:T(8,128)(2,1)S(1)} %get-tuple-element.31), channel_id=1, source_target_pairs={{0,20},{1,21},{2,22},{3,23},{4,16},{5,17},{6,18},{7,19},{8,0},{9,1... | collective-permute-start | bytes 393224 | tf_op jit(solution)/shard_map/ppermute | solution.py:380
  7.1 19.7 %collective-permute-start.11 = (bf16[1,128,512]{2,1,0:T(8,128)(2,1)S(1)}, bf16[1,128,512]{2,1,0:T(8,128)(2,1)S(1)}, u32[]{:S(2)}, u32[]{:S(2)}) collective-permute-start(bf16[1,128,512]{2,1,0:T(8,128)(2,1)S(1)} %get-tuple-element.32), channel_id=1, source_target_pairs={{0,19},{1,18},{2,17},{3,16},{4,23},{5,22},{6,21},{7,20},{8,7},{9,6... | collective-permute-start | bytes 393224 | tf_op jit(solution)/shard_map/ppermute | solution.py:380
  10.2 17.1 %collective-permute-start.10 = (bf16[1,128,512]{2,1,0:T(8,128)(2,1)S(1)}, bf16[1,128,512]{2,1,0:T(8,128)(2,1)S(1)}, u32[]{:S(2)}, u32[]{:S(2)}) collective-permute-start(bf16[1,128,512]{2,1,0:T(8,128)(2,1)S(1)} %get-tuple-element.33), channel_id=1, source_target_pairs={{0,18},{1,19},{2,16},{3,17},{4,22},{5,23},{6,20},{7,21},{8,6},{9,7... | collective-permute-start | bytes 393224 | tf_op jit(solution)/shard_map/ppermute | solution.py:380
  10.2 18.3 %collective-permute-start.9 = (bf16[1,128,512]{2,1,0:T(8,128)(2,1)S(1)}, bf16[1,128,512]{2,1,0:T(8,128)(2,1)S(1)}, u32[]{:S(2)}, u32[]{:S(2)}) collective-permute-start(bf16[1,128,512]{2,1,0:T(8,128)(2,1)S(1)} %get-tuple-element.34), channel_id=1, source_target_pairs={{0,17},{1,16},{2,19},{3,18},{4,21},{5,20},{6,23},{7,22},{8,5},{9,4... | collective-permute-start | bytes 393224 | tf_op jit(solution)/shard_map/ppermute | solution.py:380
  12.0 19.2 %collective-permute-start.8 = (bf16[1,128,512]{2,1,0:T(8,128)(2,1)S(1)}, bf16[1,128,512]{2,1,0:T(8,128)(2,1)S(1)}, u32[]{:S(2)}, u32[]{:S(2)}) collective-permute-start(bf16[1,128,512]{2,1,0:T(8,128)(2,1)S(1)} %get-tuple-element.35), channel_id=1, source_target_pairs={{0,16},{1,17},{2,18},{3,19},{4,20},{5,21},{6,22},{7,23},{8,4},{9,5... | collective-permute-start | bytes 393224 | tf_op jit(solution)/shard_map/ppermute | solution.py:380
  16.0 16.8 %collective-permute-start.7 = (bf16[1,128,512]{2,1,0:T(8,128)(2,1)S(1)}, bf16[1,128,512]{2,1,0:T(8,128)(2,1)S(1)}, u32[]{:S(2)}, u32[]{:S(2)}) collective-permute-start(bf16[1,128,512]{2,1,0:T(8,128)(2,1)S(1)} %get-tuple-element.36), channel_id=1, source_target_pairs={{0,7},{1,6},{2,5},{3,4},{4,3},{5,2},{6,1},{7,0},{8,19},{9,18},{10,... | collective-permute-start | bytes 393224 | tf_op jit(solution)/shard_map/ppermute | solution.py:380
  26.9 13.8 %collective-permute-start.6 = (bf16[1,128,512]{2,1,0:T(8,128)(2,1)S(1)}, bf16[1,128,512]{2,1,0:T(8,128)(2,1)S(1)}, u32[]{:S(2)}, u32[]{:S(2)}) collective-permute-start(bf16[1,128,512]{2,1,0:T(8,128)(2,1)S(1)} %get-tuple-element.37), channel_id=1, source_target_pairs={{0,6},{1,7},{2,4},{3,5},{4,2},{5,3},{6,0},{7,1},{8,18},{9,19},{10,... | collective-permute-start | bytes 393224 | tf_op jit(solution)/shard_map/ppermute | solution.py:380
  27.2 13.4 %collective-permute-start.5 = (bf16[1,128,512]{2,1,0:T(8,128)(2,1)S(1)}, bf16[1,128,512]{2,1,0:T(8,128)(2,1)S(1)}, u32[]{:S(2)}, u32[]{:S(2)}) collective-permute-start(bf16[1,128,512]{2,1,0:T(8,128)(2,1)S(1)} %get-tuple-element.38), channel_id=1, source_target_pairs={{0,5},{1,4},{2,7},{3,6},{4,1},{5,0},{6,3},{7,2},{8,17},{9,16},{10,... | collective-permute-start | bytes 393224 | tf_op jit(solution)/shard_map/ppermute | solution.py:380
  28.5 14.1 %collective-permute-start.4 = (bf16[1,128,512]{2,1,0:T(8,128)(2,1)S(1)}, bf16[1,128,512]{2,1,0:T(8,128)(2,1)S(1)}, u32[]{:S(2)}, u32[]{:S(2)}) collective-permute-start(bf16[1,128,512]{2,1,0:T(8,128)(2,1)S(1)} %get-tuple-element.39), channel_id=1, source_target_pairs={{0,4},{1,5},{2,6},{3,7},{4,0},{5,1},{6,2},{7,3},{8,16},{9,17},{10,... | collective-permute-start | bytes 393224 | tf_op jit(solution)/shard_map/ppermute | solution.py:380
  31.3 15.9 %collective-permute-start.3 = (bf16[1,128,512]{2,1,0:T(8,128)(2,1)S(1)}, bf16[1,128,512]{2,1,0:T(8,128)(2,1)S(1)}, u32[]{:S(2)}, u32[]{:S(2)}) collective-permute-start(bf16[1,128,512]{2,1,0:T(8,128)(2,1)S(1)} %get-tuple-element.40), channel_id=1, source_target_pairs={{0,3},{1,2},{2,1},{3,0},{4,7},{5,6},{6,5},{7,4},{8,23},{9,22},{10,... | collective-permute-start | bytes 393224 | tf_op jit(solution)/shard_map/ppermute | solution.py:380
  32.8 14.3 %collective-permute-start.2 = (bf16[1,128,512]{2,1,0:T(8,128)(2,1)S(1)}, bf16[1,128,512]{2,1,0:T(8,128)(2,1)S(1)}, u32[]{:S(2)}, u32[]{:S(2)}) collective-permute-start(bf16[1,128,512]{2,1,0:T(8,128)(2,1)S(1)} %get-tuple-element.41), channel_id=1, source_target_pairs={{0,2},{1,3},{2,0},{3,1},{4,6},{5,7},{6,4},{7,5},{8,22},{9,23},{10,... | collective-permute-start | bytes 393224 | tf_op jit(solution)/shard_map/ppermute | solution.py:380
  40.6 6.5 %collective-permute-start.1 = (bf16[1,128,512]{2,1,0:T(8,128)(2,1)S(1)}, bf16[1,128,512]{2,1,0:T(8,128)(2,1)S(1)}, u32[]{:S(2)}, u32[]{:S(2)}) collective-permute-start(bf16[1,128,512]{2,1,0:T(8,128)(2,1)S(1)} %get-tuple-element.42), channel_id=1, source_target_pairs={{0,1},{1,0},{2,3},{3,2},{4,5},{5,4},{6,7},{7,6},{8,21},{9,20},{10,... | collective-permute-start | bytes 393224 | tf_op jit(solution)/shard_map/ppermute | solution.py:380
  40.7 9.6 %collective-permute-start = (bf16[1,128,512]{2,1,0:T(8,128)(2,1)S(1)}, bf16[1,128,512]{2,1,0:T(8,128)(2,1)S(1)}, u32[]{:S(2)}, u32[]{:S(2)}) collective-permute-start(bf16[1,128,512]{2,1,0:T(8,128)(2,1)S(1)} %get-tuple-element.43), channel_id=1, source_target_pairs={{0,0},{1,1},{2,2},{3,3},{4,4},{5,5},{6,6},{7,7},{8,20},{9,21},{10,... | collective-permute-start | bytes 393224 | tf_op jit(solution)/shard_map/ppermute | solution.py:380
  42.6 7.7 %collective-permute-start.14 = (bf16[1,128,512]{2,1,0:T(8,128)(2,1)S(1)}, bf16[1,128,512]{2,1,0:T(8,128)(2,1)S(1)}, u32[]{:S(2)}, u32[]{:S(2)}) collective-permute-start(bf16[1,128,512]{2,1,0:T(8,128)(2,1)S(1)} %get-tuple-element.44), channel_id=1, source_target_pairs={{0,22},{1,23},{2,20},{3,21},{4,18},{5,19},{6,16},{7,17},{8,2},{9,3... | collective-permute-start | bytes 393224 | tf_op jit(solution)/shard_map/ppermute | solution.py:380
  50.4 6.7 %collective-permute-start.16 = (bf16[1024,128]{1,0:T(8,128)(2,1)S(1)}, bf16[1024,128]{1,0:T(8,128)(2,1)S(1)}, u32[]{:S(2)}, u32[]{:S(2)}) collective-permute-start(bf16[1024,128]{1,0:T(8,128)(2,1)S(1)} %edges.1), channel_id=1, source_target_pairs={{0,8},{8,0},{16,24},{24,16},{1,9},{9,1},{17,25},{25,17},{2,10},{10... | collective-permute-start | bytes 786440 | tf_op jit(solution)/shard_map/ppermute | solution.py:381
  67.9 11.8 %collective-permute-start.17 = (bf16[128,1024]{1,0:T(8,128)(2,1)S(1)}, bf16[128,1024]{1,0:T(8,128)(2,1)S(1)}, u32[]{:S(2)}, u32[]{:S(2)}) collective-permute-start(bf16[128,1024]{1,0:T(8,128)(2,1)S(1)} %get-tuple-element.21), channel_id=1, source_target_pairs={{0,0},{1,1},{2,2},{3,3},{4,8},{5,9},{6,10},{7,11},{8,4},{9,5},{10,... | collective-permute-start | bytes 786440 | tf_op jit(solution)/shard_map/ppermute | solution.py:390
  71.4 23.6 %collective-permute-start.18 = (bf16[128,1024]{1,0:T(8,128)(2,1)S(1)}, bf16[128,1024]{1,0:T(8,128)(2,1)S(1)}, u32[]{:S(2)}, u32[]{:S(2)}) collective-permute-start(bf16[128,1024]{1,0:T(8,128)(2,1)S(1)} %get-tuple-element.22), channel_id=1, source_target_pairs={{0,1},{1,0},{2,3},{3,2},{4,9},{5,8},{6,11},{7,10},{8,5},{9,4},{10,... | collective-permute-start | bytes 786440 | tf_op jit(solution)/shard_map/ppermute | solution.py:390
  71.6 32.8 %collective-permute-start.19 = (bf16[128,1024]{1,0:T(8,128)(2,1)S(1)}, bf16[128,1024]{1,0:T(8,128)(2,1)S(1)}, u32[]{:S(2)}, u32[]{:S(2)}) collective-permute-start(bf16[128,1024]{1,0:T(8,128)(2,1)S(1)} %get-tuple-element.23), channel_id=1, source_target_pairs={{0,2},{1,3},{2,0},{3,1},{4,10},{5,11},{6,8},{7,9},{8,6},{9,7},{10,... | collective-permute-start | bytes 786440 | tf_op jit(solution)/shard_map/ppermute | solution.py:390
  73.1 41.7 %collective-permute-start.20 = (bf16[128,1024]{1,0:T(8,128)(2,1)S(1)}, bf16[128,1024]{1,0:T(8,128)(2,1)S(1)}, u32[]{:S(2)}, u32[]{:S(2)}) collective-permute-start(bf16[128,1024]{1,0:T(8,128)(2,1)S(1)} %get-tuple-element.24), channel_id=1, source_target_pairs={{0,3},{1,2},{2,1},{3,0},{4,11},{5,10},{6,9},{7,8},{8,7},{9,6},{10,... | collective-permute-start | bytes 786440 | tf_op jit(solution)/shard_map/ppermute | solution.py:390
  75.3 39.4 %collective-permute-start.21 = (bf16[128,1024]{1,0:T(8,128)(2,1)S(1)}, bf16[128,1024]{1,0:T(8,128)(2,1)S(1)}, u32[]{:S(2)}, u32[]{:S(2)}) collective-permute-start(bf16[128,1024]{1,0:T(8,128)(2,1)S(1)} %get-tuple-element.25), channel_id=1, source_target_pairs={{0,4},{1,5},{2,6},{3,7},{4,12},{5,13},{6,14},{7,15},{8,0},{9,1},{1... | collective-permute-start | bytes 786440 | tf_op jit(solution)/shard_map/ppermute | solution.py:390
  79.7 35.1 %collective-permute-start.22 = (bf16[128,1024]{1,0:T(8,128)(2,1)S(1)}, bf16[128,1024]{1,0:T(8,128)(2,1)S(1)}, u32[]{:S(2)}, u32[]{:S(2)}) collective-permute-start(bf16[128,1024]{1,0:T(8,128)(2,1)S(1)} %get-tuple-element.26), channel_id=1, source_target_pairs={{0,5},{1,4},{2,7},{3,6},{4,13},{5,12},{6,15},{7,14},{8,1},{9,0},{1... | collective-permute-start | bytes 786440 | tf_op jit(solution)/shard_map/ppermute | solution.py:390
  95.0 20.4 %collective-permute-start.23 = (bf16[128,1024]{1,0:T(8,128)(2,1)S(1)}, bf16[128,1024]{1,0:T(8,128)(2,1)S(1)}, u32[]{:S(2)}, u32[]{:S(2)}) collective-permute-start(bf16[128,1024]{1,0:T(8,128)(2,1)S(1)} %get-tuple-element.27), channel_id=1, source_target_pairs={{0,6},{1,7},{2,4},{3,5},{4,14},{5,15},{6,12},{7,13},{8,2},{9,3},{1... | collective-permute-start | bytes 786440 | tf_op jit(solution)/shard_map/ppermute | solution.py:390
  104.4 13.8 %collective-permute-start.24 = (bf16[128,1024]{1,0:T(8,128)(2,1)S(1)}, bf16[128,1024]{1,0:T(8,128)(2,1)S(1)}, u32[]{:S(2)}, u32[]{:S(2)}) collective-permute-start(bf16[128,1024]{1,0:T(8,128)(2,1)S(1)} %get-tuple-element.28), channel_id=1, source_target_pairs={{0,7},{1,6},{2,5},{3,4},{4,15},{5,14},{6,13},{7,12},{8,3},{9,2},{1... | collective-permute-start | bytes 786440 | tf_op jit(solution)/shard_map/ppermute | solution.py:390

commit v2 on v1

--- a/solution.py
+++ b/solution.py
@@ -17,9 +17,8 @@
 COLS = 256
 MARGIN = 128
 ALIGN = 16
-TINY = 1e-30
 VMEM_BYTES = 40 * 2**20
-TALL = 512
+FIRST_STEPS = 4
 
 
 def shifted_2(x, axis, by):
@@ -135,17 +134,19 @@
     return core, brick ^ (step % bricks) ^ (core * (bricks // 2))
 
 
-def plane_kernel(bricks, row_shift, frac_index, *refs):
+def plane_kernel(bricks, part, row_shift, frac_index, *refs):
     pieces, refs = refs[: 2 * bricks], refs[2 * bricks :]
     side, x_forward, x_back, y_forward, y_back = refs[:5]
-    outs, refs = refs[5 : 5 + bricks], refs[5 + bricks :]
+    outs, refs = refs[5 : 5 + bricks // 2], refs[5 + bricks // 2 :]
     raw, observed, estimate, blur_in, back_in, wide, ratio, arrived = refs
     y, core, brick_index = place_in_chip()
     plane = y * bricks + brick_index
     shift, fraction = row_shift[plane], frac_index[plane]
     _, brick, own = pieces[0].shape
     rows, width = observed.shape
-    lead = raw.shape[0] - rows
+    lead = raw.shape[0] - bricks * brick
+    half = core ^ part
+    first_row = half * (bricks * brick - rows)
     windows = column_windows(width)
     tiles = [(r, min(ROWS, rows - r)) for r in range(0, rows, ROWS)]
     begin = core * HALO
@@ -157,7 +158,7 @@
         there = pl.ds(pl.multiple_of(begin + source_core * own, 128), own)
         copies.append((pieces[step].at[0], raw.at[here, there]))
     there = pl.ds(pl.multiple_of((1 - core) * 2 * own, 128), HALO)
-    copies.append((side, raw.at[pl.ds(lead, rows), there]))
+    copies.append((side, raw.at[pl.ds(lead, bricks * brick), there]))
     copies = [
         pltpu.make_async_copy(source, target, arrived.at[i])
         for i, (source, target) in enumerate(copies)
@@ -171,7 +172,7 @@
         buffer[RADIUS + rows :, :] = edge
 
     weight = fraction.astype(jnp.float32) / NFRAC
-    first = lead - shift - 1
+    first = lead + first_row - shift - 1
     base = (first // ALIGN) * ALIGN
     depth = ROWS + ALIGN
     ahead = lax.broadcasted_iota(jnp.int32, (ROWS, depth), 1) - (
@@ -197,8 +198,8 @@
                 blur_in[r : r + count + 2 * RADIUS, :],
                 preferred_element_type=jnp.float32,
             ).astype(jnp.bfloat16)
-        for r in range(0, rows, TALL):
-            tall = slice(r, r + TALL)
+        for r in range(0, rows, rows // 2):
+            tall = slice(r, r + rows // 2)
             for start, count, low, high, row in windows:
                 blurred = jnp.dot(
                     wide[tall, low:high],
@@ -206,11 +207,10 @@
                     preferred_element_type=jnp.float32,
                 )
                 top = observed[tall, start : start + count]
-                ratio[tall, start : start + count] = (top / jnp.maximum(blurred, TINY)).astype(
-                    jnp.bfloat16
-                )
+                quotient = top * pl.reciprocal(blurred, approx=True)
+                ratio[tall, start : start + count] = quotient.astype(jnp.bfloat16)
             for start, count, low, high, row in windows:
-                back_in[RADIUS + r : RADIUS + r + TALL, start : start + count] = jnp.dot(
+                back_in[RADIUS + r : RADIUS + r + rows // 2, start : start + count] = jnp.dot(
                     ratio[tall, low:high],
                     x_back[row : row + high - low, :count],
                     preferred_element_type=jnp.float32,
@@ -228,10 +228,11 @@
                 blur_in[RADIUS + r : RADIUS + r + count, :] = updated.astype(jnp.bfloat16)
     first_out = core * (bricks // 2) + brick_index % (bricks // 2)
     here = pl.ds(pl.multiple_of(begin, 128), 2 * own)
-    for k in range(bricks):
-        start = pl.multiple_of((first_out ^ k) * brick, ALIGN)
+    for i, out in enumerate(outs):
+        place = first_out ^ (part * (bricks // 2) + i)
+        start = pl.multiple_of(place * brick - first_row, ALIGN)
         squared = jnp.square(estimate[pl.ds(start, brick), here])
-        outs[k][...] = jnp.square(squared).astype(outs[k].dtype)
+        out[...] = jnp.square(squared).astype(out.dtype)
 
 
 def band_kernel(taps, x_forward, x_back, y_forward, y_back):
@@ -266,20 +267,20 @@
     )(rows)
 
 
-def deconvolve_plane(tables, pieces, side, matrices, lead):
+def deconvolve_rows(part, tables, pieces, side, matrices, lead):
     bricks = len(pieces) // 2
     _, brick, own = pieces[0].shape
-    rows, width = bricks * brick, 2 * own + HALO
+    rows, width = bricks * brick // 2 + HALO, 2 * own + HALO
     vmem = pl.BlockSpec(memory_space=pltpu.VMEM)
     smem = pl.BlockSpec(memory_space=pltpu.SMEM)
     anywhere = pl.BlockSpec(memory_space=pl.ANY)
     return pl.pallas_call(
-        functools.partial(plane_kernel, bricks),
-        out_shape=[jax.ShapeDtypeStruct((brick, 2 * own), jnp.bfloat16)] * bricks,
+        functools.partial(plane_kernel, bricks, part),
+        out_shape=[jax.ShapeDtypeStruct((brick, 2 * own), jnp.bfloat16)] * (bricks // 2),
         in_specs=[smem] * 2 + [anywhere] * (2 * bricks + 1) + [vmem] * 4,
-        out_specs=[vmem] * bricks,
+        out_specs=[vmem] * (bricks // 2),
         scratch_shapes=[
-            pltpu.VMEM((lead + rows, width), jnp.bfloat16),
+            pltpu.VMEM((lead + bricks * brick, width), jnp.bfloat16),
             pltpu.VMEM((rows, width), jnp.float32),
             pltpu.VMEM((rows, width), jnp.float32),
             pltpu.VMEM((rows + 2 * RADIUS, width), jnp.bfloat16),
@@ -289,7 +290,7 @@
             pltpu.SemaphoreType.DMA((2 * bricks + 1,)),
         ],
         compiler_params=pltpu.CompilerParams(vmem_limit_bytes=VMEM_BYTES),
-        name="deconvolve_plane",
+        name="deconvolve_rows",
     )(*tables, *pieces, side, *matrices)
 
 
@@ -342,7 +343,7 @@
         @pl.when(source % group == pl.program_id(0))
         def _(piece=piece, source=source):
             here = pl.ds(pl.multiple_of((source // group) * width, 128), width)
-            out[0, :, here] = jnp.sqrt(jnp.sqrt(piece[...].astype(out.dtype)))
+            out[0, :, here] = lax.rsqrt(lax.rsqrt(piece[...].astype(out.dtype)))
 
 
 def place_planes(pieces):
@@ -359,6 +360,10 @@
     )(*pieces)
 
 
+def after(x, *earlier):
+    return lax.optimization_barrier((x, *earlier))[0]
+
+
 def by_planes(raw, row_shift, frac_index, psf_y, psf_x):
     planes, brick, own = raw.shape
     bricks = lax.axis_size("ybrick")
@@ -368,18 +373,24 @@
 
     _, core, b = place_in_chip()
     devices = [(y, c, i) for y in range(2) for c in range(2) for i in range(bricks)]
-    pieces = []
+    pieces, pieces_cut = [], []
     for step in range(2 * bricks):
         turn, k = step // bricks, step % bricks
         plane = (core ^ turn) * bricks + (b ^ k ^ (core * half))
+        if step == FIRST_STEPS:
+            raw = after(raw, *pieces_cut)
         piece = lax.dynamic_slice_in_dim(raw, plane, 1, 0)
+        if step < FIRST_STEPS:
+            pieces_cut.append(piece)
         route = []
         for y, c, i in devices:
             target = (2 * (c ^ turn) + y) * bricks + (i ^ k ^ (c * half))
             route.append(((2 * y + c) * bricks + i, target))
         pieces.append(lax.ppermute(piece, ("scan", "ybrick"), route))
     side = lax.ppermute(edges(pieces), "scan", [(s, s ^ 1) for s in range(4)])
-    done = deconvolve_plane((row_shift, frac_index), pieces, side, matrices, lead)
+    done = []
+    for part in range(2):
+        done += deconvolve_rows(part, (row_shift, frac_index), pieces, side, matrices, lead)
 
     arrived = []
     for k in range(bricks):
@@ -395,7 +406,7 @@
     planes, brick, own = raw.shape
     bricks, scans = lax.axis_size("ybrick"), lax.axis_size("scan")
     fits = scans == 4 and planes == 2 * bricks and bricks >= 4 and bricks & (bricks - 1) == 0
-    fits = fits and brick % ALIGN == 0 and own % HALO == 0 and bricks * brick % TALL == 0
+    fits = fits and brick % ALIGN == 0 and own % HALO == 0
     plan = by_planes if fits else by_bricks
     return plan(raw, row_shift, frac_index, psf_y, psf_x)
 

time: 123 us -> 114 us (0.927)
  waiting for transfers between devices: 51.9 us -> 34.2 us
  starting transfers between devices: 53.1 us -> 58.4 us
  Pallas kernels: 14.8 us -> 17.9 us
    ppermute x8, waiting for transfers between devices: 42.9 us -> 28.2 us  [by_planes(): arrived.append(lax.ppermute(done[k], ('scan', 'ybrick'), route))]
    ppermute x8, starting transfers between devices: 7.45 us -> 14.7 us  [by_planes(): arrived.append(lax.ppermute(done[k], ('scan', 'ybrick'), route))]
    ppermute x1, starting transfers between devices: 5.56 us -> 1.47 us  [by_planes(): side = lax.ppermute(edges(pieces), 'scan', [(s, s ^ 1) for s in range(4)])]
    pallas_call x1 -> x2, Pallas kernels: 10.7 us -> 14.5 us  [deconvolve_rows(): pl.pallas_call(functools.partial(plane_kernel, bricks, part), out_shape=[...]
    ppermute x16, waiting for transfers between devices: 8.34 us -> 5.27 us  [by_planes(): pieces.append(lax.ppermute(piece, ('scan', 'ybrick'), route))]
    ppermute x16, starting transfers between devices: 40 us -> 42.3 us  [by_planes(): pieces.append(lax.ppermute(piece, ('scan', 'ybrick'), route))]
    dynamic_slice x1 -> x2, local copies, waits for them, and re-layouts: 1.8 us -> 2.75 us  [by_planes(): piece = lax.dynamic_slice_in_dim(raw, plane, 1, 0)]
  transfers between devices with their start and end apart: 25 -> 25, of which waited for: 10 -> 10; matrix products, arithmetic and copies ran while one was open for 0% -> 2% of each run, Pallas kernels for 0% -> 7%
where the time goes in v2:
time: 114 us
  starting transfers between devices  58.4 us (51%)
  waiting for transfers between devices  34.2 us (30%)
  Pallas kernels  17.9 us (16%)
  local copies, waits for them, and re-layouts  2.97 us (3%)
    ppermute x16, starting transfers between devices, by_planes(): pieces.append(lax.ppermute(piece, ('scan', 'ybrick'), route))  42.3 us
    ppermute x8, waiting for transfers between devices, by_planes(): arrived.append(lax.ppermute(done[k], ('scan', 'ybrick'), route))  28.2 us
    ppermute x8, starting transfers between devices, by_planes(): arrived.append(lax.ppermute(done[k], ('scan', 'ybrick'), route))  14.7 us
    pallas_call x2, Pallas kernels, deconvolve_rows(): pl.pallas_call(functools.partial(plane_kernel, bricks, part), out_shape=[...  14.5 us
    ppermute x16, waiting for transfers between devices, by_planes(): pieces.append(lax.ppermute(piece, ('scan', 'ybrick'), route))  5.27 us
    pallas_call x1, Pallas kernels, place_planes(): pl.pallas_call(place_kernel, grid=(group,), out_shape=jax.ShapeDtypeStruc...  3 us
    dynamic_slice x2, local copies, waits for them, and re-layouts, by_planes(): piece = lax.dynamic_slice_in_dim(raw, plane, 1, 0)  2.75 us
  transfers between devices with their start and end apart: 25, of which 10 were waited for; matrix products, arithmetic and copies ran while one was open for 2% of the time, Pallas kernels for 7%

profile of v2, /device:TPU:9, one launch (start us, length us, event | category | flops | bytes accessed | tf_op | source)
XLA Modules:
  0.0 113.7 jit_solution(12102888628642494273)
XLA Ops:
  0.0 1.1 constant_dynamic-slice_fusion.12
  1.1 3.8 %collective-permute-start.3 = (bf16[1,128,512]{2,1,0:T(8,128)(2,1)S(1)}, bf16[1,128,512]{2,1,0:T(8,128)(2,1)S(1)}, u32[]{:S(2)}, u32[]{:S(2)}) collective-permute-start(bf16[1,128,512]{2,1,0:T(8,128)(2,1)S(1)} %get-tuple-element.43), channel_id=1, source_target_pairs={{0,3},{1,2},{2,1},{3,0},{4,7},{5,6},{6,5},{7,4},{8,23},{9,22},{10,... | collective-permute-start | bytes 393224 | tf_op jit(solution)/shard_map/ppermute | solution.py:389
  4.9 1.0 collective-permute-start.2
  5.9 1.5 %collective-permute-start.1 = (bf16[1,128,512]{2,1,0:T(8,128)(2,1)S(1)}, bf16[1,128,512]{2,1,0:T(8,128)(2,1)S(1)}, u32[]{:S(2)}, u32[]{:S(2)}) collective-permute-start(bf16[1,128,512]{2,1,0:T(8,128)(2,1)S(1)} %get-tuple-element.45), channel_id=1, source_target_pairs={{0,1},{1,0},{2,3},{3,2},{4,5},{5,4},{6,7},{7,6},{8,21},{9,20},{10,... | collective-permute-start | bytes 393224 | tf_op jit(solution)/shard_map/ppermute | solution.py:389
  7.4 2.7 %collective-permute-start = (bf16[1,128,512]{2,1,0:T(8,128)(2,1)S(1)}, bf16[1,128,512]{2,1,0:T(8,128)(2,1)S(1)}, u32[]{:S(2)}, u32[]{:S(2)}) collective-permute-start(bf16[1,128,512]{2,1,0:T(8,128)(2,1)S(1)} %get-tuple-element.46), channel_id=1, source_target_pairs={{0,0},{1,1},{2,2},{3,3},{4,4},{5,5},{6,6},{7,7},{8,20},{9,21},{10,... | collective-permute-start | bytes 393224 | tf_op jit(solution)/shard_map/ppermute | solution.py:389
  10.3 0.0 copy-start.2
  10.3 0.0 copy-start.3
  10.3 0.0 copy-start
  10.3 0.0 copy-start.1
  10.3 1.6 %constant_dynamic-slice_fusion = (bf16[1,128,512]{2,1,0:T(8,128)(2,1)S(1)}, bf16[1,128,512]{2,1,0:T(8,128)(2,1)S(1)}, bf16[1,128,512]{2,1,0:T(8,128)(2,1)S(1)}, ...) fusion(bf16[16,128,512]{2,1,0:T(8,128)(2,1)} %param.5, ...), kind=kLoop, calls=%fused_computation | loop fusion | bytes 3145776 | tf_op jit(solution)/shard_map/dynamic_slice | solution.py:382
  11.9 0.1 collective-permute-start.15
  12.0 0.0 collective-permute-done.3.refs_3_
  12.0 6.2 %collective-permute-start.14 = (bf16[1,128,512]{2,1,0:T(8,128)(2,1)S(1)}, bf16[1,128,512]{2,1,0:T(8,128)(2,1)S(1)}, u32[]{:S(2)}, u32[]{:S(2)}) collective-permute-start(bf16[1,128,512]{2,1,0:T(8,128)(2,1)S(1)} %get-tuple-element.32), channel_id=1, source_target_pairs={{0,22},{1,23},{2,20},{3,21},{4,18},{5,19},{6,16},{7,17},{8,2},{9,3... | collective-permute-start | bytes 393224 | tf_op jit(solution)/shard_map/ppermute | solution.py:389
  18.2 0.0 collective-permute-done.2.refs_2_
  18.2 0.0 collective-permute-start.13
  18.2 0.0 collective-permute-done.1.refs_1_
  18.2 0.1 collective-permute-start.12
  18.3 0.0 collective-permute-done.refs_0_
  18.3 3.1 %collective-permute-start.11 = (bf16[1,128,512]{2,1,0:T(8,128)(2,1)S(1)}, bf16[1,128,512]{2,1,0:T(8,128)(2,1)S(1)}, u32[]{:S(2)}, u32[]{:S(2)}) collective-permute-start(bf16[1,128,512]{2,1,0:T(8,128)(2,1)S(1)} %get-tuple-element.35), channel_id=1, source_target_pairs={{0,19},{1,18},{2,17},{3,16},{4,23},{5,22},{6,21},{7,20},{8,7},{9,6... | collective-permute-start | bytes 393224 | tf_op jit(solution)/shard_map/ppermute | solution.py:389
  21.4 0.0 collective-permute-done.15.refs_15_
  21.4 11.4 %collective-permute-start.10 = (bf16[1,128,512]{2,1,0:T(8,128)(2,1)S(1)}, bf16[1,128,512]{2,1,0:T(8,128)(2,1)S(1)}, u32[]{:S(2)}, u32[]{:S(2)}) collective-permute-start(bf16[1,128,512]{2,1,0:T(8,128)(2,1)S(1)} %get-tuple-element.36), channel_id=1, source_target_pairs={{0,18},{1,19},{2,16},{3,17},{4,22},{5,23},{6,20},{7,21},{8,6},{9,7... | collective-permute-start | bytes 393224 | tf_op jit(solution)/shard_map/ppermute | solution.py:389
  32.8 0.0 collective-permute-done.14.refs_14_
  32.8 0.0 collective-permute-start.9
  32.8 0.0 collective-permute-done.13.refs_13_
  32.8 0.1 collective-permute-start.8
  32.9 0.0 collective-permute-done.12.refs_12_
  32.9 7.4 %collective-permute-start.7 = (bf16[1,128,512]{2,1,0:T(8,128)(2,1)S(1)}, bf16[1,128,512]{2,1,0:T(8,128)(2,1)S(1)}, u32[]{:S(2)}, u32[]{:S(2)}) collective-permute-start(bf16[1,128,512]{2,1,0:T(8,128)(2,1)S(1)} %get-tuple-element.39), channel_id=1, source_target_pairs={{0,7},{1,6},{2,5},{3,4},{4,3},{5,2},{6,1},{7,0},{8,19},{9,18},{10,... | collective-permute-start | bytes 393224 | tf_op jit(solution)/shard_map/ppermute | solution.py:389
  40.3 0.0 collective-permute-done.11.refs_11_
  40.3 0.0 collective-permute-start.6
  40.3 0.0 collective-permute-done.10.refs_10_
  40.3 0.1 collective-permute-start.5
  40.4 0.9 collective-permute-done.9.refs_9_
  41.3 4.9 %collective-permute-start.4 = (bf16[1,128,512]{2,1,0:T(8,128)(2,1)S(1)}, bf16[1,128,512]{2,1,0:T(8,128)(2,1)S(1)}, u32[]{:S(2)}, u32[]{:S(2)}) collective-permute-start(bf16[1,128,512]{2,1,0:T(8,128)(2,1)S(1)} %get-tuple-element.42), channel_id=1, source_target_pairs={{0,4},{1,5},{2,6},{3,7},{4,0},{5,1},{6,2},{7,3},{8,16},{9,17},{10,... | collective-permute-start | bytes 393224 | tf_op jit(solution)/shard_map/ppermute | solution.py:389
  46.2 2.3 %collective-permute-done.8.refs_8_ = bf16[1,128,512]{2,1,0:T(8,128)(2,1)S(1)} collective-permute-done((bf16[1,128,512]{2,1,0:T(8,128)(2,1)S(1)}, bf16[1,128,512]{2,1,0:T(8,128)(2,1)S(1)}, u32[]{:S(2)}, u32[]{:S(2)}) %collective-permute-start.8) | collective-permute-done | bytes 131104 | tf_op jit(solution)/shard_map/ppermute | solution.py:389
  48.4 0.0 collective-permute-done.7.refs_7_
  48.5 0.3 collective-permute-done.6.refs_6_
  48.7 0.8 collective-permute-done.5.refs_5_
  49.6 1.0 collective-permute-done.4.refs_4_
  50.5 0.1 edges.1
  50.7 1.5 %collective-permute-start.16 = (bf16[1024,128]{1,0:T(8,128)(2,1)S(1)}, bf16[1024,128]{1,0:T(8,128)(2,1)S(1)}, u32[]{:S(2)}, u32[]{:S(2)}) collective-permute-start(bf16[1024,128]{1,0:T(8,128)(2,1)S(1)} %edges.1), channel_id=1, source_target_pairs={{0,8},{8,0},{16,24},{24,16},{1,9},{9,1},{17,25},{25,17},{2,10},{10... | collective-permute-start | bytes 786440 | tf_op jit(solution)/shard_map/ppermute | solution.py:390
  52.2 0.0 copy-done.2
  52.2 0.1 rev.7
  52.3 0.1 rev.6
  52.4 0.2 band_matrices.1
  52.6 0.7 collective-permute-done.16.refs_16_
  53.3 7.2 %deconvolve_rows.3 = (bf16[128,1024]{1,0:T(8,128)(2,1)S(1)}, bf16[128,1024]{1,0:T(8,128)(2,1)S(1)}, bf16[128,1024]{1,0:T(8,128)(2,1)S(1)}, bf16[128,1024]{1,0:T(8,128)(2,1)S(1)}) custom-call(s32[16]{0:T(128)S(1)} %copy-done, s32[16]{0:T(128)S(1)} %copy-done.1, bf16[1,128,512]{2,1,0:T(8,128)(2,1)S(1)} %collective-permute-done.refs_0_, ...), custom_call_target="tpu_custom_call" | custom-call | tf_op jit(solution)/shard_map/deconvolve_rows/pallas_call | solution.py:277
  60.6 0.4 collective-permute-start.21
  61.0 3.6 %collective-permute-start.22 = (bf16[128,1024]{1,0:T(8,128)(2,1)S(1)}, bf16[128,1024]{1,0:T(8,128)(2,1)S(1)}, u32[]{:S(2)}, u32[]{:S(2)}) collective-permute-start(bf16[128,1024]{1,0:T(8,128)(2,1)S(1)} %get-tuple-element.28), channel_id=1, source_target_pairs={{0,5},{1,4},{2,7},{3,6},{4,13},{5,12},{6,15},{7,14},{8,1},{9,0},{1... | collective-permute-start | bytes 786440 | tf_op jit(solution)/shard_map/ppermute | solution.py:401
  64.6 0.0 collective-permute-start.23
  64.6 2.1 %collective-permute-start.24 = (bf16[128,1024]{1,0:T(8,128)(2,1)S(1)}, bf16[128,1024]{1,0:T(8,128)(2,1)S(1)}, u32[]{:S(2)}, u32[]{:S(2)}) collective-permute-start(bf16[128,1024]{1,0:T(8,128)(2,1)S(1)} %get-tuple-element.30), channel_id=1, source_target_pairs={{0,7},{1,6},{2,5},{3,4},{4,15},{5,14},{6,13},{7,12},{8,3},{9,2},{1... | collective-permute-start | bytes 786440 | tf_op jit(solution)/shard_map/ppermute | solution.py:401
  66.8 7.2 %deconvolve_rows.2 = (bf16[128,1024]{1,0:T(8,128)(2,1)S(1)}, bf16[128,1024]{1,0:T(8,128)(2,1)S(1)}, bf16[128,1024]{1,0:T(8,128)(2,1)S(1)}, bf16[128,1024]{1,0:T(8,128)(2,1)S(1)}) custom-call(s32[16]{0:T(128)S(1)} %copy-done, s32[16]{0:T(128)S(1)} %copy-done.1, bf16[1,128,512]{2,1,0:T(8,128)(2,1)S(1)} %collective-permute-done.refs_0_, ...), custom_call_target="tpu_custom_call" | custom-call | tf_op jit(solution)/shard_map/deconvolve_rows/pallas_call | solution.py:277
  74.0 3.5 %collective-permute-start.17 = (bf16[128,1024]{1,0:T(8,128)(2,1)S(1)}, bf16[128,1024]{1,0:T(8,128)(2,1)S(1)}, u32[]{:S(2)}, u32[]{:S(2)}) collective-permute-start(bf16[128,1024]{1,0:T(8,128)(2,1)S(1)} %get-tuple-element.23), channel_id=1, source_target_pairs={{0,0},{1,1},{2,2},{3,3},{4,8},{5,9},{6,10},{7,11},{8,4},{9,5},{10,... | collective-permute-start | bytes 786440 | tf_op jit(solution)/shard_map/ppermute | solution.py:401
  77.6 0.0 collective-permute-done.21.refs_4_
  77.6 2.0 %collective-permute-start.18 = (bf16[128,1024]{1,0:T(8,128)(2,1)S(1)}, bf16[128,1024]{1,0:T(8,128)(2,1)S(1)}, u32[]{:S(2)}, u32[]{:S(2)}) collective-permute-start(bf16[128,1024]{1,0:T(8,128)(2,1)S(1)} %get-tuple-element.24), channel_id=1, source_target_pairs={{0,1},{1,0},{2,3},{3,2},{4,9},{5,8},{6,11},{7,10},{8,5},{9,4},{10,... | collective-permute-start | bytes 786440 | tf_op jit(solution)/shard_map/ppermute | solution.py:401
  79.6 0.0 collective-permute-done.22.refs_5_
  79.6 0.5 collective-permute-start.19
  80.1 18.6 %collective-permute-done.23.refs_6_ = bf16[128,1024]{1,0:T(8,128)(2,1)S(1)} collective-permute-done((bf16[128,1024]{1,0:T(8,128)(2,1)S(1)}, bf16[128,1024]{1,0:T(8,128)(2,1)S(1)}, u32[]{:S(2)}, u32[]{:S(2)}) %collective-permute-start.23) | collective-permute-done | bytes 262176 | tf_op jit(solution)/shard_map/ppermute | solution.py:401
  98.6 2.4 %collective-permute-start.20 = (bf16[128,1024]{1,0:T(8,128)(2,1)S(1)}, bf16[128,1024]{1,0:T(8,128)(2,1)S(1)}, u32[]{:S(2)}, u32[]{:S(2)}) collective-permute-start(bf16[128,1024]{1,0:T(8,128)(2,1)S(1)} %get-tuple-element.26), channel_id=1, source_target_pairs={{0,3},{1,2},{2,1},{3,0},{4,11},{5,10},{6,9},{7,8},{8,7},{9,6},{10,... | collective-permute-start | bytes 786440 | tf_op jit(solution)/shard_map/ppermute | solution.py:401
  101.1 4.8 %collective-permute-done.24.refs_7_ = bf16[128,1024]{1,0:T(8,128)(2,1)S(1)} collective-permute-done((bf16[128,1024]{1,0:T(8,128)(2,1)S(1)}, bf16[128,1024]{1,0:T(8,128)(2,1)S(1)}, u32[]{:S(2)}, u32[]{:S(2)}) %collective-permute-start.24) | collective-permute-done | bytes 262176 | tf_op jit(solution)/shard_map/ppermute | solution.py:401
  105.9 0.0 collective-permute-done.17.refs_0_
  105.9 0.0 collective-permute-done.18.refs_1_
  105.9 1.0 collective-permute-done.19.refs_2_
  106.9 3.8 %collective-permute-done.20.refs_3_ = bf16[128,1024]{1,0:T(8,128)(2,1)S(1)} collective-permute-done((bf16[128,1024]{1,0:T(8,128)(2,1)S(1)}, bf16[128,1024]{1,0:T(8,128)(2,1)S(1)}, u32[]{:S(2)}, u32[]{:S(2)}) %collective-permute-start.20) | collective-permute-done | bytes 262176 | tf_op jit(solution)/shard_map/ppermute | solution.py:401
  110.7 3.0 %place_planes.1 = f32[4,128,2048]{2,1,0:T(8,128)} custom-call(bf16[128,1024]{1,0:T(8,128)(2,1)S(1)} %collective-permute-done.17.refs_0_, bf16[128,1024]{1,0:T(8,128)(2,1)S(1)} %collective-permute-done.18.refs_1_, bf16[128,1024]{1,0:T(8,128)(2,1)S(1)} %collective-permute-done.19.refs_2_, bf16[128,1024]{1,0:T(8,128)(2,1)S(1)} %collective-permute-done.20.refs_3_, ...), custom_call_target="tpu_custom_call" | custom-call | tf_op jit(solution)/shard_map/place_planes/pallas_call | solution.py:352
  (4 shorter events, 0.0 us)
Async XLA Ops:
  1.1 10.9 %collective-permute-start.3 = (bf16[1,128,512]{2,1,0:T(8,128)(2,1)S(1)}, bf16[1,128,512]{2,1,0:T(8,128)(2,1)S(1)}, u32[]{:S(2)}, u32[]{:S(2)}) collective-permute-start(bf16[1,128,512]{2,1,0:T(8,128)(2,1)S(1)} %get-tuple-element.43), channel_id=1, source_target_pairs={{0,3},{1,2},{2,1},{3,0},{4,7},{5,6},{6,5},{7,4},{8,23},{9,22},{10,... | collective-permute-start | bytes 393224 | tf_op jit(solution)/shard_map/ppermute | solution.py:389
  4.9 13.3 %collective-permute-start.2 = (bf16[1,128,512]{2,1,0:T(8,128)(2,1)S(1)}, bf16[1,128,512]{2,1,0:T(8,128)(2,1)S(1)}, u32[]{:S(2)}, u32[]{:S(2)}) collective-permute-start(bf16[1,128,512]{2,1,0:T(8,128)(2,1)S(1)} %get-tuple-element.44), channel_id=1, source_target_pairs={{0,2},{1,3},{2,0},{3,1},{4,6},{5,7},{6,4},{7,5},{8,22},{9,23},{10,... | collective-permute-start | bytes 393224 | tf_op jit(solution)/shard_map/ppermute | solution.py:389
  5.9 12.4 %collective-permute-start.1 = (bf16[1,128,512]{2,1,0:T(8,128)(2,1)S(1)}, bf16[1,128,512]{2,1,0:T(8,128)(2,1)S(1)}, u32[]{:S(2)}, u32[]{:S(2)}) collective-permute-start(bf16[1,128,512]{2,1,0:T(8,128)(2,1)S(1)} %get-tuple-element.45), channel_id=1, source_target_pairs={{0,1},{1,0},{2,3},{3,2},{4,5},{5,4},{6,7},{7,6},{8,21},{9,20},{10,... | collective-permute-start | bytes 393224 | tf_op jit(solution)/shard_map/ppermute | solution.py:389
  7.4 10.9 %collective-permute-start = (bf16[1,128,512]{2,1,0:T(8,128)(2,1)S(1)}, bf16[1,128,512]{2,1,0:T(8,128)(2,1)S(1)}, u32[]{:S(2)}, u32[]{:S(2)}) collective-permute-start(bf16[1,128,512]{2,1,0:T(8,128)(2,1)S(1)} %get-tuple-element.46), channel_id=1, source_target_pairs={{0,0},{1,1},{2,2},{3,3},{4,4},{5,5},{6,6},{7,7},{8,20},{9,21},{10,... | collective-permute-start | bytes 393224 | tf_op jit(solution)/shard_map/ppermute | solution.py:389
  10.3 41.9 %copy-start.2 = (f32[65]{0:T(128)S(1)}, f32[65]{0:T(128)}, u32[]{:S(2)}) copy-start(f32[65]{0:T(128)} %param.8) | copy-start | bytes 784
  10.3 42.0 %copy-start.3 = (f32[65]{0:T(128)S(1)}, f32[65]{0:T(128)}, u32[]{:S(2)}) copy-start(f32[65]{0:T(128)} %param.9) | copy-start | bytes 784
  10.3 43.0 %copy-start = (s32[16]{0:T(128)S(1)}, s32[16]{0:T(128)}, u32[]{:S(2)}) copy-start(s32[16]{0:T(128)} %row_shift.3) | copy-start | bytes 196
  10.3 43.0 %copy-start.1 = (s32[16]{0:T(128)S(1)}, s32[16]{0:T(128)}, u32[]{:S(2)}) copy-start(s32[16]{0:T(128)} %frac_index.3) | copy-start | bytes 196
  11.9 9.5 %collective-permute-start.15 = (bf16[1,128,512]{2,1,0:T(8,128)(2,1)S(1)}, bf16[1,128,512]{2,1,0:T(8,128)(2,1)S(1)}, u32[]{:S(2)}, u32[]{:S(2)}) collective-permute-start(bf16[1,128,512]{2,1,0:T(8,128)(2,1)S(1)} %get-tuple-element.31), channel_id=1, source_target_pairs={{0,23},{1,22},{2,21},{3,20},{4,19},{5,18},{6,17},{7,16},{8,3},{9,2... | collective-permute-start | bytes 393224 | tf_op jit(solution)/shard_map/ppermute | solution.py:389
  12.0 20.7 %collective-permute-start.14 = (bf16[1,128,512]{2,1,0:T(8,128)(2,1)S(1)}, bf16[1,128,512]{2,1,0:T(8,128)(2,1)S(1)}, u32[]{:S(2)}, u32[]{:S(2)}) collective-permute-start(bf16[1,128,512]{2,1,0:T(8,128)(2,1)S(1)} %get-tuple-element.32), channel_id=1, source_target_pairs={{0,22},{1,23},{2,20},{3,21},{4,18},{5,19},{6,16},{7,17},{8,2},{9,3... | collective-permute-start | bytes 393224 | tf_op jit(solution)/shard_map/ppermute | solution.py:389
  18.2 14.5 %collective-permute-start.13 = (bf16[1,128,512]{2,1,0:T(8,128)(2,1)S(1)}, bf16[1,128,512]{2,1,0:T(8,128)(2,1)S(1)}, u32[]{:S(2)}, u32[]{:S(2)}) collective-permute-start(bf16[1,128,512]{2,1,0:T(8,128)(2,1)S(1)} %get-tuple-element.33), channel_id=1, source_target_pairs={{0,21},{1,20},{2,23},{3,22},{4,17},{5,16},{6,19},{7,18},{8,1},{9,0... | collective-permute-start | bytes 393224 | tf_op jit(solution)/shard_map/ppermute | solution.py:389
  18.2 14.6 %collective-permute-start.12 = (bf16[1,128,512]{2,1,0:T(8,128)(2,1)S(1)}, bf16[1,128,512]{2,1,0:T(8,128)(2,1)S(1)}, u32[]{:S(2)}, u32[]{:S(2)}) collective-permute-start(bf16[1,128,512]{2,1,0:T(8,128)(2,1)S(1)} %get-tuple-element.34), channel_id=1, source_target_pairs={{0,20},{1,21},{2,22},{3,23},{4,16},{5,17},{6,18},{7,19},{8,0},{9,1... | collective-permute-start | bytes 393224 | tf_op jit(solution)/shard_map/ppermute | solution.py:389
  18.3 22.0 %collective-permute-start.11 = (bf16[1,128,512]{2,1,0:T(8,128)(2,1)S(1)}, bf16[1,128,512]{2,1,0:T(8,128)(2,1)S(1)}, u32[]{:S(2)}, u32[]{:S(2)}) collective-permute-start(bf16[1,128,512]{2,1,0:T(8,128)(2,1)S(1)} %get-tuple-element.35), channel_id=1, source_target_pairs={{0,19},{1,18},{2,17},{3,16},{4,23},{5,22},{6,21},{7,20},{8,7},{9,6... | collective-permute-start | bytes 393224 | tf_op jit(solution)/shard_map/ppermute | solution.py:389
  21.4 18.9 %collective-permute-start.10 = (bf16[1,128,512]{2,1,0:T(8,128)(2,1)S(1)}, bf16[1,128,512]{2,1,0:T(8,128)(2,1)S(1)}, u32[]{:S(2)}, u32[]{:S(2)}) collective-permute-start(bf16[1,128,512]{2,1,0:T(8,128)(2,1)S(1)} %get-tuple-element.36), channel_id=1, source_target_pairs={{0,18},{1,19},{2,16},{3,17},{4,22},{5,23},{6,20},{7,21},{8,6},{9,7... | collective-permute-start | bytes 393224 | tf_op jit(solution)/shard_map/ppermute | solution.py:389
  32.8 8.5 %collective-permute-start.9 = (bf16[1,128,512]{2,1,0:T(8,128)(2,1)S(1)}, bf16[1,128,512]{2,1,0:T(8,128)(2,1)S(1)}, u32[]{:S(2)}, u32[]{:S(2)}) collective-permute-start(bf16[1,128,512]{2,1,0:T(8,128)(2,1)S(1)} %get-tuple-element.37), channel_id=1, source_target_pairs={{0,17},{1,16},{2,19},{3,18},{4,21},{5,20},{6,23},{7,22},{8,5},{9,4... | collective-permute-start | bytes 393224 | tf_op jit(solution)/shard_map/ppermute | solution.py:389
  32.8 15.7 %collective-permute-start.8 = (bf16[1,128,512]{2,1,0:T(8,128)(2,1)S(1)}, bf16[1,128,512]{2,1,0:T(8,128)(2,1)S(1)}, u32[]{:S(2)}, u32[]{:S(2)}) collective-permute-start(bf16[1,128,512]{2,1,0:T(8,128)(2,1)S(1)} %get-tuple-element.38), channel_id=1, source_target_pairs={{0,16},{1,17},{2,18},{3,19},{4,20},{5,21},{6,22},{7,23},{8,4},{9,5... | collective-permute-start | bytes 393224 | tf_op jit(solution)/shard_map/ppermute | solution.py:389
  32.9 15.6 %collective-permute-start.7 = (bf16[1,128,512]{2,1,0:T(8,128)(2,1)S(1)}, bf16[1,128,512]{2,1,0:T(8,128)(2,1)S(1)}, u32[]{:S(2)}, u32[]{:S(2)}) collective-permute-start(bf16[1,128,512]{2,1,0:T(8,128)(2,1)S(1)} %get-tuple-element.39), channel_id=1, source_target_pairs={{0,7},{1,6},{2,5},{3,4},{4,3},{5,2},{6,1},{7,0},{8,19},{9,18},{10,... | collective-permute-start | bytes 393224 | tf_op jit(solution)/shard_map/ppermute | solution.py:389
  40.3 8.4 %collective-permute-start.6 = (bf16[1,128,512]{2,1,0:T(8,128)(2,1)S(1)}, bf16[1,128,512]{2,1,0:T(8,128)(2,1)S(1)}, u32[]{:S(2)}, u32[]{:S(2)}) collective-permute-start(bf16[1,128,512]{2,1,0:T(8,128)(2,1)S(1)} %get-tuple-element.40), channel_id=1, source_target_pairs={{0,6},{1,7},{2,4},{3,5},{4,2},{5,3},{6,0},{7,1},{8,18},{9,19},{10,... | collective-permute-start | bytes 393224 | tf_op jit(solution)/shard_map/ppermute | solution.py:389
  40.3 9.3 %collective-permute-start.5 = (bf16[1,128,512]{2,1,0:T(8,128)(2,1)S(1)}, bf16[1,128,512]{2,1,0:T(8,128)(2,1)S(1)}, u32[]{:S(2)}, u32[]{:S(2)}) collective-permute-start(bf16[1,128,512]{2,1,0:T(8,128)(2,1)S(1)} %get-tuple-element.41), channel_id=1, source_target_pairs={{0,5},{1,4},{2,7},{3,6},{4,1},{5,0},{6,3},{7,2},{8,17},{9,16},{10,... | collective-permute-start | bytes 393224 | tf_op jit(solution)/shard_map/ppermute | solution.py:389
  41.3 9.3 %collective-permute-start.4 = (bf16[1,128,512]{2,1,0:T(8,128)(2,1)S(1)}, bf16[1,128,512]{2,1,0:T(8,128)(2,1)S(1)}, u32[]{:S(2)}, u32[]{:S(2)}) collective-permute-start(bf16[1,128,512]{2,1,0:T(8,128)(2,1)S(1)} %get-tuple-element.42), channel_id=1, source_target_pairs={{0,4},{1,5},{2,6},{3,7},{4,0},{5,1},{6,2},{7,3},{8,16},{9,17},{10,... | collective-permute-start | bytes 393224 | tf_op jit(solution)/shard_map/ppermute | solution.py:389
  50.7 2.6 %collective-permute-start.16 = (bf16[1024,128]{1,0:T(8,128)(2,1)S(1)}, bf16[1024,128]{1,0:T(8,128)(2,1)S(1)}, u32[]{:S(2)}, u32[]{:S(2)}) collective-permute-start(bf16[1024,128]{1,0:T(8,128)(2,1)S(1)} %edges.1), channel_id=1, source_target_pairs={{0,8},{8,0},{16,24},{24,16},{1,9},{9,1},{17,25},{25,17},{2,10},{10... | collective-permute-start | bytes 786440 | tf_op jit(solution)/shard_map/ppermute | solution.py:390
  60.6 17.0 %collective-permute-start.21 = (bf16[128,1024]{1,0:T(8,128)(2,1)S(1)}, bf16[128,1024]{1,0:T(8,128)(2,1)S(1)}, u32[]{:S(2)}, u32[]{:S(2)}) collective-permute-start(bf16[128,1024]{1,0:T(8,128)(2,1)S(1)} %get-tuple-element.27), channel_id=1, source_target_pairs={{0,4},{1,5},{2,6},{3,7},{4,12},{5,13},{6,14},{7,15},{8,0},{9,1},{1... | collective-permute-start | bytes 786440 | tf_op jit(solution)/shard_map/ppermute | solution.py:401
  61.0 18.6 %collective-permute-start.22 = (bf16[128,1024]{1,0:T(8,128)(2,1)S(1)}, bf16[128,1024]{1,0:T(8,128)(2,1)S(1)}, u32[]{:S(2)}, u32[]{:S(2)}) collective-permute-start(bf16[128,1024]{1,0:T(8,128)(2,1)S(1)} %get-tuple-element.28), channel_id=1, source_target_pairs={{0,5},{1,4},{2,7},{3,6},{4,13},{5,12},{6,15},{7,14},{8,1},{9,0},{1... | collective-permute-start | bytes 786440 | tf_op jit(solution)/shard_map/ppermute | solution.py:401
  64.6 34.0 %collective-permute-start.23 = (bf16[128,1024]{1,0:T(8,128)(2,1)S(1)}, bf16[128,1024]{1,0:T(8,128)(2,1)S(1)}, u32[]{:S(2)}, u32[]{:S(2)}) collective-permute-start(bf16[128,1024]{1,0:T(8,128)(2,1)S(1)} %get-tuple-element.29), channel_id=1, source_target_pairs={{0,6},{1,7},{2,4},{3,5},{4,14},{5,15},{6,12},{7,13},{8,2},{9,3},{1... | collective-permute-start | bytes 786440 | tf_op jit(solution)/shard_map/ppermute | solution.py:401
  64.6 41.3 %collective-permute-start.24 = (bf16[128,1024]{1,0:T(8,128)(2,1)S(1)}, bf16[128,1024]{1,0:T(8,128)(2,1)S(1)}, u32[]{:S(2)}, u32[]{:S(2)}) collective-permute-start(bf16[128,1024]{1,0:T(8,128)(2,1)S(1)} %get-tuple-element.30), channel_id=1, source_target_pairs={{0,7},{1,6},{2,5},{3,4},{4,15},{5,14},{6,13},{7,12},{8,3},{9,2},{1... | collective-permute-start | bytes 786440 | tf_op jit(solution)/shard_map/ppermute | solution.py:401
  74.0 31.9 %collective-permute-start.17 = (bf16[128,1024]{1,0:T(8,128)(2,1)S(1)}, bf16[128,1024]{1,0:T(8,128)(2,1)S(1)}, u32[]{:S(2)}, u32[]{:S(2)}) collective-permute-start(bf16[128,1024]{1,0:T(8,128)(2,1)S(1)} %get-tuple-element.23), channel_id=1, source_target_pairs={{0,0},{1,1},{2,2},{3,3},{4,8},{5,9},{6,10},{7,11},{8,4},{9,5},{10,... | collective-permute-start | bytes 786440 | tf_op jit(solution)/shard_map/ppermute | solution.py:401
  77.6 28.3 %collective-permute-start.18 = (bf16[128,1024]{1,0:T(8,128)(2,1)S(1)}, bf16[128,1024]{1,0:T(8,128)(2,1)S(1)}, u32[]{:S(2)}, u32[]{:S(2)}) collective-permute-start(bf16[128,1024]{1,0:T(8,128)(2,1)S(1)} %get-tuple-element.24), channel_id=1, source_target_pairs={{0,1},{1,0},{2,3},{3,2},{4,9},{5,8},{6,11},{7,10},{8,5},{9,4},{10,... | collective-permute-start | bytes 786440 | tf_op jit(solution)/shard_map/ppermute | solution.py:401
  79.6 27.3 %collective-permute-start.19 = (bf16[128,1024]{1,0:T(8,128)(2,1)S(1)}, bf16[128,1024]{1,0:T(8,128)(2,1)S(1)}, u32[]{:S(2)}, u32[]{:S(2)}) collective-permute-start(bf16[128,1024]{1,0:T(8,128)(2,1)S(1)} %get-tuple-element.25), channel_id=1, source_target_pairs={{0,2},{1,3},{2,0},{3,1},{4,10},{5,11},{6,8},{7,9},{8,6},{9,7},{10,... | collective-permute-start | bytes 786440 | tf_op jit(solution)/shard_map/ppermute | solution.py:401
  98.6 12.1 %collective-permute-start.20 = (bf16[128,1024]{1,0:T(8,128)(2,1)S(1)}, bf16[128,1024]{1,0:T(8,128)(2,1)S(1)}, u32[]{:S(2)}, u32[]{:S(2)}) collective-permute-start(bf16[128,1024]{1,0:T(8,128)(2,1)S(1)} %get-tuple-element.26), channel_id=1, source_target_pairs={{0,3},{1,2},{2,1},{3,0},{4,11},{5,10},{6,9},{7,8},{8,7},{9,6},{10,... | collective-permute-start | bytes 786440 | tf_op jit(solution)/shard_map/ppermute | solution.py:401

commit v3 on v2

--- a/solution.py
+++ b/solution.py
@@ -17,6 +17,8 @@
 COLS = 256
 MARGIN = 128
 ALIGN = 16
+SHARES = (4, 4, 2)
+PLACED = ((0, 4), (4, 8))
 VMEM_BYTES = 40 * 2**20
 FIRST_STEPS = 4
 
@@ -134,22 +136,37 @@
     return core, brick ^ (step % bricks) ^ (core * (bricks // 2))
 
 
-def plane_kernel(bricks, part, row_shift, frac_index, *refs):
+def halo_sides(total, wanted):
+    return 1 if 2 * wanted == total else 2
+
+
+def rows_kernel(bricks, first_k, count_out, row_shift, frac_index, *refs):
     pieces, refs = refs[: 2 * bricks], refs[2 * bricks :]
     side, x_forward, x_back, y_forward, y_back = refs[:5]
-    outs, refs = refs[5 : 5 + bricks // 2], refs[5 + bricks // 2 :]
+    outs, refs = refs[5 : 5 + count_out], refs[5 + count_out :]
     raw, observed, estimate, blur_in, back_in, wide, ratio, arrived = refs
     y, core, brick_index = place_in_chip()
     plane = y * bricks + brick_index
     shift, fraction = row_shift[plane], frac_index[plane]
     _, brick, own = pieces[0].shape
     rows, width = observed.shape
-    lead = raw.shape[0] - bricks * brick
-    half = core ^ part
-    first_row = half * (bricks * brick - rows)
+    total, wanted = bricks * brick, count_out * brick
+    lead = raw.shape[0] - total
     windows = column_windows(width)
-    tiles = [(r, min(ROWS, rows - r)) for r in range(0, rows, ROWS)]
     begin = core * HALO
+
+    first_out = core * (bricks // 2) + brick_index % (bricks // 2)
+    first_wanted = ((first_out ^ first_k) // count_out) * wanted
+    first_row = jnp.clip(first_wanted - HALO, 0, total - rows)
+
+    def reach(extra):
+        count = wanted + halo_sides(total, wanted) * extra
+        start = jnp.clip(first_wanted - extra, 0, total - count) - first_row
+        return start, count
+
+    def tiles_of(start, count):
+        for r in range(0, count, ROWS):
+            yield pl.multiple_of(start + r, RADIUS), min(ROWS, count - r)
 
     copies = []
     for step in range(2 * bricks):
@@ -158,7 +175,7 @@
         there = pl.ds(pl.multiple_of(begin + source_core * own, 128), own)
         copies.append((pieces[step].at[0], raw.at[here, there]))
     there = pl.ds(pl.multiple_of((1 - core) * 2 * own, 128), HALO)
-    copies.append((side, raw.at[pl.ds(lead, bricks * brick), there]))
+    copies.append((side, raw.at[pl.ds(lead, total), there]))
     copies = [
         pltpu.make_async_copy(source, target, arrived.at[i])
         for i, (source, target) in enumerate(copies)
@@ -182,7 +199,8 @@
     mixing = mixing.astype(jnp.bfloat16)
     for copy in copies:
         copy.wait()
-    for r, count in tiles:
+    for r in range(0, rows, ROWS):
+        count = min(ROWS, rows - r)
         window = raw[pl.ds(pl.multiple_of(base + r, ALIGN), count + ALIGN), :]
         moved = jnp.dot(
             mixing[:count, : count + ALIGN], window, preferred_element_type=jnp.float32
@@ -191,47 +209,58 @@
         observed[r : r + count, :] = level
         blur_in[RADIUS + r : RADIUS + r + count, :] = level.astype(jnp.bfloat16)
 
+    extra = HALO
     for turn in range(ITERS):
-        for r, count in tiles:
-            wide[r : r + count, :] = jnp.dot(
-                y_forward[:count, : count + 2 * RADIUS],
-                blur_in[r : r + count + 2 * RADIUS, :],
+        extra -= RADIUS
+        start, count = reach(extra)
+        for r, tile in tiles_of(start, count):
+            wide[pl.ds(r, tile), :] = jnp.dot(
+                y_forward[:tile, : tile + 2 * RADIUS],
+                blur_in[pl.ds(r, tile + 2 * RADIUS), :],
                 preferred_element_type=jnp.float32,
             ).astype(jnp.bfloat16)
-        for r in range(0, rows, rows // 2):
-            tall = slice(r, r + rows // 2)
-            for start, count, low, high, row in windows:
-                blurred = jnp.dot(
-                    wide[tall, low:high],
-                    x_forward[row : row + high - low, :count],
-                    preferred_element_type=jnp.float32,
-                )
-                top = observed[tall, start : start + count]
-                quotient = top * pl.reciprocal(blurred, approx=True)
-                ratio[tall, start : start + count] = quotient.astype(jnp.bfloat16)
-            for start, count, low, high, row in windows:
-                back_in[RADIUS + r : RADIUS + r + rows // 2, start : start + count] = jnp.dot(
-                    ratio[tall, low:high],
-                    x_back[row : row + high - low, :count],
-                    preferred_element_type=jnp.float32,
-                ).astype(jnp.bfloat16)
-        for r, count in tiles:
-            correction = jnp.dot(
-                y_back[:count, : count + 2 * RADIUS],
-                back_in[r : r + count + 2 * RADIUS, :],
+        tall = pl.ds(pl.multiple_of(start, RADIUS), count)
+        tall_in = pl.ds(pl.multiple_of(start + RADIUS, RADIUS), count)
+        for column, span, low, high, row in windows:
+            blurred = jnp.dot(
+                wide[tall, low:high],
+                x_forward[row : row + high - low, :span],
                 preferred_element_type=jnp.float32,
             )
-            before = observed if turn == 0 else estimate
-            updated = before[r : r + count, :] * correction
-            estimate[r : r + count, :] = updated
-            if turn < ITERS - 1:
-                blur_in[RADIUS + r : RADIUS + r + count, :] = updated.astype(jnp.bfloat16)
-    first_out = core * (bricks // 2) + brick_index % (bricks // 2)
-    here = pl.ds(pl.multiple_of(begin, 128), 2 * own)
+            quotient = observed[tall, column : column + span] * pl.reciprocal(blurred, approx=True)
+            ratio[tall, column : column + span] = quotient.astype(jnp.bfloat16)
+        for column, span, low, high, row in windows:
+            back_in[tall_in, column : column + span] = jnp.dot(
+                ratio[tall, low:high],
+                x_back[row : row + high - low, :span],
+                preferred_element_type=jnp.float32,
+            ).astype(jnp.bfloat16)
+        extra -= RADIUS
+        before = observed if turn == 0 else estimate
+        if turn == ITERS - 1:
+            break
+        for r, tile in tiles_of(*reach(extra)):
+            correction = jnp.dot(
+                y_back[:tile, : tile + 2 * RADIUS],
+                back_in[pl.ds(r, tile + 2 * RADIUS), :],
+                preferred_element_type=jnp.float32,
+            )
+            updated = before[pl.ds(r, tile), :] * correction
+            estimate[pl.ds(r, tile), :] = updated
+            blur_in[pl.ds(pl.multiple_of(r + RADIUS, RADIUS), tile), :] = updated.astype(
+                jnp.bfloat16
+            )
+
+    columns = pl.ds(pl.multiple_of(begin, 128), 2 * own)
     for i, out in enumerate(outs):
-        place = first_out ^ (part * (bricks // 2) + i)
-        start = pl.multiple_of(place * brick - first_row, ALIGN)
-        squared = jnp.square(estimate[pl.ds(start, brick), here])
+        place = first_out ^ (first_k + i)
+        r = pl.multiple_of(place * brick - first_row, RADIUS)
+        correction = jnp.dot(
+            y_back[:brick, : brick + 2 * RADIUS],
+            back_in[pl.ds(r, brick + 2 * RADIUS), columns],
+            preferred_element_type=jnp.float32,
+        )
+        squared = jnp.square(before[pl.ds(r, brick), columns] * correction)
         out[...] = jnp.square(squared).astype(out.dtype)
 
 
@@ -267,20 +296,21 @@
     )(rows)
 
 
-def deconvolve_rows(part, tables, pieces, side, matrices, lead):
+def deconvolve_rows(first_k, count, tables, pieces, side, matrices, lead):
     bricks = len(pieces) // 2
     _, brick, own = pieces[0].shape
-    rows, width = bricks * brick // 2 + HALO, 2 * own + HALO
+    total, wanted = bricks * brick, count * brick
+    rows, width = wanted + halo_sides(total, wanted) * HALO, 2 * own + HALO
     vmem = pl.BlockSpec(memory_space=pltpu.VMEM)
     smem = pl.BlockSpec(memory_space=pltpu.SMEM)
     anywhere = pl.BlockSpec(memory_space=pl.ANY)
     return pl.pallas_call(
-        functools.partial(plane_kernel, bricks, part),
-        out_shape=[jax.ShapeDtypeStruct((brick, 2 * own), jnp.bfloat16)] * (bricks // 2),
+        functools.partial(rows_kernel, bricks, first_k, count),
+        out_shape=[jax.ShapeDtypeStruct((brick, 2 * own), jnp.bfloat16)] * count,
         in_specs=[smem] * 2 + [anywhere] * (2 * bricks + 1) + [vmem] * 4,
-        out_specs=[vmem] * (bricks // 2),
+        out_specs=[vmem] * count,
         scratch_shapes=[
-            pltpu.VMEM((lead + bricks * brick, width), jnp.bfloat16),
+            pltpu.VMEM((lead + total, width), jnp.bfloat16),
             pltpu.VMEM((rows, width), jnp.float32),
             pltpu.VMEM((rows, width), jnp.float32),
             pltpu.VMEM((rows + 2 * RADIUS, width), jnp.bfloat16),
@@ -333,31 +363,38 @@
     )(*pieces)
 
 
-def place_kernel(*refs):
-    pieces, out = refs[:-1], refs[-1]
-    width = pieces[0].shape[1]
-    group = len(pieces) // 2
-    for k, piece in enumerate(pieces):
-        source = lax.axis_index("ybrick") ^ k
-
-        @pl.when(source % group == pl.program_id(0))
-        def _(piece=piece, source=source):
-            here = pl.ds(pl.multiple_of((source // group) * width, 128), width)
-            out[0, :, here] = lax.rsqrt(lax.rsqrt(piece[...].astype(out.dtype)))
-
-
-def place_planes(pieces):
+def place_kernel(count, spots, *refs):
+    del spots
+    pieces, out = refs[:count], refs[-1]
+    for i, piece in enumerate(pieces):
+
+        @pl.when(pl.program_id(0) == i)
+        def _(piece=piece):
+            out[0] = lax.rsqrt(lax.rsqrt(piece[...].astype(out.dtype)))
+
+
+def place_pieces(first, brick_index, pieces, bricks, before):
     brick, width = pieces[0].shape
-    group = len(pieces) // 2
+    planes, count = bricks // 2, len(pieces)
+    sources = brick_index ^ jnp.arange(first, first + count, dtype=jnp.int32)
+    spots = jnp.concatenate([sources % planes, sources // planes])
+    kept = [] if before is None else [before]
     return pl.pallas_call(
-        place_kernel,
-        grid=(group,),
-        out_shape=jax.ShapeDtypeStruct((group, brick, 2 * width), jnp.float32),
-        in_specs=[pl.BlockSpec(memory_space=pltpu.VMEM)] * len(pieces),
-        out_specs=pl.BlockSpec((1, brick, 2 * width), lambda i: (i, 0, 0)),
+        functools.partial(place_kernel, count),
+        grid_spec=pltpu.PrefetchScalarGridSpec(
+            num_scalar_prefetch=1,
+            grid=(count,),
+            in_specs=[pl.BlockSpec(memory_space=pltpu.VMEM)] * count
+            + [pl.BlockSpec(memory_space=pl.ANY)] * len(kept),
+            out_specs=pl.BlockSpec(
+                (1, brick, width), lambda i, spots: (spots[i], 0, spots[count + i])
+            ),
+        ),
+        out_shape=jax.ShapeDtypeStruct((planes, brick, 2 * width), jnp.float32),
+        input_output_aliases={1 + count: 0} if kept else {},
         compiler_params=pltpu.CompilerParams(vmem_limit_bytes=VMEM_BYTES),
-        name="place_planes",
-    )(*pieces)
+        name="place_pieces",
+    )(spots, *pieces, *kept)
 
 
 def after(x, *earlier):
@@ -388,25 +425,30 @@
             route.append(((2 * y + c) * bricks + i, target))
         pieces.append(lax.ppermute(piece, ("scan", "ybrick"), route))
     side = lax.ppermute(edges(pieces), "scan", [(s, s ^ 1) for s in range(4)])
-    done = []
-    for part in range(2):
-        done += deconvolve_rows(part, (row_shift, frac_index), pieces, side, matrices, lead)
-
     arrived = []
-    for k in range(bricks):
-        route = []
-        for y, c, i in devices:
-            target = (2 * y + i // half) * bricks + ((c * half + i % half) ^ k)
-            route.append(((2 * y + c) * bricks + i, target))
-        arrived.append(lax.ppermute(done[k], ("scan", "ybrick"), route))
-    return place_planes(arrived)
+    for share in SHARES:
+        k = len(arrived)
+        tables = (row_shift, frac_index)
+        done = deconvolve_rows(k, bricks // share, tables, pieces, side, matrices, lead)
+        for k, piece in enumerate(done, k):
+            route = []
+            for y, c, i in devices:
+                target = (2 * y + i // half) * bricks + ((c * half + i % half) ^ k)
+                route.append(((2 * y + c) * bricks + i, target))
+            arrived.append(lax.ppermute(piece, ("scan", "ybrick"), route))
+    out = None
+    for first, last in PLACED:
+        first, last = first * bricks // 8, last * bricks // 8
+        out = place_pieces(first, b, arrived[first:last], bricks, out)
+    return out
 
 
 def local(raw, row_shift, frac_index, psf_y, psf_x):
     planes, brick, own = raw.shape
     bricks, scans = lax.axis_size("ybrick"), lax.axis_size("scan")
-    fits = scans == 4 and planes == 2 * bricks and bricks >= 4 and bricks & (bricks - 1) == 0
-    fits = fits and brick % ALIGN == 0 and own % HALO == 0
+    fits = scans == 4 and planes == 2 * bricks and bricks >= max(SHARES) and bricks & (bricks - 1) == 0
+    fits = fits and brick % RADIUS == 0 and own % HALO == 0 and brick <= ROWS
+    fits = fits and bricks // max(SHARES) * brick + 2 * HALO <= bricks * brick
     plan = by_planes if fits else by_bricks
     return plan(raw, row_shift, frac_index, psf_y, psf_x)
 

time: 114 us -> 112 us (0.982)
  waiting for transfers between devices: 34.2 us -> 26.3 us
  Pallas kernels: 17.9 us -> 23.8 us
    ppermute x8, waiting for transfers between devices: 28.2 us -> 19.4 us  [by_planes(): arrived.append(lax.ppermute(piece, ('scan', 'ybrick'), route))]
    pallas_call x3 -> x5, Pallas kernels: 17.5 us -> 23.4 us  [the longest x3 18.1 us: deconvolve_rows(): pl.pallas_call(functools.partial(rows_kernel, bricks, first_k, count), ou...]
  transfers between devices with their start and end apart: 25 -> 25, of which waited for: 10 -> 9; matrix products, arithmetic and copies ran while one was open for 2% -> 2% of each run, Pallas kernels for 7% -> 14%
where the time goes in v3:
time: 112 us
  starting transfers between devices  58.2 us (52%)
  waiting for transfers between devices  26.3 us (23%)
  Pallas kernels  23.8 us (21%)
  local copies, waits for them, and re-layouts  2.91 us (3%)
    ppermute x16, starting transfers between devices, by_planes(): pieces.append(lax.ppermute(piece, ('scan', 'ybrick'), route))  41.7 us
    ppermute x8, waiting for transfers between devices, by_planes(): arrived.append(lax.ppermute(piece, ('scan', 'ybrick'), route))  19.4 us
    pallas_call x3, Pallas kernels, deconvolve_rows(): pl.pallas_call(functools.partial(rows_kernel, bricks, first_k, count), ou...  18.1 us
    ppermute x8, starting transfers between devices, by_planes(): arrived.append(lax.ppermute(piece, ('scan', 'ybrick'), route))  15.3 us
    ppermute x16, waiting for transfers between devices, by_planes(): pieces.append(lax.ppermute(piece, ('scan', 'ybrick'), route))  6.19 us
    pallas_call x2, Pallas kernels, place_pieces(): pl.pallas_call(functools.partial(place_kernel, count), grid_spec=pltpu.Pr...  5.3 us
    dynamic_slice x2, local copies, waits for them, and re-layouts, by_planes(): piece = lax.dynamic_slice_in_dim(raw, plane, 1, 0)  2.7 us
  transfers between devices with their start and end apart: 25, of which 9 were waited for; matrix products, arithmetic and copies ran while one was open for 2% of the time, Pallas kernels for 14%

profile of v3, /device:TPU:9, one launch (start us, length us, event | category | flops | bytes accessed | tf_op | source)
XLA Modules:
  0.0 111.7 jit_solution(6251027408443361993)
XLA Ops:
  0.0 1.1 %constant_dynamic-slice_fusion.12 = (bf16[1,128,512]{2,1,0:T(8,128)(2,1)S(1)}, bf16[1,128,512]{2,1,0:T(8,128)(2,1)S(1)}, bf16[1,128,512]{2,1,0:T(8,128)(2,1)S(1)}, bf16[1,128,512]{2,1,0:T(8,128)(2,1)S(1)}) fusion(bf16[16,128,512]{2,1,0:T(8,128)(2,1)} %param.5, s32[]{:T(128)S(6)} %select_n.79, s32[]{:T(128)S(6)} %select_n.78, s32[]{:T(128)S(6)} %select_n.77, ...), kind=kLoop, calls=%fused_computation.12 | loop fusion | bytes 1048592 | tf_op jit(solution)/shard_map/dynamic_slice | solution.py:419
  1.1 3.8 %collective-permute-start.3 = (bf16[1,128,512]{2,1,0:T(8,128)(2,1)S(1)}, bf16[1,128,512]{2,1,0:T(8,128)(2,1)S(1)}, u32[]{:S(2)}, u32[]{:S(2)}) collective-permute-start(bf16[1,128,512]{2,1,0:T(8,128)(2,1)S(1)} %get-tuple-element.43), channel_id=1, source_target_pairs={{0,3},{1,2},{2,1},{3,0},{4,7},{5,6},{6,5},{7,4},{8,23},{9,22},{10,... | collective-permute-start | bytes 393224 | tf_op jit(solution)/shard_map/ppermute | solution.py:426
  4.9 1.0 collective-permute-start.2
  5.9 1.5 %collective-permute-start.1 = (bf16[1,128,512]{2,1,0:T(8,128)(2,1)S(1)}, bf16[1,128,512]{2,1,0:T(8,128)(2,1)S(1)}, u32[]{:S(2)}, u32[]{:S(2)}) collective-permute-start(bf16[1,128,512]{2,1,0:T(8,128)(2,1)S(1)} %get-tuple-element.45), channel_id=1, source_target_pairs={{0,1},{1,0},{2,3},{3,2},{4,5},{5,4},{6,7},{7,6},{8,21},{9,20},{10,... | collective-permute-start | bytes 393224 | tf_op jit(solution)/shard_map/ppermute | solution.py:426
  7.4 2.7 %collective-permute-start = (bf16[1,128,512]{2,1,0:T(8,128)(2,1)S(1)}, bf16[1,128,512]{2,1,0:T(8,128)(2,1)S(1)}, u32[]{:S(2)}, u32[]{:S(2)}) collective-permute-start(bf16[1,128,512]{2,1,0:T(8,128)(2,1)S(1)} %get-tuple-element.46), channel_id=1, source_target_pairs={{0,0},{1,1},{2,2},{3,3},{4,4},{5,5},{6,6},{7,7},{8,20},{9,21},{10,... | collective-permute-start | bytes 393224 | tf_op jit(solution)/shard_map/ppermute | solution.py:426
  10.3 0.0 copy-start.2
  10.3 0.0 copy-start.3
  10.3 0.0 copy-start
  10.3 0.0 copy-start.1
  10.3 1.6 %constant_dynamic-slice_fusion = (bf16[1,128,512]{2,1,0:T(8,128)(2,1)S(1)}, bf16[1,128,512]{2,1,0:T(8,128)(2,1)S(1)}, bf16[1,128,512]{2,1,0:T(8,128)(2,1)S(1)}, ...) fusion(bf16[16,128,512]{2,1,0:T(8,128)(2,1)} %param.5, ...), kind=kLoop, calls=%fused_computation | loop fusion | bytes 3145776 | tf_op jit(solution)/shard_map/dynamic_slice | solution.py:419
  11.9 0.1 collective-permute-start.15
  12.0 0.0 collective-permute-done.3.refs_3_
  12.0 6.2 %collective-permute-start.14 = (bf16[1,128,512]{2,1,0:T(8,128)(2,1)S(1)}, bf16[1,128,512]{2,1,0:T(8,128)(2,1)S(1)}, u32[]{:S(2)}, u32[]{:S(2)}) collective-permute-start(bf16[1,128,512]{2,1,0:T(8,128)(2,1)S(1)} %get-tuple-element.32), channel_id=1, source_target_pairs={{0,22},{1,23},{2,20},{3,21},{4,18},{5,19},{6,16},{7,17},{8,2},{9,3... | collective-permute-start | bytes 393224 | tf_op jit(solution)/shard_map/ppermute | solution.py:426
  18.2 0.0 collective-permute-done.2.refs_2_
  18.2 0.0 collective-permute-start.13
  18.2 0.0 collective-permute-done.1.refs_1_
  18.2 0.1 collective-permute-start.12
  18.3 0.0 collective-permute-done.refs_0_
  18.3 3.1 %collective-permute-start.11 = (bf16[1,128,512]{2,1,0:T(8,128)(2,1)S(1)}, bf16[1,128,512]{2,1,0:T(8,128)(2,1)S(1)}, u32[]{:S(2)}, u32[]{:S(2)}) collective-permute-start(bf16[1,128,512]{2,1,0:T(8,128)(2,1)S(1)} %get-tuple-element.35), channel_id=1, source_target_pairs={{0,19},{1,18},{2,17},{3,16},{4,23},{5,22},{6,21},{7,20},{8,7},{9,6... | collective-permute-start | bytes 393224 | tf_op jit(solution)/shard_map/ppermute | solution.py:426
  21.4 0.0 collective-permute-done.15.refs_15_
  21.4 11.4 %collective-permute-start.10 = (bf16[1,128,512]{2,1,0:T(8,128)(2,1)S(1)}, bf16[1,128,512]{2,1,0:T(8,128)(2,1)S(1)}, u32[]{:S(2)}, u32[]{:S(2)}) collective-permute-start(bf16[1,128,512]{2,1,0:T(8,128)(2,1)S(1)} %get-tuple-element.36), channel_id=1, source_target_pairs={{0,18},{1,19},{2,16},{3,17},{4,22},{5,23},{6,20},{7,21},{8,6},{9,7... | collective-permute-start | bytes 393224 | tf_op jit(solution)/shard_map/ppermute | solution.py:426
  32.8 0.0 collective-permute-done.14.refs_14_
  32.8 0.0 collective-permute-start.9
  32.8 0.0 collective-permute-done.13.refs_13_
  32.8 0.1 collective-permute-start.8
  32.9 0.0 collective-permute-done.12.refs_12_
  32.9 7.5 %collective-permute-start.7 = (bf16[1,128,512]{2,1,0:T(8,128)(2,1)S(1)}, bf16[1,128,512]{2,1,0:T(8,128)(2,1)S(1)}, u32[]{:S(2)}, u32[]{:S(2)}) collective-permute-start(bf16[1,128,512]{2,1,0:T(8,128)(2,1)S(1)} %get-tuple-element.39), channel_id=1, source_target_pairs={{0,7},{1,6},{2,5},{3,4},{4,3},{5,2},{6,1},{7,0},{8,19},{9,18},{10,... | collective-permute-start | bytes 393224 | tf_op jit(solution)/shard_map/ppermute | solution.py:426
  40.3 0.0 collective-permute-done.11.refs_11_
  40.3 0.0 collective-permute-start.6
  40.4 0.0 collective-permute-done.10.refs_10_
  40.4 0.1 collective-permute-start.5
  40.4 1.5 %collective-permute-done.9.refs_9_ = bf16[1,128,512]{2,1,0:T(8,128)(2,1)S(1)} collective-permute-done((bf16[1,128,512]{2,1,0:T(8,128)(2,1)S(1)}, bf16[1,128,512]{2,1,0:T(8,128)(2,1)S(1)}, u32[]{:S(2)}, u32[]{:S(2)}) %collective-permute-start.9) | collective-permute-done | bytes 131104 | tf_op jit(solution)/shard_map/ppermute | solution.py:426
  41.9 4.2 %collective-permute-start.4 = (bf16[1,128,512]{2,1,0:T(8,128)(2,1)S(1)}, bf16[1,128,512]{2,1,0:T(8,128)(2,1)S(1)}, u32[]{:S(2)}, u32[]{:S(2)}) collective-permute-start(bf16[1,128,512]{2,1,0:T(8,128)(2,1)S(1)} %get-tuple-element.42), channel_id=1, source_target_pairs={{0,4},{1,5},{2,6},{3,7},{4,0},{5,1},{6,2},{7,3},{8,16},{9,17},{10,... | collective-permute-start | bytes 393224 | tf_op jit(solution)/shard_map/ppermute | solution.py:426
  46.1 2.6 %collective-permute-done.8.refs_8_ = bf16[1,128,512]{2,1,0:T(8,128)(2,1)S(1)} collective-permute-done((bf16[1,128,512]{2,1,0:T(8,128)(2,1)S(1)}, bf16[1,128,512]{2,1,0:T(8,128)(2,1)S(1)}, u32[]{:S(2)}, u32[]{:S(2)}) %collective-permute-start.8) | collective-permute-done | bytes 131104 | tf_op jit(solution)/shard_map/ppermute | solution.py:426
  48.7 0.0 collective-permute-done.7.refs_7_
  48.7 0.2 collective-permute-done.6.refs_6_
  48.9 0.6 collective-permute-done.5.refs_5_
  49.5 1.3 %collective-permute-done.4.refs_4_ = bf16[1,128,512]{2,1,0:T(8,128)(2,1)S(1)} collective-permute-done((bf16[1,128,512]{2,1,0:T(8,128)(2,1)S(1)}, bf16[1,128,512]{2,1,0:T(8,128)(2,1)S(1)}, u32[]{:S(2)}, u32[]{:S(2)}) %collective-permute-start.4) | collective-permute-done | bytes 131104 | tf_op jit(solution)/shard_map/ppermute | solution.py:426
  50.8 0.1 edges.1
  50.9 1.2 %collective-permute-start.16 = (bf16[1024,128]{1,0:T(8,128)(2,1)S(1)}, bf16[1024,128]{1,0:T(8,128)(2,1)S(1)}, u32[]{:S(2)}, u32[]{:S(2)}) collective-permute-start(bf16[1024,128]{1,0:T(8,128)(2,1)S(1)} %edges.1), channel_id=1, source_target_pairs={{0,8},{8,0},{16,24},{24,16},{1,9},{9,1},{17,25},{25,17},{2,10},{10... | collective-permute-start | bytes 786440 | tf_op jit(solution)/shard_map/ppermute | solution.py:427
  52.2 0.1 rev.7
  52.3 0.1 rev.6
  52.4 0.2 band_matrices.1
  52.6 0.7 collective-permute-done.16.refs_16_
  53.3 5.6 %deconvolve_rows.5 = (bf16[128,1024]{1,0:T(8,128)(2,1)S(1)}, bf16[128,1024]{1,0:T(8,128)(2,1)S(1)}) custom-call(s32[16]{0:T(128)S(1)} %copy-done, s32[16]{0:T(128)S(1)} %copy-done.1, bf16[1,128,512]{2,1,0:T(8,128)(2,1)S(1)} %collective-permute-done.refs_0_, bf16[1,128,512]{2,1,0:T(8,128)(2,1)S(1)} %collective-permute-done.1.refs_1_, ...), custom_call_target="tpu_custom_call" | custom-call | tf_op jit(solution)/shard_map/deconvolve_rows/pallas_call | solution.py:307
  58.9 0.8 collective-permute-start.23
  59.7 2.7 %collective-permute-start.24 = (bf16[128,1024]{1,0:T(8,128)(2,1)S(1)}, bf16[128,1024]{1,0:T(8,128)(2,1)S(1)}, u32[]{:S(2)}, u32[]{:S(2)}) collective-permute-start(bf16[128,1024]{1,0:T(8,128)(2,1)S(1)} %get-tuple-element.30), channel_id=1, source_target_pairs={{0,3},{1,2},{2,1},{3,0},{4,11},{5,10},{6,9},{7,8},{8,7},{9,6},{10,... | collective-permute-start | bytes 786440 | tf_op jit(solution)/shard_map/ppermute | solution.py:438
  62.4 5.4 %deconvolve_rows.4 = (bf16[128,1024]{1,0:T(8,128)(2,1)S(1)}, bf16[128,1024]{1,0:T(8,128)(2,1)S(1)}) custom-call(s32[16]{0:T(128)S(1)} %copy-done, s32[16]{0:T(128)S(1)} %copy-done.1, bf16[1,128,512]{2,1,0:T(8,128)(2,1)S(1)} %collective-permute-done.refs_0_, bf16[1,128,512]{2,1,0:T(8,128)(2,1)S(1)} %collective-permute-done.1.refs_1_, ...), custom_call_target="tpu_custom_call" | custom-call | tf_op jit(solution)/shard_map/deconvolve_rows/pallas_call | solution.py:307
  67.8 5.6 %collective-permute-start.21 = (bf16[128,1024]{1,0:T(8,128)(2,1)S(1)}, bf16[128,1024]{1,0:T(8,128)(2,1)S(1)}, u32[]{:S(2)}, u32[]{:S(2)}) collective-permute-start(bf16[128,1024]{1,0:T(8,128)(2,1)S(1)} %get-tuple-element.27), channel_id=1, source_target_pairs={{0,0},{1,1},{2,2},{3,3},{4,8},{5,9},{6,10},{7,11},{8,4},{9,5},{10,... | collective-permute-start | bytes 786440 | tf_op jit(solution)/shard_map/ppermute | solution.py:438
  73.4 0.9 collective-permute-start.22
  74.4 7.1 %deconvolve_rows.3 = (bf16[128,1024]{1,0:T(8,128)(2,1)S(1)}, bf16[128,1024]{1,0:T(8,128)(2,1)S(1)}, bf16[128,1024]{1,0:T(8,128)(2,1)S(1)}, bf16[128,1024]{1,0:T(8,128)(2,1)S(1)}) custom-call(s32[16]{0:T(128)S(1)} %copy-done, s32[16]{0:T(128)S(1)} %copy-done.1, bf16[1,128,512]{2,1,0:T(8,128)(2,1)S(1)} %collective-permute-done.refs_0_, ...), custom_call_target="tpu_custom_call" | custom-call | tf_op jit(solution)/shard_map/deconvolve_rows/pallas_call | solution.py:307
  81.5 0.1 collective-permute-start.17
  81.5 0.0 collective-permute-done.23.refs_2_
  81.5 3.4 %collective-permute-start.18 = (bf16[128,1024]{1,0:T(8,128)(2,1)S(1)}, bf16[128,1024]{1,0:T(8,128)(2,1)S(1)}, u32[]{:S(2)}, u32[]{:S(2)}) collective-permute-start(bf16[128,1024]{1,0:T(8,128)(2,1)S(1)} %get-tuple-element.24), channel_id=1, source_target_pairs={{0,5},{1,4},{2,7},{3,6},{4,13},{5,12},{6,15},{7,14},{8,1},{9,0},{1... | collective-permute-start | bytes 786440 | tf_op jit(solution)/shard_map/ppermute | solution.py:438
  84.9 0.2 collective-permute-start.19
  85.1 0.0 collective-permute-done.21.refs_0_
  85.1 1.7 %collective-permute-start.20 = (bf16[128,1024]{1,0:T(8,128)(2,1)S(1)}, bf16[128,1024]{1,0:T(8,128)(2,1)S(1)}, u32[]{:S(2)}, u32[]{:S(2)}) collective-permute-start(bf16[128,1024]{1,0:T(8,128)(2,1)S(1)} %get-tuple-element.26), channel_id=1, source_target_pairs={{0,7},{1,6},{2,5},{3,4},{4,15},{5,14},{6,13},{7,12},{8,3},{9,2},{1... | collective-permute-start | bytes 786440 | tf_op jit(solution)/shard_map/ppermute | solution.py:438
  86.8 0.1 pad_add_fusion.spots
  86.9 0.1 pad_add_fusion.1.spots
  87.0 2.6 %place_pieces.2.refs_4_ = f32[4,128,2048]{2,1,0:T(8,128)} custom-call(s32[8]{0:T(128)S(1)} %pad_add_fusion.1.spots, bf16[128,1024]{1,0:T(8,128)(2,1)S(1)} %collective-permute-done.21.refs_0_, bf16[128,1024]{1,0:T(8,128)(2,1)S(1)} %collective-permute-done.22.refs_1_, bf16[128,1024]{1,0:T(8,128)(2,1)S(1)} %collective-permute-done.23.refs_2_, ...), custom_call_target="tpu_custom_call" | custom-call | tf_op jit(solution)/shard_map/place_pieces/pallas_call | solution.py:382
  89.6 2.8 %collective-permute-done.18.refs_1_ = bf16[128,1024]{1,0:T(8,128)(2,1)S(1)} collective-permute-done((bf16[128,1024]{1,0:T(8,128)(2,1)S(1)}, bf16[128,1024]{1,0:T(8,128)(2,1)S(1)}, u32[]{:S(2)}, u32[]{:S(2)}) %collective-permute-start.18) | collective-permute-done | bytes 262176 | tf_op jit(solution)/shard_map/ppermute | solution.py:438
  92.5 12.9 %collective-permute-done.19.refs_2_ = bf16[128,1024]{1,0:T(8,128)(2,1)S(1)} collective-permute-done((bf16[128,1024]{1,0:T(8,128)(2,1)S(1)}, bf16[128,1024]{1,0:T(8,128)(2,1)S(1)}, u32[]{:S(2)}, u32[]{:S(2)}) %collective-permute-start.19) | collective-permute-done | bytes 262176 | tf_op jit(solution)/shard_map/ppermute | solution.py:438
  105.4 3.7 %collective-permute-done.20.refs_3_ = bf16[128,1024]{1,0:T(8,128)(2,1)S(1)} collective-permute-done((bf16[128,1024]{1,0:T(8,128)(2,1)S(1)}, bf16[128,1024]{1,0:T(8,128)(2,1)S(1)}, u32[]{:S(2)}, u32[]{:S(2)}) %collective-permute-start.20) | collective-permute-done | bytes 262176 | tf_op jit(solution)/shard_map/ppermute | solution.py:438
  109.0 2.6 %place_pieces.3 = f32[4,128,2048]{2,1,0:T(8,128)} custom-call(s32[8]{0:T(128)S(1)} %pad_add_fusion.spots, bf16[128,1024]{1,0:T(8,128)(2,1)S(1)} %collective-permute-done.17.refs_0_, bf16[128,1024]{1,0:T(8,128)(2,1)S(1)} %collective-permute-done.18.refs_1_, bf16[128,1024]{1,0:T(8,128)(2,1)S(1)} %collective-permute-done.19.refs_2_, ...), custom_call_target="tpu_custom_call", output_to_operand_aliasing={{}: (5, {})} | custom-call | tf_op jit(solution)/shard_map/place_pieces/pallas_call | solution.py:382
  (10 shorter events, 0.1 us)
Async XLA Ops:
  1.1 10.8 %collective-permute-start.3 = (bf16[1,128,512]{2,1,0:T(8,128)(2,1)S(1)}, bf16[1,128,512]{2,1,0:T(8,128)(2,1)S(1)}, u32[]{:S(2)}, u32[]{:S(2)}) collective-permute-start(bf16[1,128,512]{2,1,0:T(8,128)(2,1)S(1)} %get-tuple-element.43), channel_id=1, source_target_pairs={{0,3},{1,2},{2,1},{3,0},{4,7},{5,6},{6,5},{7,4},{8,23},{9,22},{10,... | collective-permute-start | bytes 393224 | tf_op jit(solution)/shard_map/ppermute | solution.py:426
  4.9 13.2 %collective-permute-start.2 = (bf16[1,128,512]{2,1,0:T(8,128)(2,1)S(1)}, bf16[1,128,512]{2,1,0:T(8,128)(2,1)S(1)}, u32[]{:S(2)}, u32[]{:S(2)}) collective-permute-start(bf16[1,128,512]{2,1,0:T(8,128)(2,1)S(1)} %get-tuple-element.44), channel_id=1, source_target_pairs={{0,2},{1,3},{2,0},{3,1},{4,6},{5,7},{6,4},{7,5},{8,22},{9,23},{10,... | collective-permute-start | bytes 393224 | tf_op jit(solution)/shard_map/ppermute | solution.py:426
  5.9 12.3 %collective-permute-start.1 = (bf16[1,128,512]{2,1,0:T(8,128)(2,1)S(1)}, bf16[1,128,512]{2,1,0:T(8,128)(2,1)S(1)}, u32[]{:S(2)}, u32[]{:S(2)}) collective-permute-start(bf16[1,128,512]{2,1,0:T(8,128)(2,1)S(1)} %get-tuple-element.45), channel_id=1, source_target_pairs={{0,1},{1,0},{2,3},{3,2},{4,5},{5,4},{6,7},{7,6},{8,21},{9,20},{10,... | collective-permute-start | bytes 393224 | tf_op jit(solution)/shard_map/ppermute | solution.py:426
  7.4 10.8 %collective-permute-start = (bf16[1,128,512]{2,1,0:T(8,128)(2,1)S(1)}, bf16[1,128,512]{2,1,0:T(8,128)(2,1)S(1)}, u32[]{:S(2)}, u32[]{:S(2)}) collective-permute-start(bf16[1,128,512]{2,1,0:T(8,128)(2,1)S(1)} %get-tuple-element.46), channel_id=1, source_target_pairs={{0,0},{1,1},{2,2},{3,3},{4,4},{5,5},{6,6},{7,7},{8,20},{9,21},{10,... | collective-permute-start | bytes 393224 | tf_op jit(solution)/shard_map/ppermute | solution.py:426
  10.3 41.9 %copy-start.2 = (f32[65]{0:T(128)S(1)}, f32[65]{0:T(128)}, u32[]{:S(2)}) copy-start(f32[65]{0:T(128)} %param.8) | copy-start | bytes 784
  10.3 42.0 %copy-start.3 = (f32[65]{0:T(128)S(1)}, f32[65]{0:T(128)}, u32[]{:S(2)}) copy-start(f32[65]{0:T(128)} %param.9) | copy-start | bytes 784
  10.3 43.0 %copy-start = (s32[16]{0:T(128)S(1)}, s32[16]{0:T(128)}, u32[]{:S(2)}) copy-start(s32[16]{0:T(128)} %row_shift.5) | copy-start | bytes 196
  10.3 43.0 %copy-start.1 = (s32[16]{0:T(128)S(1)}, s32[16]{0:T(128)}, u32[]{:S(2)}) copy-start(s32[16]{0:T(128)} %frac_index.5) | copy-start | bytes 196
  11.9 9.5 %collective-permute-start.15 = (bf16[1,128,512]{2,1,0:T(8,128)(2,1)S(1)}, bf16[1,128,512]{2,1,0:T(8,128)(2,1)S(1)}, u32[]{:S(2)}, u32[]{:S(2)}) collective-permute-start(bf16[1,128,512]{2,1,0:T(8,128)(2,1)S(1)} %get-tuple-element.31), channel_id=1, source_target_pairs={{0,23},{1,22},{2,21},{3,20},{4,19},{5,18},{6,17},{7,16},{8,3},{9,2... | collective-permute-start | bytes 393224 | tf_op jit(solution)/shard_map/ppermute | solution.py:426
  12.0 20.8 %collective-permute-start.14 = (bf16[1,128,512]{2,1,0:T(8,128)(2,1)S(1)}, bf16[1,128,512]{2,1,0:T(8,128)(2,1)S(1)}, u32[]{:S(2)}, u32[]{:S(2)}) collective-permute-start(bf16[1,128,512]{2,1,0:T(8,128)(2,1)S(1)} %get-tuple-element.32), channel_id=1, source_target_pairs={{0,22},{1,23},{2,20},{3,21},{4,18},{5,19},{6,16},{7,17},{8,2},{9,3... | collective-permute-start | bytes 393224 | tf_op jit(solution)/shard_map/ppermute | solution.py:426
  18.2 14.6 %collective-permute-start.13 = (bf16[1,128,512]{2,1,0:T(8,128)(2,1)S(1)}, bf16[1,128,512]{2,1,0:T(8,128)(2,1)S(1)}, u32[]{:S(2)}, u32[]{:S(2)}) collective-permute-start(bf16[1,128,512]{2,1,0:T(8,128)(2,1)S(1)} %get-tuple-element.33), channel_id=1, source_target_pairs={{0,21},{1,20},{2,23},{3,22},{4,17},{5,16},{6,19},{7,18},{8,1},{9,0... | collective-permute-start | bytes 393224 | tf_op jit(solution)/shard_map/ppermute | solution.py:426
  18.2 14.7 %collective-permute-start.12 = (bf16[1,128,512]{2,1,0:T(8,128)(2,1)S(1)}, bf16[1,128,512]{2,1,0:T(8,128)(2,1)S(1)}, u32[]{:S(2)}, u32[]{:S(2)}) collective-permute-start(bf16[1,128,512]{2,1,0:T(8,128)(2,1)S(1)} %get-tuple-element.34), channel_id=1, source_target_pairs={{0,20},{1,21},{2,22},{3,23},{4,16},{5,17},{6,18},{7,19},{8,0},{9,1... | collective-permute-start | bytes 393224 | tf_op jit(solution)/shard_map/ppermute | solution.py:426
  18.3 22.1 %collective-permute-start.11 = (bf16[1,128,512]{2,1,0:T(8,128)(2,1)S(1)}, bf16[1,128,512]{2,1,0:T(8,128)(2,1)S(1)}, u32[]{:S(2)}, u32[]{:S(2)}) collective-permute-start(bf16[1,128,512]{2,1,0:T(8,128)(2,1)S(1)} %get-tuple-element.35), channel_id=1, source_target_pairs={{0,19},{1,18},{2,17},{3,16},{4,23},{5,22},{6,21},{7,20},{8,7},{9,6... | collective-permute-start | bytes 393224 | tf_op jit(solution)/shard_map/ppermute | solution.py:426
  21.4 19.0 %collective-permute-start.10 = (bf16[1,128,512]{2,1,0:T(8,128)(2,1)S(1)}, bf16[1,128,512]{2,1,0:T(8,128)(2,1)S(1)}, u32[]{:S(2)}, u32[]{:S(2)}) collective-permute-start(bf16[1,128,512]{2,1,0:T(8,128)(2,1)S(1)} %get-tuple-element.36), channel_id=1, source_target_pairs={{0,18},{1,19},{2,16},{3,17},{4,22},{5,23},{6,20},{7,21},{8,6},{9,7... | collective-permute-start | bytes 393224 | tf_op jit(solution)/shard_map/ppermute | solution.py:426
  32.8 9.1 %collective-permute-start.9 = (bf16[1,128,512]{2,1,0:T(8,128)(2,1)S(1)}, bf16[1,128,512]{2,1,0:T(8,128)(2,1)S(1)}, u32[]{:S(2)}, u32[]{:S(2)}) collective-permute-start(bf16[1,128,512]{2,1,0:T(8,128)(2,1)S(1)} %get-tuple-element.37), channel_id=1, source_target_pairs={{0,17},{1,16},{2,19},{3,18},{4,21},{5,20},{6,23},{7,22},{8,5},{9,4... | collective-permute-start | bytes 393224 | tf_op jit(solution)/shard_map/ppermute | solution.py:426
  32.8 15.9 %collective-permute-start.8 = (bf16[1,128,512]{2,1,0:T(8,128)(2,1)S(1)}, bf16[1,128,512]{2,1,0:T(8,128)(2,1)S(1)}, u32[]{:S(2)}, u32[]{:S(2)}) collective-permute-start(bf16[1,128,512]{2,1,0:T(8,128)(2,1)S(1)} %get-tuple-element.38), channel_id=1, source_target_pairs={{0,16},{1,17},{2,18},{3,19},{4,20},{5,21},{6,22},{7,23},{8,4},{9,5... | collective-permute-start | bytes 393224 | tf_op jit(solution)/shard_map/ppermute | solution.py:426
  32.9 15.8 %collective-permute-start.7 = (bf16[1,128,512]{2,1,0:T(8,128)(2,1)S(1)}, bf16[1,128,512]{2,1,0:T(8,128)(2,1)S(1)}, u32[]{:S(2)}, u32[]{:S(2)}) collective-permute-start(bf16[1,128,512]{2,1,0:T(8,128)(2,1)S(1)} %get-tuple-element.39), channel_id=1, source_target_pairs={{0,7},{1,6},{2,5},{3,4},{4,3},{5,2},{6,1},{7,0},{8,19},{9,18},{10,... | collective-permute-start | bytes 393224 | tf_op jit(solution)/shard_map/ppermute | solution.py:426
  40.3 8.5 %collective-permute-start.6 = (bf16[1,128,512]{2,1,0:T(8,128)(2,1)S(1)}, bf16[1,128,512]{2,1,0:T(8,128)(2,1)S(1)}, u32[]{:S(2)}, u32[]{:S(2)}) collective-permute-start(bf16[1,128,512]{2,1,0:T(8,128)(2,1)S(1)} %get-tuple-element.40), channel_id=1, source_target_pairs={{0,6},{1,7},{2,4},{3,5},{4,2},{5,3},{6,0},{7,1},{8,18},{9,19},{10,... | collective-permute-start | bytes 393224 | tf_op jit(solution)/shard_map/ppermute | solution.py:426
  40.4 9.1 %collective-permute-start.5 = (bf16[1,128,512]{2,1,0:T(8,128)(2,1)S(1)}, bf16[1,128,512]{2,1,0:T(8,128)(2,1)S(1)}, u32[]{:S(2)}, u32[]{:S(2)}) collective-permute-start(bf16[1,128,512]{2,1,0:T(8,128)(2,1)S(1)} %get-tuple-element.41), channel_id=1, source_target_pairs={{0,5},{1,4},{2,7},{3,6},{4,1},{5,0},{6,3},{7,2},{8,17},{9,16},{10,... | collective-permute-start | bytes 393224 | tf_op jit(solution)/shard_map/ppermute | solution.py:426
  41.9 8.9 %collective-permute-start.4 = (bf16[1,128,512]{2,1,0:T(8,128)(2,1)S(1)}, bf16[1,128,512]{2,1,0:T(8,128)(2,1)S(1)}, u32[]{:S(2)}, u32[]{:S(2)}) collective-permute-start(bf16[1,128,512]{2,1,0:T(8,128)(2,1)S(1)} %get-tuple-element.42), channel_id=1, source_target_pairs={{0,4},{1,5},{2,6},{3,7},{4,0},{5,1},{6,2},{7,3},{8,16},{9,17},{10,... | collective-permute-start | bytes 393224 | tf_op jit(solution)/shard_map/ppermute | solution.py:426
  50.9 2.4 %collective-permute-start.16 = (bf16[1024,128]{1,0:T(8,128)(2,1)S(1)}, bf16[1024,128]{1,0:T(8,128)(2,1)S(1)}, u32[]{:S(2)}, u32[]{:S(2)}) collective-permute-start(bf16[1024,128]{1,0:T(8,128)(2,1)S(1)} %edges.1), channel_id=1, source_target_pairs={{0,8},{8,0},{16,24},{24,16},{1,9},{9,1},{17,25},{25,17},{2,10},{10... | collective-permute-start | bytes 786440 | tf_op jit(solution)/shard_map/ppermute | solution.py:427
  58.9 22.6 %collective-permute-start.23 = (bf16[128,1024]{1,0:T(8,128)(2,1)S(1)}, bf16[128,1024]{1,0:T(8,128)(2,1)S(1)}, u32[]{:S(2)}, u32[]{:S(2)}) collective-permute-start(bf16[128,1024]{1,0:T(8,128)(2,1)S(1)} %get-tuple-element.29), channel_id=1, source_target_pairs={{0,2},{1,3},{2,0},{3,1},{4,10},{5,11},{6,8},{7,9},{8,6},{9,7},{10,... | collective-permute-start | bytes 786440 | tf_op jit(solution)/shard_map/ppermute | solution.py:438
  59.7 25.2 %collective-permute-start.24 = (bf16[128,1024]{1,0:T(8,128)(2,1)S(1)}, bf16[128,1024]{1,0:T(8,128)(2,1)S(1)}, u32[]{:S(2)}, u32[]{:S(2)}) collective-permute-start(bf16[128,1024]{1,0:T(8,128)(2,1)S(1)} %get-tuple-element.30), channel_id=1, source_target_pairs={{0,3},{1,2},{2,1},{3,0},{4,11},{5,10},{6,9},{7,8},{8,7},{9,6},{10,... | collective-permute-start | bytes 786440 | tf_op jit(solution)/shard_map/ppermute | solution.py:438
  67.8 17.3 %collective-permute-start.21 = (bf16[128,1024]{1,0:T(8,128)(2,1)S(1)}, bf16[128,1024]{1,0:T(8,128)(2,1)S(1)}, u32[]{:S(2)}, u32[]{:S(2)}) collective-permute-start(bf16[128,1024]{1,0:T(8,128)(2,1)S(1)} %get-tuple-element.27), channel_id=1, source_target_pairs={{0,0},{1,1},{2,2},{3,3},{4,8},{5,9},{6,10},{7,11},{8,4},{9,5},{10,... | collective-permute-start | bytes 786440 | tf_op jit(solution)/shard_map/ppermute | solution.py:438
  73.4 13.5 %collective-permute-start.22 = (bf16[128,1024]{1,0:T(8,128)(2,1)S(1)}, bf16[128,1024]{1,0:T(8,128)(2,1)S(1)}, u32[]{:S(2)}, u32[]{:S(2)}) collective-permute-start(bf16[128,1024]{1,0:T(8,128)(2,1)S(1)} %get-tuple-element.28), channel_id=1, source_target_pairs={{0,1},{1,0},{2,3},{3,2},{4,9},{5,8},{6,11},{7,10},{8,5},{9,4},{10,... | collective-permute-start | bytes 786440 | tf_op jit(solution)/shard_map/ppermute | solution.py:438
  81.5 8.2 %collective-permute-start.17 = (bf16[128,1024]{1,0:T(8,128)(2,1)S(1)}, bf16[128,1024]{1,0:T(8,128)(2,1)S(1)}, u32[]{:S(2)}, u32[]{:S(2)}) collective-permute-start(bf16[128,1024]{1,0:T(8,128)(2,1)S(1)} %get-tuple-element.23), channel_id=1, source_target_pairs={{0,4},{1,5},{2,6},{3,7},{4,12},{5,13},{6,14},{7,15},{8,0},{9,1},{1... | collective-permute-start | bytes 786440 | tf_op jit(solution)/shard_map/ppermute | solution.py:438
  81.5 10.9 %collective-permute-start.18 = (bf16[128,1024]{1,0:T(8,128)(2,1)S(1)}, bf16[128,1024]{1,0:T(8,128)(2,1)S(1)}, u32[]{:S(2)}, u32[]{:S(2)}) collective-permute-start(bf16[128,1024]{1,0:T(8,128)(2,1)S(1)} %get-tuple-element.24), channel_id=1, source_target_pairs={{0,5},{1,4},{2,7},{3,6},{4,13},{5,12},{6,15},{7,14},{8,1},{9,0},{1... | collective-permute-start | bytes 786440 | tf_op jit(solution)/shard_map/ppermute | solution.py:438
  84.9 20.4 %collective-permute-start.19 = (bf16[128,1024]{1,0:T(8,128)(2,1)S(1)}, bf16[128,1024]{1,0:T(8,128)(2,1)S(1)}, u32[]{:S(2)}, u32[]{:S(2)}) collective-permute-start(bf16[128,1024]{1,0:T(8,128)(2,1)S(1)} %get-tuple-element.25), channel_id=1, source_target_pairs={{0,6},{1,7},{2,4},{3,5},{4,14},{5,15},{6,12},{7,13},{8,2},{9,3},{1... | collective-permute-start | bytes 786440 | tf_op jit(solution)/shard_map/ppermute | solution.py:438
  85.1 23.9 %collective-permute-start.20 = (bf16[128,1024]{1,0:T(8,128)(2,1)S(1)}, bf16[128,1024]{1,0:T(8,128)(2,1)S(1)}, u32[]{:S(2)}, u32[]{:S(2)}) collective-permute-start(bf16[128,1024]{1,0:T(8,128)(2,1)S(1)} %get-tuple-element.26), channel_id=1, source_target_pairs={{0,7},{1,6},{2,5},{3,4},{4,15},{5,14},{6,13},{7,12},{8,3},{9,2},{1... | collective-permute-start | bytes 786440 | tf_op jit(solution)/shard_map/ppermute | solution.py:438

commit v4 on v3

--- a/solution.py
+++ b/solution.py
@@ -17,9 +17,11 @@
 COLS = 256
 MARGIN = 128
 ALIGN = 16
+TINY = 1e-30
 SHARES = (4, 4, 2)
+CHUNKS = 1
 PLACED = ((0, 4), (4, 8))
-VMEM_BYTES = 40 * 2**20
+VMEM_BYTES = 24 * 2**20
 FIRST_STEPS = 4
 
 
@@ -136,10 +138,6 @@
     return core, brick ^ (step % bricks) ^ (core * (bricks // 2))
 
 
-def halo_sides(total, wanted):
-    return 1 if 2 * wanted == total else 2
-
-
 def rows_kernel(bricks, first_k, count_out, row_shift, frac_index, *refs):
     pieces, refs = refs[: 2 * bricks], refs[2 * bricks :]
     side, x_forward, x_back, y_forward, y_back = refs[:5]
@@ -151,22 +149,17 @@
     _, brick, own = pieces[0].shape
     rows, width = observed.shape
     total, wanted = bricks * brick, count_out * brick
-    lead = raw.shape[0] - total
+    lead = total // 4 + HALO
     windows = column_windows(width)
     begin = core * HALO
 
     first_out = core * (bricks // 2) + brick_index % (bricks // 2)
     first_wanted = ((first_out ^ first_k) // count_out) * wanted
-    first_row = jnp.clip(first_wanted - HALO, 0, total - rows)
-
-    def reach(extra):
-        count = wanted + halo_sides(total, wanted) * extra
-        start = jnp.clip(first_wanted - extra, 0, total - count) - first_row
-        return start, count
-
-    def tiles_of(start, count):
-        for r in range(0, count, ROWS):
-            yield pl.multiple_of(start + r, RADIUS), min(ROWS, count - r)
+    first_row = first_wanted - HALO
+
+    def tiles_of(extra):
+        stop = HALO + wanted + extra
+        return [(r, min(ROWS, stop - r)) for r in range(HALO - extra, stop, ROWS)]
 
     copies = []
     for step in range(2 * bricks):
@@ -183,10 +176,7 @@
     for copy in copies:
         copy.start()
     raw[:lead, :] = jnp.zeros((lead, width), raw.dtype)
-    edge = jnp.zeros((RADIUS, width), blur_in.dtype)
-    for buffer in (blur_in, back_in):
-        buffer[:RADIUS, :] = edge
-        buffer[RADIUS + rows :, :] = edge
+    raw[lead + total :, :] = jnp.zeros((raw.shape[0] - lead - total, width), raw.dtype)
 
     weight = fraction.astype(jnp.float32) / NFRAC
     first = lead + first_row - shift - 1
@@ -206,61 +196,57 @@
             mixing[:count, : count + ALIGN], window, preferred_element_type=jnp.float32
         )
         level = moved.astype(jnp.bfloat16).astype(jnp.float32) + BACKGROUND
+        row = first_row + r + lax.broadcasted_iota(jnp.int32, (count, 1), 0)
+        level = jnp.where(jnp.logical_and(row >= 0, row < total), level, 0.0)
         observed[r : r + count, :] = level
-        blur_in[RADIUS + r : RADIUS + r + count, :] = level.astype(jnp.bfloat16)
+        blur_in[r : r + count, :] = level.astype(jnp.bfloat16)
 
     extra = HALO
     for turn in range(ITERS):
         extra -= RADIUS
-        start, count = reach(extra)
-        for r, tile in tiles_of(start, count):
-            wide[pl.ds(r, tile), :] = jnp.dot(
-                y_forward[:tile, : tile + 2 * RADIUS],
-                blur_in[pl.ds(r, tile + 2 * RADIUS), :],
+        for r, count in tiles_of(extra):
+            wide[r : r + count, :] = jnp.dot(
+                y_forward[:count, : count + 2 * RADIUS],
+                blur_in[r - RADIUS : r + count + RADIUS, :],
                 preferred_element_type=jnp.float32,
             ).astype(jnp.bfloat16)
-        tall = pl.ds(pl.multiple_of(start, RADIUS), count)
-        tall_in = pl.ds(pl.multiple_of(start + RADIUS, RADIUS), count)
-        for column, span, low, high, row in windows:
-            blurred = jnp.dot(
-                wide[tall, low:high],
-                x_forward[row : row + high - low, :span],
+        stop = HALO + wanted + extra
+        block = (wanted + 2 * extra) // CHUNKS
+        for r in range(HALO - extra, stop, block):
+            tall = slice(r, r + block)
+            for column, span, low, high, row in windows:
+                blurred = jnp.dot(
+                    wide[tall, low:high],
+                    x_forward[row : row + high - low, :span],
+                    preferred_element_type=jnp.float32,
+                )
+                inverse = pl.reciprocal(jnp.maximum(blurred, TINY), approx=True)
+                quotient = observed[tall, column : column + span] * inverse
+                ratio[tall, column : column + span] = quotient.astype(jnp.bfloat16)
+            for column, span, low, high, row in windows:
+                back_in[tall, column : column + span] = jnp.dot(
+                    ratio[tall, low:high],
+                    x_back[row : row + high - low, :span],
+                    preferred_element_type=jnp.float32,
+                ).astype(jnp.bfloat16)
+        extra -= RADIUS
+        before = observed if turn == 0 else estimate
+        last = turn == ITERS - 1
+        columns = pl.ds(pl.multiple_of(begin, 128), 2 * own) if last else slice(None)
+        for r, count in tiles_of(extra):
+            correction = jnp.dot(
+                y_back[:count, : count + 2 * RADIUS],
+                back_in[r - RADIUS : r + count + RADIUS, columns],
                 preferred_element_type=jnp.float32,
             )
-            quotient = observed[tall, column : column + span] * pl.reciprocal(blurred, approx=True)
-            ratio[tall, column : column + span] = quotient.astype(jnp.bfloat16)
-        for column, span, low, high, row in windows:
-            back_in[tall_in, column : column + span] = jnp.dot(
-                ratio[tall, low:high],
-                x_back[row : row + high - low, :span],
-                preferred_element_type=jnp.float32,
-            ).astype(jnp.bfloat16)
-        extra -= RADIUS
-        before = observed if turn == 0 else estimate
-        if turn == ITERS - 1:
-            break
-        for r, tile in tiles_of(*reach(extra)):
-            correction = jnp.dot(
-                y_back[:tile, : tile + 2 * RADIUS],
-                back_in[pl.ds(r, tile + 2 * RADIUS), :],
-                preferred_element_type=jnp.float32,
-            )
-            updated = before[pl.ds(r, tile), :] * correction
-            estimate[pl.ds(r, tile), :] = updated
-            blur_in[pl.ds(pl.multiple_of(r + RADIUS, RADIUS), tile), :] = updated.astype(
-                jnp.bfloat16
-            )
-
-    columns = pl.ds(pl.multiple_of(begin, 128), 2 * own)
+            updated = before[r : r + count, columns] * correction
+            estimate[r : r + count, columns] = updated
+            if not last:
+                blur_in[r : r + count, :] = updated.astype(jnp.bfloat16)
     for i, out in enumerate(outs):
         place = first_out ^ (first_k + i)
         r = pl.multiple_of(place * brick - first_row, RADIUS)
-        correction = jnp.dot(
-            y_back[:brick, : brick + 2 * RADIUS],
-            back_in[pl.ds(r, brick + 2 * RADIUS), columns],
-            preferred_element_type=jnp.float32,
-        )
-        squared = jnp.square(before[pl.ds(r, brick), columns] * correction)
+        squared = jnp.square(estimate[pl.ds(r, brick), columns])
         out[...] = jnp.square(squared).astype(out.dtype)
 
 
@@ -296,11 +282,11 @@
     )(rows)
 
 
-def deconvolve_rows(first_k, count, tables, pieces, side, matrices, lead):
+def deconvolve_rows(first_k, count, tables, pieces, side, matrices):
     bricks = len(pieces) // 2
     _, brick, own = pieces[0].shape
     total, wanted = bricks * brick, count * brick
-    rows, width = wanted + halo_sides(total, wanted) * HALO, 2 * own + HALO
+    rows, width = wanted + 2 * HALO, 2 * own + HALO
     vmem = pl.BlockSpec(memory_space=pltpu.VMEM)
     smem = pl.BlockSpec(memory_space=pltpu.SMEM)
     anywhere = pl.BlockSpec(memory_space=pl.ANY)
@@ -310,11 +296,11 @@
         in_specs=[smem] * 2 + [anywhere] * (2 * bricks + 1) + [vmem] * 4,
         out_specs=[vmem] * count,
         scratch_shapes=[
-            pltpu.VMEM((lead + total, width), jnp.bfloat16),
+            pltpu.VMEM((total + total // 4 + 2 * HALO + ALIGN, width), jnp.bfloat16),
             pltpu.VMEM((rows, width), jnp.float32),
             pltpu.VMEM((rows, width), jnp.float32),
-            pltpu.VMEM((rows + 2 * RADIUS, width), jnp.bfloat16),
-            pltpu.VMEM((rows + 2 * RADIUS, width), jnp.bfloat16),
+            pltpu.VMEM((rows, width), jnp.bfloat16),
+            pltpu.VMEM((rows, width), jnp.bfloat16),
             pltpu.VMEM((rows, width), jnp.bfloat16),
             pltpu.VMEM((rows, width), jnp.bfloat16),
             pltpu.SemaphoreType.DMA((2 * bricks + 1,)),
@@ -405,7 +391,6 @@
     planes, brick, own = raw.shape
     bricks = lax.axis_size("ybrick")
     half = bricks // 2
-    lead = bricks * brick // 4
     matrices = band_matrices(psf_y, psf_x)
 
     _, core, b = place_in_chip()
@@ -429,7 +414,7 @@
     for share in SHARES:
         k = len(arrived)
         tables = (row_shift, frac_index)
-        done = deconvolve_rows(k, bricks // share, tables, pieces, side, matrices, lead)
+        done = deconvolve_rows(k, bricks // share, tables, pieces, side, matrices)
         for k, piece in enumerate(done, k):
             route = []
             for y, c, i in devices:

time: 112 us -> 111 us (level)
  Pallas kernels: 23.8 us -> 22.6 us
    pallas_call x3, Pallas kernels: 18.1 us -> 16.9 us  [deconvolve_rows(): pl.pallas_call(functools.partial(rows_kernel, bricks, first_k, count), ou...]
where the time goes in v4:
time: 111 us
  starting transfers between devices  58.3 us (53%)
  waiting for transfers between devices  26.3 us (24%)
  Pallas kernels  22.6 us (20%)
  local copies, waits for them, and re-layouts  2.91 us (3%)
    ppermute x16, starting transfers between devices, by_planes(): pieces.append(lax.ppermute(piece, ('scan', 'ybrick'), route))  41.7 us
    ppermute x8, waiting for transfers between devices, by_planes(): arrived.append(lax.ppermute(piece, ('scan', 'ybrick'), route))  19.4 us
    pallas_call x3, Pallas kernels, deconvolve_rows(): pl.pallas_call(functools.partial(rows_kernel, bricks, first_k, count), ou...  16.9 us
    ppermute x8, starting transfers between devices, by_planes(): arrived.append(lax.ppermute(piece, ('scan', 'ybrick'), route))  15.4 us
    ppermute x16, waiting for transfers between devices, by_planes(): pieces.append(lax.ppermute(piece, ('scan', 'ybrick'), route))  6.19 us
    pallas_call x2, Pallas kernels, place_pieces(): pl.pallas_call(functools.partial(place_kernel, count), grid_spec=pltpu.Pr...  5.3 us
    dynamic_slice x2, local copies, waits for them, and re-layouts, by_planes(): piece = lax.dynamic_slice_in_dim(raw, plane, 1, 0)  2.7 us
  transfers between devices with their start and end apart: 25, of which 9 were waited for; matrix products, arithmetic and copies ran while one was open for 2% of the time, Pallas kernels for 14%

profile of v4, /device:TPU:9, one launch (start us, length us, event | category | flops | bytes accessed | tf_op | source)
XLA Modules:
  0.0 110.5 jit_solution(16970620267129499006)
XLA Ops:
  0.0 1.1 %constant_dynamic-slice_fusion.12 = (bf16[1,128,512]{2,1,0:T(8,128)(2,1)S(1)}, bf16[1,128,512]{2,1,0:T(8,128)(2,1)S(1)}, bf16[1,128,512]{2,1,0:T(8,128)(2,1)S(1)}, bf16[1,128,512]{2,1,0:T(8,128)(2,1)S(1)}) fusion(bf16[16,128,512]{2,1,0:T(8,128)(2,1)} %param.5, s32[]{:T(128)S(6)} %select_n.79, s32[]{:T(128)S(6)} %select_n.78, s32[]{:T(128)S(6)} %select_n.77, ...), kind=kLoop, calls=%fused_computation.12 | loop fusion | bytes 1048592 | tf_op jit(solution)/shard_map/dynamic_slice | solution.py:404
  1.1 3.8 %collective-permute-start.3 = (bf16[1,128,512]{2,1,0:T(8,128)(2,1)S(1)}, bf16[1,128,512]{2,1,0:T(8,128)(2,1)S(1)}, u32[]{:S(2)}, u32[]{:S(2)}) collective-permute-start(bf16[1,128,512]{2,1,0:T(8,128)(2,1)S(1)} %get-tuple-element.43), channel_id=1, source_target_pairs={{0,3},{1,2},{2,1},{3,0},{4,7},{5,6},{6,5},{7,4},{8,23},{9,22},{10,... | collective-permute-start | bytes 393224 | tf_op jit(solution)/shard_map/ppermute | solution.py:411
  4.9 1.0 collective-permute-start.2
  5.9 1.5 %collective-permute-start.1 = (bf16[1,128,512]{2,1,0:T(8,128)(2,1)S(1)}, bf16[1,128,512]{2,1,0:T(8,128)(2,1)S(1)}, u32[]{:S(2)}, u32[]{:S(2)}) collective-permute-start(bf16[1,128,512]{2,1,0:T(8,128)(2,1)S(1)} %get-tuple-element.45), channel_id=1, source_target_pairs={{0,1},{1,0},{2,3},{3,2},{4,5},{5,4},{6,7},{7,6},{8,21},{9,20},{10,... | collective-permute-start | bytes 393224 | tf_op jit(solution)/shard_map/ppermute | solution.py:411
  7.4 2.7 %collective-permute-start = (bf16[1,128,512]{2,1,0:T(8,128)(2,1)S(1)}, bf16[1,128,512]{2,1,0:T(8,128)(2,1)S(1)}, u32[]{:S(2)}, u32[]{:S(2)}) collective-permute-start(bf16[1,128,512]{2,1,0:T(8,128)(2,1)S(1)} %get-tuple-element.46), channel_id=1, source_target_pairs={{0,0},{1,1},{2,2},{3,3},{4,4},{5,5},{6,6},{7,7},{8,20},{9,21},{10,... | collective-permute-start | bytes 393224 | tf_op jit(solution)/shard_map/ppermute | solution.py:411
  10.3 0.0 copy-start.2
  10.3 0.0 copy-start.3
  10.3 0.0 copy-start
  10.3 0.0 copy-start.1
  10.3 1.6 %constant_dynamic-slice_fusion = (bf16[1,128,512]{2,1,0:T(8,128)(2,1)S(1)}, bf16[1,128,512]{2,1,0:T(8,128)(2,1)S(1)}, bf16[1,128,512]{2,1,0:T(8,128)(2,1)S(1)}, ...) fusion(bf16[16,128,512]{2,1,0:T(8,128)(2,1)} %param.5, ...), kind=kLoop, calls=%fused_computation | loop fusion | bytes 3145776 | tf_op jit(solution)/shard_map/dynamic_slice | solution.py:404
  11.9 0.1 collective-permute-start.15
  12.0 0.0 collective-permute-done.3.refs_3_
  12.0 6.2 %collective-permute-start.14 = (bf16[1,128,512]{2,1,0:T(8,128)(2,1)S(1)}, bf16[1,128,512]{2,1,0:T(8,128)(2,1)S(1)}, u32[]{:S(2)}, u32[]{:S(2)}) collective-permute-start(bf16[1,128,512]{2,1,0:T(8,128)(2,1)S(1)} %get-tuple-element.32), channel_id=1, source_target_pairs={{0,22},{1,23},{2,20},{3,21},{4,18},{5,19},{6,16},{7,17},{8,2},{9,3... | collective-permute-start | bytes 393224 | tf_op jit(solution)/shard_map/ppermute | solution.py:411
  18.2 0.0 collective-permute-done.2.refs_2_
  18.2 0.0 collective-permute-start.13
  18.2 0.0 collective-permute-done.1.refs_1_
  18.2 0.1 collective-permute-start.12
  18.3 0.0 collective-permute-done.refs_0_
  18.3 3.1 %collective-permute-start.11 = (bf16[1,128,512]{2,1,0:T(8,128)(2,1)S(1)}, bf16[1,128,512]{2,1,0:T(8,128)(2,1)S(1)}, u32[]{:S(2)}, u32[]{:S(2)}) collective-permute-start(bf16[1,128,512]{2,1,0:T(8,128)(2,1)S(1)} %get-tuple-element.35), channel_id=1, source_target_pairs={{0,19},{1,18},{2,17},{3,16},{4,23},{5,22},{6,21},{7,20},{8,7},{9,6... | collective-permute-start | bytes 393224 | tf_op jit(solution)/shard_map/ppermute | solution.py:411
  21.4 0.0 collective-permute-done.15.refs_15_
  21.4 11.4 %collective-permute-start.10 = (bf16[1,128,512]{2,1,0:T(8,128)(2,1)S(1)}, bf16[1,128,512]{2,1,0:T(8,128)(2,1)S(1)}, u32[]{:S(2)}, u32[]{:S(2)}) collective-permute-start(bf16[1,128,512]{2,1,0:T(8,128)(2,1)S(1)} %get-tuple-element.36), channel_id=1, source_target_pairs={{0,18},{1,19},{2,16},{3,17},{4,22},{5,23},{6,20},{7,21},{8,6},{9,7... | collective-permute-start | bytes 393224 | tf_op jit(solution)/shard_map/ppermute | solution.py:411
  32.8 0.0 collective-permute-done.14.refs_14_
  32.8 0.0 collective-permute-start.9
  32.8 0.0 collective-permute-done.13.refs_13_
  32.8 0.1 collective-permute-start.8
  32.9 0.0 collective-permute-done.12.refs_12_
  32.9 7.5 %collective-permute-start.7 = (bf16[1,128,512]{2,1,0:T(8,128)(2,1)S(1)}, bf16[1,128,512]{2,1,0:T(8,128)(2,1)S(1)}, u32[]{:S(2)}, u32[]{:S(2)}) collective-permute-start(bf16[1,128,512]{2,1,0:T(8,128)(2,1)S(1)} %get-tuple-element.39), channel_id=1, source_target_pairs={{0,7},{1,6},{2,5},{3,4},{4,3},{5,2},{6,1},{7,0},{8,19},{9,18},{10,... | collective-permute-start | bytes 393224 | tf_op jit(solution)/shard_map/ppermute | solution.py:411
  40.3 0.0 collective-permute-done.11.refs_11_
  40.4 0.1 collective-permute-start.5
  40.4 1.5 %collective-permute-done.9.refs_9_ = bf16[1,128,512]{2,1,0:T(8,128)(2,1)S(1)} collective-permute-done((bf16[1,128,512]{2,1,0:T(8,128)(2,1)S(1)}, bf16[1,128,512]{2,1,0:T(8,128)(2,1)S(1)}, u32[]{:S(2)}, u32[]{:S(2)}) %collective-permute-start.9) | collective-permute-done | bytes 131104 | tf_op jit(solution)/shard_map/ppermute | solution.py:411
  41.9 4.2 %collective-permute-start.4 = (bf16[1,128,512]{2,1,0:T(8,128)(2,1)S(1)}, bf16[1,128,512]{2,1,0:T(8,128)(2,1)S(1)}, u32[]{:S(2)}, u32[]{:S(2)}) collective-permute-start(bf16[1,128,512]{2,1,0:T(8,128)(2,1)S(1)} %get-tuple-element.42), channel_id=1, source_target_pairs={{0,4},{1,5},{2,6},{3,7},{4,0},{5,1},{6,2},{7,3},{8,16},{9,17},{10,... | collective-permute-start | bytes 393224 | tf_op jit(solution)/shard_map/ppermute | solution.py:411
  46.1 2.6 %collective-permute-done.8.refs_8_ = bf16[1,128,512]{2,1,0:T(8,128)(2,1)S(1)} collective-permute-done((bf16[1,128,512]{2,1,0:T(8,128)(2,1)S(1)}, bf16[1,128,512]{2,1,0:T(8,128)(2,1)S(1)}, u32[]{:S(2)}, u32[]{:S(2)}) %collective-permute-start.8) | collective-permute-done | bytes 131104 | tf_op jit(solution)/shard_map/ppermute | solution.py:411
  48.7 0.0 collective-permute-done.7.refs_7_
  48.7 0.2 collective-permute-done.6.refs_6_
  48.9 0.6 collective-permute-done.5.refs_5_
  49.5 1.3 %collective-permute-done.4.refs_4_ = bf16[1,128,512]{2,1,0:T(8,128)(2,1)S(1)} collective-permute-done((bf16[1,128,512]{2,1,0:T(8,128)(2,1)S(1)}, bf16[1,128,512]{2,1,0:T(8,128)(2,1)S(1)}, u32[]{:S(2)}, u32[]{:S(2)}) %collective-permute-start.4) | collective-permute-done | bytes 131104 | tf_op jit(solution)/shard_map/ppermute | solution.py:411
  50.8 0.1 edges.1
  50.9 1.2 %collective-permute-start.16 = (bf16[1024,128]{1,0:T(8,128)(2,1)S(1)}, bf16[1024,128]{1,0:T(8,128)(2,1)S(1)}, u32[]{:S(2)}, u32[]{:S(2)}) collective-permute-start(bf16[1024,128]{1,0:T(8,128)(2,1)S(1)} %edges.1), channel_id=1, source_target_pairs={{0,8},{8,0},{16,24},{24,16},{1,9},{9,1},{17,25},{25,17},{2,10},{10... | collective-permute-start | bytes 786440 | tf_op jit(solution)/shard_map/ppermute | solution.py:412
  52.2 0.1 rev.7
  52.3 0.1 rev.6
  52.4 0.2 band_matrices.1
  52.6 0.7 collective-permute-done.16.refs_16_
  53.3 4.9 %deconvolve_rows.5 = (bf16[128,1024]{1,0:T(8,128)(2,1)S(1)}, bf16[128,1024]{1,0:T(8,128)(2,1)S(1)}) custom-call(s32[16]{0:T(128)S(1)} %copy-done, s32[16]{0:T(128)S(1)} %copy-done.1, bf16[1,128,512]{2,1,0:T(8,128)(2,1)S(1)} %collective-permute-done.refs_0_, bf16[1,128,512]{2,1,0:T(8,128)(2,1)S(1)} %collective-permute-done.1.refs_1_, ...), custom_call_target="tpu_custom_call" | custom-call | tf_op jit(solution)/shard_map/deconvolve_rows/pallas_call | solution.py:293
  58.2 0.8 collective-permute-start.23
  59.0 2.7 %collective-permute-start.24 = (bf16[128,1024]{1,0:T(8,128)(2,1)S(1)}, bf16[128,1024]{1,0:T(8,128)(2,1)S(1)}, u32[]{:S(2)}, u32[]{:S(2)}) collective-permute-start(bf16[128,1024]{1,0:T(8,128)(2,1)S(1)} %get-tuple-element.30), channel_id=1, source_target_pairs={{0,3},{1,2},{2,1},{3,0},{4,11},{5,10},{6,9},{7,8},{8,7},{9,6},{10,... | collective-permute-start | bytes 786440 | tf_op jit(solution)/shard_map/ppermute | solution.py:423
  61.7 4.9 %deconvolve_rows.4 = (bf16[128,1024]{1,0:T(8,128)(2,1)S(1)}, bf16[128,1024]{1,0:T(8,128)(2,1)S(1)}) custom-call(s32[16]{0:T(128)S(1)} %copy-done, s32[16]{0:T(128)S(1)} %copy-done.1, bf16[1,128,512]{2,1,0:T(8,128)(2,1)S(1)} %collective-permute-done.refs_0_, bf16[1,128,512]{2,1,0:T(8,128)(2,1)S(1)} %collective-permute-done.1.refs_1_, ...), custom_call_target="tpu_custom_call" | custom-call | tf_op jit(solution)/shard_map/deconvolve_rows/pallas_call | solution.py:293
  66.6 5.6 %collective-permute-start.21 = (bf16[128,1024]{1,0:T(8,128)(2,1)S(1)}, bf16[128,1024]{1,0:T(8,128)(2,1)S(1)}, u32[]{:S(2)}, u32[]{:S(2)}) collective-permute-start(bf16[128,1024]{1,0:T(8,128)(2,1)S(1)} %get-tuple-element.27), channel_id=1, source_target_pairs={{0,0},{1,1},{2,2},{3,3},{4,8},{5,9},{6,10},{7,11},{8,4},{9,5},{10,... | collective-permute-start | bytes 786440 | tf_op jit(solution)/shard_map/ppermute | solution.py:423
  72.2 0.9 collective-permute-start.22
  73.2 7.2 %deconvolve_rows.3 = (bf16[128,1024]{1,0:T(8,128)(2,1)S(1)}, bf16[128,1024]{1,0:T(8,128)(2,1)S(1)}, bf16[128,1024]{1,0:T(8,128)(2,1)S(1)}, bf16[128,1024]{1,0:T(8,128)(2,1)S(1)}) custom-call(s32[16]{0:T(128)S(1)} %copy-done, s32[16]{0:T(128)S(1)} %copy-done.1, bf16[1,128,512]{2,1,0:T(8,128)(2,1)S(1)} %collective-permute-done.refs_0_, ...), custom_call_target="tpu_custom_call" | custom-call | tf_op jit(solution)/shard_map/deconvolve_rows/pallas_call | solution.py:293
  80.3 0.1 collective-permute-start.17
  80.4 0.0 collective-permute-done.23.refs_2_
  80.4 3.2 %collective-permute-start.18 = (bf16[128,1024]{1,0:T(8,128)(2,1)S(1)}, bf16[128,1024]{1,0:T(8,128)(2,1)S(1)}, u32[]{:S(2)}, u32[]{:S(2)}) collective-permute-start(bf16[128,1024]{1,0:T(8,128)(2,1)S(1)} %get-tuple-element.24), channel_id=1, source_target_pairs={{0,5},{1,4},{2,7},{3,6},{4,13},{5,12},{6,15},{7,14},{8,1},{9,0},{1... | collective-permute-start | bytes 786440 | tf_op jit(solution)/shard_map/ppermute | solution.py:423
  83.6 0.2 collective-permute-start.19
  83.8 0.0 collective-permute-done.21.refs_0_
  83.8 1.9 %collective-permute-start.20 = (bf16[128,1024]{1,0:T(8,128)(2,1)S(1)}, bf16[128,1024]{1,0:T(8,128)(2,1)S(1)}, u32[]{:S(2)}, u32[]{:S(2)}) collective-permute-start(bf16[128,1024]{1,0:T(8,128)(2,1)S(1)} %get-tuple-element.26), channel_id=1, source_target_pairs={{0,7},{1,6},{2,5},{3,4},{4,15},{5,14},{6,13},{7,12},{8,3},{9,2},{1... | collective-permute-start | bytes 786440 | tf_op jit(solution)/shard_map/ppermute | solution.py:423
  85.7 0.1 pad_add_fusion.spots
  85.8 0.1 pad_add_fusion.1.spots
  85.9 0.0 collective-permute-done.22.refs_1_
  85.9 2.6 %place_pieces.2.refs_4_ = f32[4,128,2048]{2,1,0:T(8,128)} custom-call(s32[8]{0:T(128)S(1)} %pad_add_fusion.1.spots, bf16[128,1024]{1,0:T(8,128)(2,1)S(1)} %collective-permute-done.21.refs_0_, bf16[128,1024]{1,0:T(8,128)(2,1)S(1)} %collective-permute-done.22.refs_1_, bf16[128,1024]{1,0:T(8,128)(2,1)S(1)} %collective-permute-done.23.refs_2_, ...), custom_call_target="tpu_custom_call" | custom-call | tf_op jit(solution)/shard_map/place_pieces/pallas_call | solution.py:368
  88.5 0.0 collective-permute-done.17.refs_0_
  88.5 2.8 %collective-permute-done.18.refs_1_ = bf16[128,1024]{1,0:T(8,128)(2,1)S(1)} collective-permute-done((bf16[128,1024]{1,0:T(8,128)(2,1)S(1)}, bf16[128,1024]{1,0:T(8,128)(2,1)S(1)}, u32[]{:S(2)}, u32[]{:S(2)}) %collective-permute-start.18) | collective-permute-done | bytes 262176 | tf_op jit(solution)/shard_map/ppermute | solution.py:423
  91.3 13.2 %collective-permute-done.19.refs_2_ = bf16[128,1024]{1,0:T(8,128)(2,1)S(1)} collective-permute-done((bf16[128,1024]{1,0:T(8,128)(2,1)S(1)}, bf16[128,1024]{1,0:T(8,128)(2,1)S(1)}, u32[]{:S(2)}, u32[]{:S(2)}) %collective-permute-start.19) | collective-permute-done | bytes 262176 | tf_op jit(solution)/shard_map/ppermute | solution.py:423
  104.6 3.3 %collective-permute-done.20.refs_3_ = bf16[128,1024]{1,0:T(8,128)(2,1)S(1)} collective-permute-done((bf16[128,1024]{1,0:T(8,128)(2,1)S(1)}, bf16[128,1024]{1,0:T(8,128)(2,1)S(1)}, u32[]{:S(2)}, u32[]{:S(2)}) %collective-permute-start.20) | collective-permute-done | bytes 262176 | tf_op jit(solution)/shard_map/ppermute | solution.py:423
  107.9 2.6 %place_pieces.3 = f32[4,128,2048]{2,1,0:T(8,128)} custom-call(s32[8]{0:T(128)S(1)} %pad_add_fusion.spots, bf16[128,1024]{1,0:T(8,128)(2,1)S(1)} %collective-permute-done.17.refs_0_, bf16[128,1024]{1,0:T(8,128)(2,1)S(1)} %collective-permute-done.18.refs_1_, bf16[128,1024]{1,0:T(8,128)(2,1)S(1)} %collective-permute-done.19.refs_2_, ...), custom_call_target="tpu_custom_call", output_to_operand_aliasing={{}: (5, {})} | custom-call | tf_op jit(solution)/shard_map/place_pieces/pallas_call | solution.py:368
  (10 shorter events, 0.1 us)
Async XLA Ops:
  1.1 10.8 %collective-permute-start.3 = (bf16[1,128,512]{2,1,0:T(8,128)(2,1)S(1)}, bf16[1,128,512]{2,1,0:T(8,128)(2,1)S(1)}, u32[]{:S(2)}, u32[]{:S(2)}) collective-permute-start(bf16[1,128,512]{2,1,0:T(8,128)(2,1)S(1)} %get-tuple-element.43), channel_id=1, source_target_pairs={{0,3},{1,2},{2,1},{3,0},{4,7},{5,6},{6,5},{7,4},{8,23},{9,22},{10,... | collective-permute-start | bytes 393224 | tf_op jit(solution)/shard_map/ppermute | solution.py:411
  4.9 13.2 %collective-permute-start.2 = (bf16[1,128,512]{2,1,0:T(8,128)(2,1)S(1)}, bf16[1,128,512]{2,1,0:T(8,128)(2,1)S(1)}, u32[]{:S(2)}, u32[]{:S(2)}) collective-permute-start(bf16[1,128,512]{2,1,0:T(8,128)(2,1)S(1)} %get-tuple-element.44), channel_id=1, source_target_pairs={{0,2},{1,3},{2,0},{3,1},{4,6},{5,7},{6,4},{7,5},{8,22},{9,23},{10,... | collective-permute-start | bytes 393224 | tf_op jit(solution)/shard_map/ppermute | solution.py:411
  5.9 12.3 %collective-permute-start.1 = (bf16[1,128,512]{2,1,0:T(8,128)(2,1)S(1)}, bf16[1,128,512]{2,1,0:T(8,128)(2,1)S(1)}, u32[]{:S(2)}, u32[]{:S(2)}) collective-permute-start(bf16[1,128,512]{2,1,0:T(8,128)(2,1)S(1)} %get-tuple-element.45), channel_id=1, source_target_pairs={{0,1},{1,0},{2,3},{3,2},{4,5},{5,4},{6,7},{7,6},{8,21},{9,20},{10,... | collective-permute-start | bytes 393224 | tf_op jit(solution)/shard_map/ppermute | solution.py:411
  7.4 10.8 %collective-permute-start = (bf16[1,128,512]{2,1,0:T(8,128)(2,1)S(1)}, bf16[1,128,512]{2,1,0:T(8,128)(2,1)S(1)}, u32[]{:S(2)}, u32[]{:S(2)}) collective-permute-start(bf16[1,128,512]{2,1,0:T(8,128)(2,1)S(1)} %get-tuple-element.46), channel_id=1, source_target_pairs={{0,0},{1,1},{2,2},{3,3},{4,4},{5,5},{6,6},{7,7},{8,20},{9,21},{10,... | collective-permute-start | bytes 393224 | tf_op jit(solution)/shard_map/ppermute | solution.py:411
  10.3 41.9 %copy-start.2 = (f32[65]{0:T(128)S(1)}, f32[65]{0:T(128)}, u32[]{:S(2)}) copy-start(f32[65]{0:T(128)} %param.8) | copy-start | bytes 784
  10.3 42.0 %copy-start.3 = (f32[65]{0:T(128)S(1)}, f32[65]{0:T(128)}, u32[]{:S(2)}) copy-start(f32[65]{0:T(128)} %param.9) | copy-start | bytes 784
  10.3 43.0 %copy-start = (s32[16]{0:T(128)S(1)}, s32[16]{0:T(128)}, u32[]{:S(2)}) copy-start(s32[16]{0:T(128)} %row_shift.5) | copy-start | bytes 196
  10.3 43.0 %copy-start.1 = (s32[16]{0:T(128)S(1)}, s32[16]{0:T(128)}, u32[]{:S(2)}) copy-start(s32[16]{0:T(128)} %frac_index.5) | copy-start | bytes 196
  11.9 9.5 %collective-permute-start.15 = (bf16[1,128,512]{2,1,0:T(8,128)(2,1)S(1)}, bf16[1,128,512]{2,1,0:T(8,128)(2,1)S(1)}, u32[]{:S(2)}, u32[]{:S(2)}) collective-permute-start(bf16[1,128,512]{2,1,0:T(8,128)(2,1)S(1)} %get-tuple-element.31), channel_id=1, source_target_pairs={{0,23},{1,22},{2,21},{3,20},{4,19},{5,18},{6,17},{7,16},{8,3},{9,2... | collective-permute-start | bytes 393224 | tf_op jit(solution)/shard_map/ppermute | solution.py:411
  12.0 20.8 %collective-permute-start.14 = (bf16[1,128,512]{2,1,0:T(8,128)(2,1)S(1)}, bf16[1,128,512]{2,1,0:T(8,128)(2,1)S(1)}, u32[]{:S(2)}, u32[]{:S(2)}) collective-permute-start(bf16[1,128,512]{2,1,0:T(8,128)(2,1)S(1)} %get-tuple-element.32), channel_id=1, source_target_pairs={{0,22},{1,23},{2,20},{3,21},{4,18},{5,19},{6,16},{7,17},{8,2},{9,3... | collective-permute-start | bytes 393224 | tf_op jit(solution)/shard_map/ppermute | solution.py:411
  18.2 14.6 %collective-permute-start.13 = (bf16[1,128,512]{2,1,0:T(8,128)(2,1)S(1)}, bf16[1,128,512]{2,1,0:T(8,128)(2,1)S(1)}, u32[]{:S(2)}, u32[]{:S(2)}) collective-permute-start(bf16[1,128,512]{2,1,0:T(8,128)(2,1)S(1)} %get-tuple-element.33), channel_id=1, source_target_pairs={{0,21},{1,20},{2,23},{3,22},{4,17},{5,16},{6,19},{7,18},{8,1},{9,0... | collective-permute-start | bytes 393224 | tf_op jit(solution)/shard_map/ppermute | solution.py:411
  18.2 14.7 %collective-permute-start.12 = (bf16[1,128,512]{2,1,0:T(8,128)(2,1)S(1)}, bf16[1,128,512]{2,1,0:T(8,128)(2,1)S(1)}, u32[]{:S(2)}, u32[]{:S(2)}) collective-permute-start(bf16[1,128,512]{2,1,0:T(8,128)(2,1)S(1)} %get-tuple-element.34), channel_id=1, source_target_pairs={{0,20},{1,21},{2,22},{3,23},{4,16},{5,17},{6,18},{7,19},{8,0},{9,1... | collective-permute-start | bytes 393224 | tf_op jit(solution)/shard_map/ppermute | solution.py:411
  18.3 22.1 %collective-permute-start.11 = (bf16[1,128,512]{2,1,0:T(8,128)(2,1)S(1)}, bf16[1,128,512]{2,1,0:T(8,128)(2,1)S(1)}, u32[]{:S(2)}, u32[]{:S(2)}) collective-permute-start(bf16[1,128,512]{2,1,0:T(8,128)(2,1)S(1)} %get-tuple-element.35), channel_id=1, source_target_pairs={{0,19},{1,18},{2,17},{3,16},{4,23},{5,22},{6,21},{7,20},{8,7},{9,6... | collective-permute-start | bytes 393224 | tf_op jit(solution)/shard_map/ppermute | solution.py:411
  21.4 19.0 %collective-permute-start.10 = (bf16[1,128,512]{2,1,0:T(8,128)(2,1)S(1)}, bf16[1,128,512]{2,1,0:T(8,128)(2,1)S(1)}, u32[]{:S(2)}, u32[]{:S(2)}) collective-permute-start(bf16[1,128,512]{2,1,0:T(8,128)(2,1)S(1)} %get-tuple-element.36), channel_id=1, source_target_pairs={{0,18},{1,19},{2,16},{3,17},{4,22},{5,23},{6,20},{7,21},{8,6},{9,7... | collective-permute-start | bytes 393224 | tf_op jit(solution)/shard_map/ppermute | solution.py:411
  32.8 9.1 %collective-permute-start.9 = (bf16[1,128,512]{2,1,0:T(8,128)(2,1)S(1)}, bf16[1,128,512]{2,1,0:T(8,128)(2,1)S(1)}, u32[]{:S(2)}, u32[]{:S(2)}) collective-permute-start(bf16[1,128,512]{2,1,0:T(8,128)(2,1)S(1)} %get-tuple-element.37), channel_id=1, source_target_pairs={{0,17},{1,16},{2,19},{3,18},{4,21},{5,20},{6,23},{7,22},{8,5},{9,4... | collective-permute-start | bytes 393224 | tf_op jit(solution)/shard_map/ppermute | solution.py:411
  32.8 15.9 %collective-permute-start.8 = (bf16[1,128,512]{2,1,0:T(8,128)(2,1)S(1)}, bf16[1,128,512]{2,1,0:T(8,128)(2,1)S(1)}, u32[]{:S(2)}, u32[]{:S(2)}) collective-permute-start(bf16[1,128,512]{2,1,0:T(8,128)(2,1)S(1)} %get-tuple-element.38), channel_id=1, source_target_pairs={{0,16},{1,17},{2,18},{3,19},{4,20},{5,21},{6,22},{7,23},{8,4},{9,5... | collective-permute-start | bytes 393224 | tf_op jit(solution)/shard_map/ppermute | solution.py:411
  32.9 15.8 %collective-permute-start.7 = (bf16[1,128,512]{2,1,0:T(8,128)(2,1)S(1)}, bf16[1,128,512]{2,1,0:T(8,128)(2,1)S(1)}, u32[]{:S(2)}, u32[]{:S(2)}) collective-permute-start(bf16[1,128,512]{2,1,0:T(8,128)(2,1)S(1)} %get-tuple-element.39), channel_id=1, source_target_pairs={{0,7},{1,6},{2,5},{3,4},{4,3},{5,2},{6,1},{7,0},{8,19},{9,18},{10,... | collective-permute-start | bytes 393224 | tf_op jit(solution)/shard_map/ppermute | solution.py:411
  40.3 8.5 %collective-permute-start.6 = (bf16[1,128,512]{2,1,0:T(8,128)(2,1)S(1)}, bf16[1,128,512]{2,1,0:T(8,128)(2,1)S(1)}, u32[]{:S(2)}, u32[]{:S(2)}) collective-permute-start(bf16[1,128,512]{2,1,0:T(8,128)(2,1)S(1)} %get-tuple-element.40), channel_id=1, source_target_pairs={{0,6},{1,7},{2,4},{3,5},{4,2},{5,3},{6,0},{7,1},{8,18},{9,19},{10,... | collective-permute-start | bytes 393224 | tf_op jit(solution)/shard_map/ppermute | solution.py:411
  40.4 9.1 %collective-permute-start.5 = (bf16[1,128,512]{2,1,0:T(8,128)(2,1)S(1)}, bf16[1,128,512]{2,1,0:T(8,128)(2,1)S(1)}, u32[]{:S(2)}, u32[]{:S(2)}) collective-permute-start(bf16[1,128,512]{2,1,0:T(8,128)(2,1)S(1)} %get-tuple-element.41), channel_id=1, source_target_pairs={{0,5},{1,4},{2,7},{3,6},{4,1},{5,0},{6,3},{7,2},{8,17},{9,16},{10,... | collective-permute-start | bytes 393224 | tf_op jit(solution)/shard_map/ppermute | solution.py:411
  41.9 8.9 %collective-permute-start.4 = (bf16[1,128,512]{2,1,0:T(8,128)(2,1)S(1)}, bf16[1,128,512]{2,1,0:T(8,128)(2,1)S(1)}, u32[]{:S(2)}, u32[]{:S(2)}) collective-permute-start(bf16[1,128,512]{2,1,0:T(8,128)(2,1)S(1)} %get-tuple-element.42), channel_id=1, source_target_pairs={{0,4},{1,5},{2,6},{3,7},{4,0},{5,1},{6,2},{7,3},{8,16},{9,17},{10,... | collective-permute-start | bytes 393224 | tf_op jit(solution)/shard_map/ppermute | solution.py:411
  50.9 2.4 %collective-permute-start.16 = (bf16[1024,128]{1,0:T(8,128)(2,1)S(1)}, bf16[1024,128]{1,0:T(8,128)(2,1)S(1)}, u32[]{:S(2)}, u32[]{:S(2)}) collective-permute-start(bf16[1024,128]{1,0:T(8,128)(2,1)S(1)} %edges.1), channel_id=1, source_target_pairs={{0,8},{8,0},{16,24},{24,16},{1,9},{9,1},{17,25},{25,17},{2,10},{10... | collective-permute-start | bytes 786440 | tf_op jit(solution)/shard_map/ppermute | solution.py:412
  58.2 22.2 %collective-permute-start.23 = (bf16[128,1024]{1,0:T(8,128)(2,1)S(1)}, bf16[128,1024]{1,0:T(8,128)(2,1)S(1)}, u32[]{:S(2)}, u32[]{:S(2)}) collective-permute-start(bf16[128,1024]{1,0:T(8,128)(2,1)S(1)} %get-tuple-element.29), channel_id=1, source_target_pairs={{0,2},{1,3},{2,0},{3,1},{4,10},{5,11},{6,8},{7,9},{8,6},{9,7},{10,... | collective-permute-start | bytes 786440 | tf_op jit(solution)/shard_map/ppermute | solution.py:423
  59.0 24.6 %collective-permute-start.24 = (bf16[128,1024]{1,0:T(8,128)(2,1)S(1)}, bf16[128,1024]{1,0:T(8,128)(2,1)S(1)}, u32[]{:S(2)}, u32[]{:S(2)}) collective-permute-start(bf16[128,1024]{1,0:T(8,128)(2,1)S(1)} %get-tuple-element.30), channel_id=1, source_target_pairs={{0,3},{1,2},{2,1},{3,0},{4,11},{5,10},{6,9},{7,8},{8,7},{9,6},{10,... | collective-permute-start | bytes 786440 | tf_op jit(solution)/shard_map/ppermute | solution.py:423
  66.6 17.2 %collective-permute-start.21 = (bf16[128,1024]{1,0:T(8,128)(2,1)S(1)}, bf16[128,1024]{1,0:T(8,128)(2,1)S(1)}, u32[]{:S(2)}, u32[]{:S(2)}) collective-permute-start(bf16[128,1024]{1,0:T(8,128)(2,1)S(1)} %get-tuple-element.27), channel_id=1, source_target_pairs={{0,0},{1,1},{2,2},{3,3},{4,8},{5,9},{6,10},{7,11},{8,4},{9,5},{10,... | collective-permute-start | bytes 786440 | tf_op jit(solution)/shard_map/ppermute | solution.py:423
  72.2 13.6 %collective-permute-start.22 = (bf16[128,1024]{1,0:T(8,128)(2,1)S(1)}, bf16[128,1024]{1,0:T(8,128)(2,1)S(1)}, u32[]{:S(2)}, u32[]{:S(2)}) collective-permute-start(bf16[128,1024]{1,0:T(8,128)(2,1)S(1)} %get-tuple-element.28), channel_id=1, source_target_pairs={{0,1},{1,0},{2,3},{3,2},{4,9},{5,8},{6,11},{7,10},{8,5},{9,4},{10,... | collective-permute-start | bytes 786440 | tf_op jit(solution)/shard_map/ppermute | solution.py:423
  80.3 8.2 %collective-permute-start.17 = (bf16[128,1024]{1,0:T(8,128)(2,1)S(1)}, bf16[128,1024]{1,0:T(8,128)(2,1)S(1)}, u32[]{:S(2)}, u32[]{:S(2)}) collective-permute-start(bf16[128,1024]{1,0:T(8,128)(2,1)S(1)} %get-tuple-element.23), channel_id=1, source_target_pairs={{0,4},{1,5},{2,6},{3,7},{4,12},{5,13},{6,14},{7,15},{8,0},{9,1},{1... | collective-permute-start | bytes 786440 | tf_op jit(solution)/shard_map/ppermute | solution.py:423
  80.4 10.9 %collective-permute-start.18 = (bf16[128,1024]{1,0:T(8,128)(2,1)S(1)}, bf16[128,1024]{1,0:T(8,128)(2,1)S(1)}, u32[]{:S(2)}, u32[]{:S(2)}) collective-permute-start(bf16[128,1024]{1,0:T(8,128)(2,1)S(1)} %get-tuple-element.24), channel_id=1, source_target_pairs={{0,5},{1,4},{2,7},{3,6},{4,13},{5,12},{6,15},{7,14},{8,1},{9,0},{1... | collective-permute-start | bytes 786440 | tf_op jit(solution)/shard_map/ppermute | solution.py:423
  83.6 20.9 %collective-permute-start.19 = (bf16[128,1024]{1,0:T(8,128)(2,1)S(1)}, bf16[128,1024]{1,0:T(8,128)(2,1)S(1)}, u32[]{:S(2)}, u32[]{:S(2)}) collective-permute-start(bf16[128,1024]{1,0:T(8,128)(2,1)S(1)} %get-tuple-element.25), channel_id=1, source_target_pairs={{0,6},{1,7},{2,4},{3,5},{4,14},{5,15},{6,12},{7,13},{8,2},{9,3},{1... | collective-permute-start | bytes 786440 | tf_op jit(solution)/shard_map/ppermute | solution.py:423
  83.8 24.1 %collective-permute-start.20 = (bf16[128,1024]{1,0:T(8,128)(2,1)S(1)}, bf16[128,1024]{1,0:T(8,128)(2,1)S(1)}, u32[]{:S(2)}, u32[]{:S(2)}) collective-permute-start(bf16[128,1024]{1,0:T(8,128)(2,1)S(1)} %get-tuple-element.26), channel_id=1, source_target_pairs={{0,7},{1,6},{2,5},{3,4},{4,15},{5,14},{6,13},{7,12},{8,3},{9,2},{1... | collective-permute-start | bytes 786440 | tf_op jit(solution)/shard_map/ppermute | solution.py:423

commit v5 on v4

--- a/solution.py
+++ b/solution.py
@@ -349,38 +349,39 @@
     )(*pieces)
 
 
-def place_kernel(count, spots, *refs):
-    del spots
-    pieces, out = refs[:count], refs[-1]
+def place_kernel(first, count, *refs):
+    pieces, (out, decoded, left) = refs[:count], refs[-3:]
+    width = pieces[0].shape[1]
+    copies = []
     for i, piece in enumerate(pieces):
-
-        @pl.when(pl.program_id(0) == i)
-        def _(piece=piece):
-            out[0] = lax.rsqrt(lax.rsqrt(piece[...].astype(out.dtype)))
-
-
-def place_pieces(first, brick_index, pieces, bricks, before):
+        decoded[i] = lax.rsqrt(lax.rsqrt(piece[...].astype(decoded.dtype)))
+        source = lax.axis_index("ybrick") ^ (first + i)
+        columns = pl.ds(pl.multiple_of(source // out.shape[0] * width, 128), width)
+        spot = out.at[source % out.shape[0], :, columns]
+        copies.append(pltpu.make_async_copy(decoded.at[i], spot, left.at[i]))
+        copies[-1].start()
+    for copy in copies:
+        copy.wait()
+
+
+def place_pieces(first, pieces, bricks, before):
     brick, width = pieces[0].shape
-    planes, count = bricks // 2, len(pieces)
-    sources = brick_index ^ jnp.arange(first, first + count, dtype=jnp.int32)
-    spots = jnp.concatenate([sources % planes, sources // planes])
+    count = len(pieces)
     kept = [] if before is None else [before]
+    anywhere = pl.BlockSpec(memory_space=pl.ANY)
     return pl.pallas_call(
-        functools.partial(place_kernel, count),
-        grid_spec=pltpu.PrefetchScalarGridSpec(
-            num_scalar_prefetch=1,
-            grid=(count,),
-            in_specs=[pl.BlockSpec(memory_space=pltpu.VMEM)] * count
-            + [pl.BlockSpec(memory_space=pl.ANY)] * len(kept),
-            out_specs=pl.BlockSpec(
-                (1, brick, width), lambda i, spots: (spots[i], 0, spots[count + i])
-            ),
-        ),
-        out_shape=jax.ShapeDtypeStruct((planes, brick, 2 * width), jnp.float32),
-        input_output_aliases={1 + count: 0} if kept else {},
+        functools.partial(place_kernel, first, count),
+        in_specs=[pl.BlockSpec(memory_space=pltpu.VMEM)] * count + [anywhere] * len(kept),
+        out_specs=anywhere,
+        out_shape=jax.ShapeDtypeStruct((bricks // 2, brick, 2 * width), jnp.float32),
+        scratch_shapes=[
+            pltpu.VMEM((count, brick, width), jnp.float32),
+            pltpu.SemaphoreType.DMA((count,)),
+        ],
+        input_output_aliases={count: 0} if kept else {},
         compiler_params=pltpu.CompilerParams(vmem_limit_bytes=VMEM_BYTES),
         name="place_pieces",
-    )(spots, *pieces, *kept)
+    )(*pieces, *kept)
 
 
 def after(x, *earlier):
@@ -424,7 +425,7 @@
     out = None
     for first, last in PLACED:
         first, last = first * bricks // 8, last * bricks // 8
-        out = place_pieces(first, b, arrived[first:last], bricks, out)
+        out = place_pieces(first, arrived[first:last], bricks, out)
     return out
 
 

time: 111 us -> 110 us (level)
  Pallas kernels: 22.6 us -> 20.3 us
  waiting for transfers between devices: 26.3 us -> 27.7 us
    pallas_call x2, Pallas kernels: 5.3 us -> 2.98 us  [place_pieces(): pl.pallas_call(functools.partial(place_kernel, first, count), in_specs=[p...]
    ppermute x8, waiting for transfers between devices: 19.4 us -> 20.8 us  [by_planes(): arrived.append(lax.ppermute(piece, ('scan', 'ybrick'), route))]
  transfers between devices with their start and end apart: 25 -> 25, of which waited for: 9 -> 10; matrix products, arithmetic and copies ran while one was open for 2% -> 2% of each run, Pallas kernels for 14% -> 13%
where the time goes in v5:
time: 110 us
  starting transfers between devices  58.3 us (53%)
  waiting for transfers between devices  27.7 us (25%)
  Pallas kernels  20.3 us (18%)
  local copies, waits for them, and re-layouts  2.91 us (3%)
    ppermute x16, starting transfers between devices, by_planes(): pieces.append(lax.ppermute(piece, ('scan', 'ybrick'), route))  41.7 us
    ppermute x8, waiting for transfers between devices, by_planes(): arrived.append(lax.ppermute(piece, ('scan', 'ybrick'), route))  20.8 us
    pallas_call x3, Pallas kernels, deconvolve_rows(): pl.pallas_call(functools.partial(rows_kernel, bricks, first_k, count), ou...  16.9 us
    ppermute x8, starting transfers between devices, by_planes(): arrived.append(lax.ppermute(piece, ('scan', 'ybrick'), route))  15.4 us
    ppermute x16, waiting for transfers between devices, by_planes(): pieces.append(lax.ppermute(piece, ('scan', 'ybrick'), route))  6.19 us
    pallas_call x2, Pallas kernels, place_pieces(): pl.pallas_call(functools.partial(place_kernel, first, count), in_specs=[p...  2.98 us
    dynamic_slice x2, local copies, waits for them, and re-layouts, by_planes(): piece = lax.dynamic_slice_in_dim(raw, plane, 1, 0)  2.7 us
  transfers between devices with their start and end apart: 25, of which 10 were waited for; matrix products, arithmetic and copies ran while one was open for 2% of the time, Pallas kernels for 13%

profile of v5, /device:TPU:9, one launch (start us, length us, event | category | flops | bytes accessed | tf_op | source)
XLA Modules:
  0.0 109.6 jit_solution(3420471296971780273)
XLA Ops:
  0.0 1.1 %constant_dynamic-slice_fusion.12 = (bf16[1,128,512]{2,1,0:T(8,128)(2,1)S(1)}, bf16[1,128,512]{2,1,0:T(8,128)(2,1)S(1)}, bf16[1,128,512]{2,1,0:T(8,128)(2,1)S(1)}, bf16[1,128,512]{2,1,0:T(8,128)(2,1)S(1)}) fusion(bf16[16,128,512]{2,1,0:T(8,128)(2,1)} %param.5, s32[]{:T(128)S(6)} %select_n.59, s32[]{:T(128)S(6)} %select_n.58, s32[]{:T(128)S(6)} %select_n.57, ...), kind=kLoop, calls=%fused_computation.12 | loop fusion | bytes 1048592 | tf_op jit(solution)/shard_map/dynamic_slice | solution.py:405
  1.1 3.8 %collective-permute-start.3 = (bf16[1,128,512]{2,1,0:T(8,128)(2,1)S(1)}, bf16[1,128,512]{2,1,0:T(8,128)(2,1)S(1)}, u32[]{:S(2)}, u32[]{:S(2)}) collective-permute-start(bf16[1,128,512]{2,1,0:T(8,128)(2,1)S(1)} %get-tuple-element.43), channel_id=1, source_target_pairs={{0,3},{1,2},{2,1},{3,0},{4,7},{5,6},{6,5},{7,4},{8,23},{9,22},{10,... | collective-permute-start | bytes 393224 | tf_op jit(solution)/shard_map/ppermute | solution.py:412
  4.9 1.0 collective-permute-start.2
  5.9 1.5 %collective-permute-start.1 = (bf16[1,128,512]{2,1,0:T(8,128)(2,1)S(1)}, bf16[1,128,512]{2,1,0:T(8,128)(2,1)S(1)}, u32[]{:S(2)}, u32[]{:S(2)}) collective-permute-start(bf16[1,128,512]{2,1,0:T(8,128)(2,1)S(1)} %get-tuple-element.45), channel_id=1, source_target_pairs={{0,1},{1,0},{2,3},{3,2},{4,5},{5,4},{6,7},{7,6},{8,21},{9,20},{10,... | collective-permute-start | bytes 393224 | tf_op jit(solution)/shard_map/ppermute | solution.py:412
  7.4 2.7 %collective-permute-start = (bf16[1,128,512]{2,1,0:T(8,128)(2,1)S(1)}, bf16[1,128,512]{2,1,0:T(8,128)(2,1)S(1)}, u32[]{:S(2)}, u32[]{:S(2)}) collective-permute-start(bf16[1,128,512]{2,1,0:T(8,128)(2,1)S(1)} %get-tuple-element.46), channel_id=1, source_target_pairs={{0,0},{1,1},{2,2},{3,3},{4,4},{5,5},{6,6},{7,7},{8,20},{9,21},{10,... | collective-permute-start | bytes 393224 | tf_op jit(solution)/shard_map/ppermute | solution.py:412
  10.3 0.0 copy-start.2
  10.3 0.0 copy-start.3
  10.3 0.0 copy-start
  10.3 0.0 copy-start.1
  10.3 1.6 %constant_dynamic-slice_fusion = (bf16[1,128,512]{2,1,0:T(8,128)(2,1)S(1)}, bf16[1,128,512]{2,1,0:T(8,128)(2,1)S(1)}, bf16[1,128,512]{2,1,0:T(8,128)(2,1)S(1)}, ...) fusion(bf16[16,128,512]{2,1,0:T(8,128)(2,1)} %param.5, ...), kind=kLoop, calls=%fused_computation | loop fusion | bytes 3145776 | tf_op jit(solution)/shard_map/dynamic_slice | solution.py:405
  11.9 0.1 collective-permute-start.15
  12.0 0.0 collective-permute-done.3.refs_3_
  12.0 6.2 %collective-permute-start.14 = (bf16[1,128,512]{2,1,0:T(8,128)(2,1)S(1)}, bf16[1,128,512]{2,1,0:T(8,128)(2,1)S(1)}, u32[]{:S(2)}, u32[]{:S(2)}) collective-permute-start(bf16[1,128,512]{2,1,0:T(8,128)(2,1)S(1)} %get-tuple-element.32), channel_id=1, source_target_pairs={{0,22},{1,23},{2,20},{3,21},{4,18},{5,19},{6,16},{7,17},{8,2},{9,3... | collective-permute-start | bytes 393224 | tf_op jit(solution)/shard_map/ppermute | solution.py:412
  18.2 0.0 collective-permute-done.2.refs_2_
  18.2 0.0 collective-permute-start.13
  18.2 0.0 collective-permute-done.1.refs_1_
  18.2 0.1 collective-permute-start.12
  18.3 0.0 collective-permute-done.refs_0_
  18.3 3.1 %collective-permute-start.11 = (bf16[1,128,512]{2,1,0:T(8,128)(2,1)S(1)}, bf16[1,128,512]{2,1,0:T(8,128)(2,1)S(1)}, u32[]{:S(2)}, u32[]{:S(2)}) collective-permute-start(bf16[1,128,512]{2,1,0:T(8,128)(2,1)S(1)} %get-tuple-element.35), channel_id=1, source_target_pairs={{0,19},{1,18},{2,17},{3,16},{4,23},{5,22},{6,21},{7,20},{8,7},{9,6... | collective-permute-start | bytes 393224 | tf_op jit(solution)/shard_map/ppermute | solution.py:412
  21.4 0.0 collective-permute-done.15.refs_15_
  21.4 11.4 %collective-permute-start.10 = (bf16[1,128,512]{2,1,0:T(8,128)(2,1)S(1)}, bf16[1,128,512]{2,1,0:T(8,128)(2,1)S(1)}, u32[]{:S(2)}, u32[]{:S(2)}) collective-permute-start(bf16[1,128,512]{2,1,0:T(8,128)(2,1)S(1)} %get-tuple-element.36), channel_id=1, source_target_pairs={{0,18},{1,19},{2,16},{3,17},{4,22},{5,23},{6,20},{7,21},{8,6},{9,7... | collective-permute-start | bytes 393224 | tf_op jit(solution)/shard_map/ppermute | solution.py:412
  32.8 0.0 collective-permute-done.14.refs_14_
  32.8 0.0 collective-permute-start.9
  32.8 0.0 collective-permute-done.13.refs_13_
  32.8 0.1 collective-permute-start.8
  32.9 0.0 collective-permute-done.12.refs_12_
  32.9 7.5 %collective-permute-start.7 = (bf16[1,128,512]{2,1,0:T(8,128)(2,1)S(1)}, bf16[1,128,512]{2,1,0:T(8,128)(2,1)S(1)}, u32[]{:S(2)}, u32[]{:S(2)}) collective-permute-start(bf16[1,128,512]{2,1,0:T(8,128)(2,1)S(1)} %get-tuple-element.39), channel_id=1, source_target_pairs={{0,7},{1,6},{2,5},{3,4},{4,3},{5,2},{6,1},{7,0},{8,19},{9,18},{10,... | collective-permute-start | bytes 393224 | tf_op jit(solution)/shard_map/ppermute | solution.py:412
  40.3 0.0 collective-permute-done.11.refs_11_
  40.3 0.0 collective-permute-start.6
  40.3 0.0 collective-permute-done.10.refs_10_
  40.4 0.1 collective-permute-start.5
  40.4 1.5 %collective-permute-done.9.refs_9_ = bf16[1,128,512]{2,1,0:T(8,128)(2,1)S(1)} collective-permute-done((bf16[1,128,512]{2,1,0:T(8,128)(2,1)S(1)}, bf16[1,128,512]{2,1,0:T(8,128)(2,1)S(1)}, u32[]{:S(2)}, u32[]{:S(2)}) %collective-permute-start.9) | collective-permute-done | bytes 131104 | tf_op jit(solution)/shard_map/ppermute | solution.py:412
  41.9 4.2 %collective-permute-start.4 = (bf16[1,128,512]{2,1,0:T(8,128)(2,1)S(1)}, bf16[1,128,512]{2,1,0:T(8,128)(2,1)S(1)}, u32[]{:S(2)}, u32[]{:S(2)}) collective-permute-start(bf16[1,128,512]{2,1,0:T(8,128)(2,1)S(1)} %get-tuple-element.42), channel_id=1, source_target_pairs={{0,4},{1,5},{2,6},{3,7},{4,0},{5,1},{6,2},{7,3},{8,16},{9,17},{10,... | collective-permute-start | bytes 393224 | tf_op jit(solution)/shard_map/ppermute | solution.py:412
  46.1 2.6 %collective-permute-done.8.refs_8_ = bf16[1,128,512]{2,1,0:T(8,128)(2,1)S(1)} collective-permute-done((bf16[1,128,512]{2,1,0:T(8,128)(2,1)S(1)}, bf16[1,128,512]{2,1,0:T(8,128)(2,1)S(1)}, u32[]{:S(2)}, u32[]{:S(2)}) %collective-permute-start.8) | collective-permute-done | bytes 131104 | tf_op jit(solution)/shard_map/ppermute | solution.py:412
  48.7 0.0 collective-permute-done.7.refs_7_
  48.7 0.2 collective-permute-done.6.refs_6_
  48.9 0.6 collective-permute-done.5.refs_5_
  49.5 1.3 %collective-permute-done.4.refs_4_ = bf16[1,128,512]{2,1,0:T(8,128)(2,1)S(1)} collective-permute-done((bf16[1,128,512]{2,1,0:T(8,128)(2,1)S(1)}, bf16[1,128,512]{2,1,0:T(8,128)(2,1)S(1)}, u32[]{:S(2)}, u32[]{:S(2)}) %collective-permute-start.4) | collective-permute-done | bytes 131104 | tf_op jit(solution)/shard_map/ppermute | solution.py:412
  50.8 0.1 edges.1
  50.9 1.2 %collective-permute-start.16 = (bf16[1024,128]{1,0:T(8,128)(2,1)S(1)}, bf16[1024,128]{1,0:T(8,128)(2,1)S(1)}, u32[]{:S(2)}, u32[]{:S(2)}) collective-permute-start(bf16[1024,128]{1,0:T(8,128)(2,1)S(1)} %edges.1), channel_id=1, source_target_pairs={{0,8},{8,0},{16,24},{24,16},{1,9},{9,1},{17,25},{25,17},{2,10},{10... | collective-permute-start | bytes 786440 | tf_op jit(solution)/shard_map/ppermute | solution.py:413
  52.2 0.1 rev.7
  52.3 0.1 rev.6
  52.4 0.2 band_matrices.1
  52.6 0.7 collective-permute-done.16.refs_16_
  53.3 4.9 %deconvolve_rows.5 = (bf16[128,1024]{1,0:T(8,128)(2,1)S(1)}, bf16[128,1024]{1,0:T(8,128)(2,1)S(1)}) custom-call(s32[16]{0:T(128)S(1)} %copy-done, s32[16]{0:T(128)S(1)} %copy-done.1, bf16[1,128,512]{2,1,0:T(8,128)(2,1)S(1)} %collective-permute-done.refs_0_, bf16[1,128,512]{2,1,0:T(8,128)(2,1)S(1)} %collective-permute-done.1.refs_1_, ...), custom_call_target="tpu_custom_call" | custom-call | tf_op jit(solution)/shard_map/deconvolve_rows/pallas_call | solution.py:293
  58.2 0.8 collective-permute-start.23
  59.0 2.7 %collective-permute-start.24 = (bf16[128,1024]{1,0:T(8,128)(2,1)S(1)}, bf16[128,1024]{1,0:T(8,128)(2,1)S(1)}, u32[]{:S(2)}, u32[]{:S(2)}) collective-permute-start(bf16[128,1024]{1,0:T(8,128)(2,1)S(1)} %get-tuple-element.30), channel_id=1, source_target_pairs={{0,3},{1,2},{2,1},{3,0},{4,11},{5,10},{6,9},{7,8},{8,7},{9,6},{10,... | collective-permute-start | bytes 786440 | tf_op jit(solution)/shard_map/ppermute | solution.py:424
  61.7 4.9 %deconvolve_rows.4 = (bf16[128,1024]{1,0:T(8,128)(2,1)S(1)}, bf16[128,1024]{1,0:T(8,128)(2,1)S(1)}) custom-call(s32[16]{0:T(128)S(1)} %copy-done, s32[16]{0:T(128)S(1)} %copy-done.1, bf16[1,128,512]{2,1,0:T(8,128)(2,1)S(1)} %collective-permute-done.refs_0_, bf16[1,128,512]{2,1,0:T(8,128)(2,1)S(1)} %collective-permute-done.1.refs_1_, ...), custom_call_target="tpu_custom_call" | custom-call | tf_op jit(solution)/shard_map/deconvolve_rows/pallas_call | solution.py:293
  66.6 5.6 %collective-permute-start.21 = (bf16[128,1024]{1,0:T(8,128)(2,1)S(1)}, bf16[128,1024]{1,0:T(8,128)(2,1)S(1)}, u32[]{:S(2)}, u32[]{:S(2)}) collective-permute-start(bf16[128,1024]{1,0:T(8,128)(2,1)S(1)} %get-tuple-element.27), channel_id=1, source_target_pairs={{0,0},{1,1},{2,2},{3,3},{4,8},{5,9},{6,10},{7,11},{8,4},{9,5},{10,... | collective-permute-start | bytes 786440 | tf_op jit(solution)/shard_map/ppermute | solution.py:424
  72.2 0.9 collective-permute-start.22
  73.2 7.1 %deconvolve_rows.3 = (bf16[128,1024]{1,0:T(8,128)(2,1)S(1)}, bf16[128,1024]{1,0:T(8,128)(2,1)S(1)}, bf16[128,1024]{1,0:T(8,128)(2,1)S(1)}, bf16[128,1024]{1,0:T(8,128)(2,1)S(1)}) custom-call(s32[16]{0:T(128)S(1)} %copy-done, s32[16]{0:T(128)S(1)} %copy-done.1, bf16[1,128,512]{2,1,0:T(8,128)(2,1)S(1)} %collective-permute-done.refs_0_, ...), custom_call_target="tpu_custom_call" | custom-call | tf_op jit(solution)/shard_map/deconvolve_rows/pallas_call | solution.py:293
  80.3 0.1 collective-permute-start.17
  80.4 0.0 collective-permute-done.23.refs_2_
  80.4 3.2 %collective-permute-start.18 = (bf16[128,1024]{1,0:T(8,128)(2,1)S(1)}, bf16[128,1024]{1,0:T(8,128)(2,1)S(1)}, u32[]{:S(2)}, u32[]{:S(2)}) collective-permute-start(bf16[128,1024]{1,0:T(8,128)(2,1)S(1)} %get-tuple-element.24), channel_id=1, source_target_pairs={{0,5},{1,4},{2,7},{3,6},{4,13},{5,12},{6,15},{7,14},{8,1},{9,0},{1... | collective-permute-start | bytes 786440 | tf_op jit(solution)/shard_map/ppermute | solution.py:424
  83.6 0.0 collective-permute-done.24.refs_3_
  83.6 0.2 collective-permute-start.19
  83.8 1.9 %collective-permute-start.20 = (bf16[128,1024]{1,0:T(8,128)(2,1)S(1)}, bf16[128,1024]{1,0:T(8,128)(2,1)S(1)}, u32[]{:S(2)}, u32[]{:S(2)}) collective-permute-start(bf16[128,1024]{1,0:T(8,128)(2,1)S(1)} %get-tuple-element.26), channel_id=1, source_target_pairs={{0,7},{1,6},{2,5},{3,4},{4,15},{5,14},{6,13},{7,12},{8,3},{9,2},{1... | collective-permute-start | bytes 786440 | tf_op jit(solution)/shard_map/ppermute | solution.py:424
  85.7 0.2 collective-permute-done.22.refs_1_
  85.9 1.5 %place_pieces.2.refs_4_ = f32[4,128,2048]{2,1,0:T(8,128)} custom-call(bf16[128,1024]{1,0:T(8,128)(2,1)S(1)} %collective-permute-done.21.refs_0_, bf16[128,1024]{1,0:T(8,128)(2,1)S(1)} %collective-permute-done.22.refs_1_, bf16[128,1024]{1,0:T(8,128)(2,1)S(1)} %collective-permute-done.23.refs_2_, bf16[128,1024]{1,0:T(8,128)(2,1)S(1)} %collective-permute-done.24.refs_3_), custom_call_target="tpu_custom_call" | custom-call | tf_op jit(solution)/shard_map/place_pieces/pallas_call | solution.py:372
  87.4 0.0 collective-permute-done.17.refs_0_
  87.4 4.0 %collective-permute-done.18.refs_1_ = bf16[128,1024]{1,0:T(8,128)(2,1)S(1)} collective-permute-done((bf16[128,1024]{1,0:T(8,128)(2,1)S(1)}, bf16[128,1024]{1,0:T(8,128)(2,1)S(1)}, u32[]{:S(2)}, u32[]{:S(2)}) %collective-permute-start.18) | collective-permute-done | bytes 262176 | tf_op jit(solution)/shard_map/ppermute | solution.py:424
  91.4 13.1 %collective-permute-done.19.refs_2_ = bf16[128,1024]{1,0:T(8,128)(2,1)S(1)} collective-permute-done((bf16[128,1024]{1,0:T(8,128)(2,1)S(1)}, bf16[128,1024]{1,0:T(8,128)(2,1)S(1)}, u32[]{:S(2)}, u32[]{:S(2)}) %collective-permute-start.19) | collective-permute-done | bytes 262176 | tf_op jit(solution)/shard_map/ppermute | solution.py:424
  104.5 3.5 %collective-permute-done.20.refs_3_ = bf16[128,1024]{1,0:T(8,128)(2,1)S(1)} collective-permute-done((bf16[128,1024]{1,0:T(8,128)(2,1)S(1)}, bf16[128,1024]{1,0:T(8,128)(2,1)S(1)}, u32[]{:S(2)}, u32[]{:S(2)}) %collective-permute-start.20) | collective-permute-done | bytes 262176 | tf_op jit(solution)/shard_map/ppermute | solution.py:424
  107.9 1.5 %place_pieces.3 = f32[4,128,2048]{2,1,0:T(8,128)} custom-call(bf16[128,1024]{1,0:T(8,128)(2,1)S(1)} %collective-permute-done.17.refs_0_, bf16[128,1024]{1,0:T(8,128)(2,1)S(1)} %collective-permute-done.18.refs_1_, bf16[128,1024]{1,0:T(8,128)(2,1)S(1)} %collective-permute-done.19.refs_2_, ...), custom_call_target="tpu_custom_call", output_to_operand_aliasing={{}: (4, {})} | custom-call | tf_op jit(solution)/shard_map/place_pieces/pallas_call | solution.py:372
  (6 shorter events, 0.0 us)
Async XLA Ops:
  1.1 10.8 %collective-permute-start.3 = (bf16[1,128,512]{2,1,0:T(8,128)(2,1)S(1)}, bf16[1,128,512]{2,1,0:T(8,128)(2,1)S(1)}, u32[]{:S(2)}, u32[]{:S(2)}) collective-permute-start(bf16[1,128,512]{2,1,0:T(8,128)(2,1)S(1)} %get-tuple-element.43), channel_id=1, source_target_pairs={{0,3},{1,2},{2,1},{3,0},{4,7},{5,6},{6,5},{7,4},{8,23},{9,22},{10,... | collective-permute-start | bytes 393224 | tf_op jit(solution)/shard_map/ppermute | solution.py:412
  4.9 13.2 %collective-permute-start.2 = (bf16[1,128,512]{2,1,0:T(8,128)(2,1)S(1)}, bf16[1,128,512]{2,1,0:T(8,128)(2,1)S(1)}, u32[]{:S(2)}, u32[]{:S(2)}) collective-permute-start(bf16[1,128,512]{2,1,0:T(8,128)(2,1)S(1)} %get-tuple-element.44), channel_id=1, source_target_pairs={{0,2},{1,3},{2,0},{3,1},{4,6},{5,7},{6,4},{7,5},{8,22},{9,23},{10,... | collective-permute-start | bytes 393224 | tf_op jit(solution)/shard_map/ppermute | solution.py:412
  5.9 12.3 %collective-permute-start.1 = (bf16[1,128,512]{2,1,0:T(8,128)(2,1)S(1)}, bf16[1,128,512]{2,1,0:T(8,128)(2,1)S(1)}, u32[]{:S(2)}, u32[]{:S(2)}) collective-permute-start(bf16[1,128,512]{2,1,0:T(8,128)(2,1)S(1)} %get-tuple-element.45), channel_id=1, source_target_pairs={{0,1},{1,0},{2,3},{3,2},{4,5},{5,4},{6,7},{7,6},{8,21},{9,20},{10,... | collective-permute-start | bytes 393224 | tf_op jit(solution)/shard_map/ppermute | solution.py:412
  7.4 10.8 %collective-permute-start = (bf16[1,128,512]{2,1,0:T(8,128)(2,1)S(1)}, bf16[1,128,512]{2,1,0:T(8,128)(2,1)S(1)}, u32[]{:S(2)}, u32[]{:S(2)}) collective-permute-start(bf16[1,128,512]{2,1,0:T(8,128)(2,1)S(1)} %get-tuple-element.46), channel_id=1, source_target_pairs={{0,0},{1,1},{2,2},{3,3},{4,4},{5,5},{6,6},{7,7},{8,20},{9,21},{10,... | collective-permute-start | bytes 393224 | tf_op jit(solution)/shard_map/ppermute | solution.py:412
  10.3 41.9 %copy-start.2 = (f32[65]{0:T(128)S(1)}, f32[65]{0:T(128)}, u32[]{:S(2)}) copy-start(f32[65]{0:T(128)} %param.8) | copy-start | bytes 784
  10.3 42.0 %copy-start.3 = (f32[65]{0:T(128)S(1)}, f32[65]{0:T(128)}, u32[]{:S(2)}) copy-start(f32[65]{0:T(128)} %param.9) | copy-start | bytes 784
  10.3 43.1 %copy-start = (s32[16]{0:T(128)S(1)}, s32[16]{0:T(128)}, u32[]{:S(2)}) copy-start(s32[16]{0:T(128)} %row_shift.5) | copy-start | bytes 196
  10.3 43.0 %copy-start.1 = (s32[16]{0:T(128)S(1)}, s32[16]{0:T(128)}, u32[]{:S(2)}) copy-start(s32[16]{0:T(128)} %frac_index.5) | copy-start | bytes 196
  11.9 9.5 %collective-permute-start.15 = (bf16[1,128,512]{2,1,0:T(8,128)(2,1)S(1)}, bf16[1,128,512]{2,1,0:T(8,128)(2,1)S(1)}, u32[]{:S(2)}, u32[]{:S(2)}) collective-permute-start(bf16[1,128,512]{2,1,0:T(8,128)(2,1)S(1)} %get-tuple-element.31), channel_id=1, source_target_pairs={{0,23},{1,22},{2,21},{3,20},{4,19},{5,18},{6,17},{7,16},{8,3},{9,2... | collective-permute-start | bytes 393224 | tf_op jit(solution)/shard_map/ppermute | solution.py:412
  12.0 20.8 %collective-permute-start.14 = (bf16[1,128,512]{2,1,0:T(8,128)(2,1)S(1)}, bf16[1,128,512]{2,1,0:T(8,128)(2,1)S(1)}, u32[]{:S(2)}, u32[]{:S(2)}) collective-permute-start(bf16[1,128,512]{2,1,0:T(8,128)(2,1)S(1)} %get-tuple-element.32), channel_id=1, source_target_pairs={{0,22},{1,23},{2,20},{3,21},{4,18},{5,19},{6,16},{7,17},{8,2},{9,3... | collective-permute-start | bytes 393224 | tf_op jit(solution)/shard_map/ppermute | solution.py:412
  18.2 14.6 %collective-permute-start.13 = (bf16[1,128,512]{2,1,0:T(8,128)(2,1)S(1)}, bf16[1,128,512]{2,1,0:T(8,128)(2,1)S(1)}, u32[]{:S(2)}, u32[]{:S(2)}) collective-permute-start(bf16[1,128,512]{2,1,0:T(8,128)(2,1)S(1)} %get-tuple-element.33), channel_id=1, source_target_pairs={{0,21},{1,20},{2,23},{3,22},{4,17},{5,16},{6,19},{7,18},{8,1},{9,0... | collective-permute-start | bytes 393224 | tf_op jit(solution)/shard_map/ppermute | solution.py:412
  18.2 14.7 %collective-permute-start.12 = (bf16[1,128,512]{2,1,0:T(8,128)(2,1)S(1)}, bf16[1,128,512]{2,1,0:T(8,128)(2,1)S(1)}, u32[]{:S(2)}, u32[]{:S(2)}) collective-permute-start(bf16[1,128,512]{2,1,0:T(8,128)(2,1)S(1)} %get-tuple-element.34), channel_id=1, source_target_pairs={{0,20},{1,21},{2,22},{3,23},{4,16},{5,17},{6,18},{7,19},{8,0},{9,1... | collective-permute-start | bytes 393224 | tf_op jit(solution)/shard_map/ppermute | solution.py:412
  18.3 22.1 %collective-permute-start.11 = (bf16[1,128,512]{2,1,0:T(8,128)(2,1)S(1)}, bf16[1,128,512]{2,1,0:T(8,128)(2,1)S(1)}, u32[]{:S(2)}, u32[]{:S(2)}) collective-permute-start(bf16[1,128,512]{2,1,0:T(8,128)(2,1)S(1)} %get-tuple-element.35), channel_id=1, source_target_pairs={{0,19},{1,18},{2,17},{3,16},{4,23},{5,22},{6,21},{7,20},{8,7},{9,6... | collective-permute-start | bytes 393224 | tf_op jit(solution)/shard_map/ppermute | solution.py:412
  21.4 19.0 %collective-permute-start.10 = (bf16[1,128,512]{2,1,0:T(8,128)(2,1)S(1)}, bf16[1,128,512]{2,1,0:T(8,128)(2,1)S(1)}, u32[]{:S(2)}, u32[]{:S(2)}) collective-permute-start(bf16[1,128,512]{2,1,0:T(8,128)(2,1)S(1)} %get-tuple-element.36), channel_id=1, source_target_pairs={{0,18},{1,19},{2,16},{3,17},{4,22},{5,23},{6,20},{7,21},{8,6},{9,7... | collective-permute-start | bytes 393224 | tf_op jit(solution)/shard_map/ppermute | solution.py:412
  32.8 9.1 %collective-permute-start.9 = (bf16[1,128,512]{2,1,0:T(8,128)(2,1)S(1)}, bf16[1,128,512]{2,1,0:T(8,128)(2,1)S(1)}, u32[]{:S(2)}, u32[]{:S(2)}) collective-permute-start(bf16[1,128,512]{2,1,0:T(8,128)(2,1)S(1)} %get-tuple-element.37), channel_id=1, source_target_pairs={{0,17},{1,16},{2,19},{3,18},{4,21},{5,20},{6,23},{7,22},{8,5},{9,4... | collective-permute-start | bytes 393224 | tf_op jit(solution)/shard_map/ppermute | solution.py:412
  32.8 15.9 %collective-permute-start.8 = (bf16[1,128,512]{2,1,0:T(8,128)(2,1)S(1)}, bf16[1,128,512]{2,1,0:T(8,128)(2,1)S(1)}, u32[]{:S(2)}, u32[]{:S(2)}) collective-permute-start(bf16[1,128,512]{2,1,0:T(8,128)(2,1)S(1)} %get-tuple-element.38), channel_id=1, source_target_pairs={{0,16},{1,17},{2,18},{3,19},{4,20},{5,21},{6,22},{7,23},{8,4},{9,5... | collective-permute-start | bytes 393224 | tf_op jit(solution)/shard_map/ppermute | solution.py:412
  32.9 15.8 %collective-permute-start.7 = (bf16[1,128,512]{2,1,0:T(8,128)(2,1)S(1)}, bf16[1,128,512]{2,1,0:T(8,128)(2,1)S(1)}, u32[]{:S(2)}, u32[]{:S(2)}) collective-permute-start(bf16[1,128,512]{2,1,0:T(8,128)(2,1)S(1)} %get-tuple-element.39), channel_id=1, source_target_pairs={{0,7},{1,6},{2,5},{3,4},{4,3},{5,2},{6,1},{7,0},{8,19},{9,18},{10,... | collective-permute-start | bytes 393224 | tf_op jit(solution)/shard_map/ppermute | solution.py:412
  40.3 8.5 %collective-permute-start.6 = (bf16[1,128,512]{2,1,0:T(8,128)(2,1)S(1)}, bf16[1,128,512]{2,1,0:T(8,128)(2,1)S(1)}, u32[]{:S(2)}, u32[]{:S(2)}) collective-permute-start(bf16[1,128,512]{2,1,0:T(8,128)(2,1)S(1)} %get-tuple-element.40), channel_id=1, source_target_pairs={{0,6},{1,7},{2,4},{3,5},{4,2},{5,3},{6,0},{7,1},{8,18},{9,19},{10,... | collective-permute-start | bytes 393224 | tf_op jit(solution)/shard_map/ppermute | solution.py:412
  40.4 9.1 %collective-permute-start.5 = (bf16[1,128,512]{2,1,0:T(8,128)(2,1)S(1)}, bf16[1,128,512]{2,1,0:T(8,128)(2,1)S(1)}, u32[]{:S(2)}, u32[]{:S(2)}) collective-permute-start(bf16[1,128,512]{2,1,0:T(8,128)(2,1)S(1)} %get-tuple-element.41), channel_id=1, source_target_pairs={{0,5},{1,4},{2,7},{3,6},{4,1},{5,0},{6,3},{7,2},{8,17},{9,16},{10,... | collective-permute-start | bytes 393224 | tf_op jit(solution)/shard_map/ppermute | solution.py:412
  41.9 8.9 %collective-permute-start.4 = (bf16[1,128,512]{2,1,0:T(8,128)(2,1)S(1)}, bf16[1,128,512]{2,1,0:T(8,128)(2,1)S(1)}, u32[]{:S(2)}, u32[]{:S(2)}) collective-permute-start(bf16[1,128,512]{2,1,0:T(8,128)(2,1)S(1)} %get-tuple-element.42), channel_id=1, source_target_pairs={{0,4},{1,5},{2,6},{3,7},{4,0},{5,1},{6,2},{7,3},{8,16},{9,17},{10,... | collective-permute-start | bytes 393224 | tf_op jit(solution)/shard_map/ppermute | solution.py:412
  50.9 2.4 %collective-permute-start.16 = (bf16[1024,128]{1,0:T(8,128)(2,1)S(1)}, bf16[1024,128]{1,0:T(8,128)(2,1)S(1)}, u32[]{:S(2)}, u32[]{:S(2)}) collective-permute-start(bf16[1024,128]{1,0:T(8,128)(2,1)S(1)} %edges.1), channel_id=1, source_target_pairs={{0,8},{8,0},{16,24},{24,16},{1,9},{9,1},{17,25},{25,17},{2,10},{10... | collective-permute-start | bytes 786440 | tf_op jit(solution)/shard_map/ppermute | solution.py:413
  58.2 22.2 %collective-permute-start.23 = (bf16[128,1024]{1,0:T(8,128)(2,1)S(1)}, bf16[128,1024]{1,0:T(8,128)(2,1)S(1)}, u32[]{:S(2)}, u32[]{:S(2)}) collective-permute-start(bf16[128,1024]{1,0:T(8,128)(2,1)S(1)} %get-tuple-element.29), channel_id=1, source_target_pairs={{0,2},{1,3},{2,0},{3,1},{4,10},{5,11},{6,8},{7,9},{8,6},{9,7},{10,... | collective-permute-start | bytes 786440 | tf_op jit(solution)/shard_map/ppermute | solution.py:424
  59.0 24.6 %collective-permute-start.24 = (bf16[128,1024]{1,0:T(8,128)(2,1)S(1)}, bf16[128,1024]{1,0:T(8,128)(2,1)S(1)}, u32[]{:S(2)}, u32[]{:S(2)}) collective-permute-start(bf16[128,1024]{1,0:T(8,128)(2,1)S(1)} %get-tuple-element.30), channel_id=1, source_target_pairs={{0,3},{1,2},{2,1},{3,0},{4,11},{5,10},{6,9},{7,8},{8,7},{9,6},{10,... | collective-permute-start | bytes 786440 | tf_op jit(solution)/shard_map/ppermute | solution.py:424
  66.6 17.2 %collective-permute-start.21 = (bf16[128,1024]{1,0:T(8,128)(2,1)S(1)}, bf16[128,1024]{1,0:T(8,128)(2,1)S(1)}, u32[]{:S(2)}, u32[]{:S(2)}) collective-permute-start(bf16[128,1024]{1,0:T(8,128)(2,1)S(1)} %get-tuple-element.27), channel_id=1, source_target_pairs={{0,0},{1,1},{2,2},{3,3},{4,8},{5,9},{6,10},{7,11},{8,4},{9,5},{10,... | collective-permute-start | bytes 786440 | tf_op jit(solution)/shard_map/ppermute | solution.py:424
  72.2 13.6 %collective-permute-start.22 = (bf16[128,1024]{1,0:T(8,128)(2,1)S(1)}, bf16[128,1024]{1,0:T(8,128)(2,1)S(1)}, u32[]{:S(2)}, u32[]{:S(2)}) collective-permute-start(bf16[128,1024]{1,0:T(8,128)(2,1)S(1)} %get-tuple-element.28), channel_id=1, source_target_pairs={{0,1},{1,0},{2,3},{3,2},{4,9},{5,8},{6,11},{7,10},{8,5},{9,4},{10,... | collective-permute-start | bytes 786440 | tf_op jit(solution)/shard_map/ppermute | solution.py:424
  80.3 7.1 %collective-permute-start.17 = (bf16[128,1024]{1,0:T(8,128)(2,1)S(1)}, bf16[128,1024]{1,0:T(8,128)(2,1)S(1)}, u32[]{:S(2)}, u32[]{:S(2)}) collective-permute-start(bf16[128,1024]{1,0:T(8,128)(2,1)S(1)} %get-tuple-element.23), channel_id=1, source_target_pairs={{0,4},{1,5},{2,6},{3,7},{4,12},{5,13},{6,14},{7,15},{8,0},{9,1},{1... | collective-permute-start | bytes 786440 | tf_op jit(solution)/shard_map/ppermute | solution.py:424
  80.4 11.0 %collective-permute-start.18 = (bf16[128,1024]{1,0:T(8,128)(2,1)S(1)}, bf16[128,1024]{1,0:T(8,128)(2,1)S(1)}, u32[]{:S(2)}, u32[]{:S(2)}) collective-permute-start(bf16[128,1024]{1,0:T(8,128)(2,1)S(1)} %get-tuple-element.24), channel_id=1, source_target_pairs={{0,5},{1,4},{2,7},{3,6},{4,13},{5,12},{6,15},{7,14},{8,1},{9,0},{1... | collective-permute-start | bytes 786440 | tf_op jit(solution)/shard_map/ppermute | solution.py:424
  83.6 20.9 %collective-permute-start.19 = (bf16[128,1024]{1,0:T(8,128)(2,1)S(1)}, bf16[128,1024]{1,0:T(8,128)(2,1)S(1)}, u32[]{:S(2)}, u32[]{:S(2)}) collective-permute-start(bf16[128,1024]{1,0:T(8,128)(2,1)S(1)} %get-tuple-element.25), channel_id=1, source_target_pairs={{0,6},{1,7},{2,4},{3,5},{4,14},{5,15},{6,12},{7,13},{8,2},{9,3},{1... | collective-permute-start | bytes 786440 | tf_op jit(solution)/shard_map/ppermute | solution.py:424
  83.8 24.1 %collective-permute-start.20 = (bf16[128,1024]{1,0:T(8,128)(2,1)S(1)}, bf16[128,1024]{1,0:T(8,128)(2,1)S(1)}, u32[]{:S(2)}, u32[]{:S(2)}) collective-permute-start(bf16[128,1024]{1,0:T(8,128)(2,1)S(1)} %get-tuple-element.26), channel_id=1, source_target_pairs={{0,7},{1,6},{2,5},{3,4},{4,15},{5,14},{6,13},{7,12},{8,3},{9,2},{1... | collective-permute-start | bytes 786440 | tf_op jit(solution)/shard_map/ppermute | solution.py:424

commit v6 on v5

--- a/solution.py
+++ b/solution.py
@@ -20,9 +20,9 @@
 TINY = 1e-30
 SHARES = (4, 4, 2)
 CHUNKS = 1
-PLACED = ((0, 4), (4, 8))
+PLACED = ((0, 4), (4, 7), (7, 8))
 VMEM_BYTES = 24 * 2**20
-FIRST_STEPS = 4
+FIRST_STEPS = 6
 
 
 def shifted_2(x, axis, by):
@@ -134,8 +134,8 @@
 
 def source_of(step, bricks):
     y, _, brick = place_in_chip()
-    core = y ^ (step // bricks)
-    return core, brick ^ (step % bricks) ^ (core * (bricks // 2))
+    core = y ^ (step % 2)
+    return core, brick ^ (step // 2) ^ (core * (bricks // 2))
 
 
 def rows_kernel(bricks, first_k, count_out, row_shift, frac_index, *refs):
@@ -318,11 +318,11 @@
     column = pl.ds(pl.multiple_of((1 - core) * (own - HALO), 128), HALO)
     for group in range(2):
 
-        @pl.when(source_of(group * bricks, bricks)[0] == 1 - core)
+        @pl.when(source_of(group, bricks)[0] == 1 - core)
         def _(group=group):
             copies = []
             for k in range(bricks):
-                step = group * bricks + k
+                step = group + 2 * k
                 start = pl.multiple_of(source_of(step, bricks)[1] * brick, ALIGN)
                 copies.append(
                     pltpu.make_async_copy(
@@ -398,7 +398,7 @@
     devices = [(y, c, i) for y in range(2) for c in range(2) for i in range(bricks)]
     pieces, pieces_cut = [], []
     for step in range(2 * bricks):
-        turn, k = step // bricks, step % bricks
+        turn, k = step % 2, step // 2
         plane = (core ^ turn) * bricks + (b ^ k ^ (core * half))
         if step == FIRST_STEPS:
             raw = after(raw, *pieces_cut)

time: 110 us -> 108 us (0.982)
  starting transfers between devices: 58.3 us -> 52.1 us
  waiting for transfers between devices: 27.7 us -> 30.7 us
  Pallas kernels: 20.3 us -> 21.5 us
    ppermute x16, starting transfers between devices: 41.7 us -> 35.5 us  [by_planes(): pieces.append(lax.ppermute(piece, ('scan', 'ybrick'), route))]
    ppermute x16, waiting for transfers between devices: 6.19 us -> 10.8 us  [by_planes(): pieces.append(lax.ppermute(piece, ('scan', 'ybrick'), route))]
    ppermute x8, waiting for transfers between devices: 20.8 us -> 19.2 us  [by_planes(): arrived.append(lax.ppermute(piece, ('scan', 'ybrick'), route))]
    pallas_call x2 -> x3, Pallas kernels: 2.98 us -> 3.74 us  [place_pieces(): pl.pallas_call(functools.partial(place_kernel, first, count), in_specs=[p...]
  transfers between devices with their start and end apart: 25 -> 25, of which waited for: 10 -> 10; matrix products, arithmetic and copies ran while one was open for 2% -> 2% of each run, Pallas kernels for 13% -> 14%
where the time goes in v6:
time: 108 us
  starting transfers between devices  52.1 us (48%)
  waiting for transfers between devices  30.7 us (28%)
  Pallas kernels  21.5 us (20%)
  local copies, waits for them, and re-layouts  2.99 us (3%)
    ppermute x16, starting transfers between devices, by_planes(): pieces.append(lax.ppermute(piece, ('scan', 'ybrick'), route))  35.5 us
    ppermute x8, waiting for transfers between devices, by_planes(): arrived.append(lax.ppermute(piece, ('scan', 'ybrick'), route))  19.2 us
    pallas_call x3, Pallas kernels, deconvolve_rows(): pl.pallas_call(functools.partial(rows_kernel, bricks, first_k, count), ou...  17.4 us
    ppermute x8, starting transfers between devices, by_planes(): arrived.append(lax.ppermute(piece, ('scan', 'ybrick'), route))  15.7 us
    ppermute x16, waiting for transfers between devices, by_planes(): pieces.append(lax.ppermute(piece, ('scan', 'ybrick'), route))  10.8 us
    pallas_call x3, Pallas kernels, place_pieces(): pl.pallas_call(functools.partial(place_kernel, first, count), in_specs=[p...  3.74 us
    dynamic_slice x2, local copies, waits for them, and re-layouts, by_planes(): piece = lax.dynamic_slice_in_dim(raw, plane, 1, 0)  2.78 us
  transfers between devices with their start and end apart: 25, of which 10 were waited for; matrix products, arithmetic and copies ran while one was open for 2% of the time, Pallas kernels for 14%

profile of v6, /device:TPU:9, one launch (start us, length us, event | category | flops | bytes accessed | tf_op | source)
XLA Modules:
  0.0 107.8 jit_solution(4481386843047851043)
XLA Ops:
  0.0 0.0 copy-start
  0.1 1.3 %constant_dynamic-slice_fusion.10 = (bf16[1,128,512]{2,1,0:T(8,128)(2,1)S(1)}, bf16[1,128,512]{2,1,0:T(8,128)(2,1)S(1)}, bf16[1,128,512]{2,1,0:T(8,128)(2,1)S(1)...) fusion(bf16[16,128,512]{2,1,0:T(8,128)(2,1)} %param.5, ...), kind=kLoop, calls=%fused_computation.10 | loop fusion | bytes 1572888 | tf_op jit(solution)/shard_map/dynamic_slice | solution.py:405
  1.3 1.9 %collective-permute-start.5 = (bf16[1,128,512]{2,1,0:T(8,128)(2,1)S(1)}, bf16[1,128,512]{2,1,0:T(8,128)(2,1)S(1)}, u32[]{:S(2)}, u32[]{:S(2)}) collective-permute-start(bf16[1,128,512]{2,1,0:T(8,128)(2,1)S(1)} %get-tuple-element.41), channel_id=1, source_target_pairs={{0,18},{1,19},{2,16},{3,17},{4,22},{5,23},{6,20},{7,21},{8,6},{9,7... | collective-permute-start | bytes 393224 | tf_op jit(solution)/shard_map/ppermute | solution.py:412
  3.3 2.0 %collective-permute-start.4 = (bf16[1,128,512]{2,1,0:T(8,128)(2,1)S(1)}, bf16[1,128,512]{2,1,0:T(8,128)(2,1)S(1)}, u32[]{:S(2)}, u32[]{:S(2)}) collective-permute-start(bf16[1,128,512]{2,1,0:T(8,128)(2,1)S(1)} %get-tuple-element.42), channel_id=1, source_target_pairs={{0,2},{1,3},{2,0},{3,1},{4,6},{5,7},{6,4},{7,5},{8,22},{9,23},{10,... | collective-permute-start | bytes 393224 | tf_op jit(solution)/shard_map/ppermute | solution.py:412
  5.2 3.0 %collective-permute-start.3 = (bf16[1,128,512]{2,1,0:T(8,128)(2,1)S(1)}, bf16[1,128,512]{2,1,0:T(8,128)(2,1)S(1)}, u32[]{:S(2)}, u32[]{:S(2)}) collective-permute-start(bf16[1,128,512]{2,1,0:T(8,128)(2,1)S(1)} %get-tuple-element.43), channel_id=1, source_target_pairs={{0,17},{1,16},{2,19},{3,18},{4,21},{5,20},{6,23},{7,22},{8,5},{9,4... | collective-permute-start | bytes 393224 | tf_op jit(solution)/shard_map/ppermute | solution.py:412
  8.2 1.2 %collective-permute-start.2 = (bf16[1,128,512]{2,1,0:T(8,128)(2,1)S(1)}, bf16[1,128,512]{2,1,0:T(8,128)(2,1)S(1)}, u32[]{:S(2)}, u32[]{:S(2)}) collective-permute-start(bf16[1,128,512]{2,1,0:T(8,128)(2,1)S(1)} %get-tuple-element.44), channel_id=1, source_target_pairs={{0,1},{1,0},{2,3},{3,2},{4,5},{5,4},{6,7},{7,6},{8,21},{9,20},{10,... | collective-permute-start | bytes 393224 | tf_op jit(solution)/shard_map/ppermute | solution.py:412
  9.3 0.0 collective-permute-start.1
  9.3 0.0 collective-permute-done.5.refs_5_
  9.3 5.4 %collective-permute-start = (bf16[1,128,512]{2,1,0:T(8,128)(2,1)S(1)}, bf16[1,128,512]{2,1,0:T(8,128)(2,1)S(1)}, u32[]{:S(2)}, u32[]{:S(2)}) collective-permute-start(bf16[1,128,512]{2,1,0:T(8,128)(2,1)S(1)} %get-tuple-element.46), channel_id=1, source_target_pairs={{0,0},{1,1},{2,2},{3,3},{4,4},{5,5},{6,6},{7,7},{8,20},{9,21},{10,... | collective-permute-start | bytes 393224 | tf_op jit(solution)/shard_map/ppermute | solution.py:412
  14.7 1.5 %constant_dynamic-slice_fusion = (bf16[1,128,512]{2,1,0:T(8,128)(2,1)S(1)}, bf16[1,128,512]{2,1,0:T(8,128)(2,1)S(1)}, bf16[1,128,512]{2,1,0:T(8,128)(2,1)S(1)}, ...) fusion(bf16[16,128,512]{2,1,0:T(8,128)(2,1)} %param.5, ...), kind=kLoop, calls=%fused_computation | loop fusion | bytes 2621480 | tf_op jit(solution)/shard_map/dynamic_slice | solution.py:405
  16.3 0.0 collective-permute-done.4.refs_4_
  16.3 0.1 collective-permute-start.15
  16.4 0.0 collective-permute-done.3.refs_3_
  16.4 2.7 %collective-permute-start.14 = (bf16[1,128,512]{2,1,0:T(8,128)(2,1)S(1)}, bf16[1,128,512]{2,1,0:T(8,128)(2,1)S(1)}, u32[]{:S(2)}, u32[]{:S(2)}) collective-permute-start(bf16[1,128,512]{2,1,0:T(8,128)(2,1)S(1)} %get-tuple-element.32), channel_id=1, source_target_pairs={{0,7},{1,6},{2,5},{3,4},{4,3},{5,2},{6,1},{7,0},{8,19},{9,18},{10,... | collective-permute-start | bytes 393224 | tf_op jit(solution)/shard_map/ppermute | solution.py:412
  19.1 0.0 collective-permute-done.2.refs_2_
  19.1 2.3 %collective-permute-start.13 = (bf16[1,128,512]{2,1,0:T(8,128)(2,1)S(1)}, bf16[1,128,512]{2,1,0:T(8,128)(2,1)S(1)}, u32[]{:S(2)}, u32[]{:S(2)}) collective-permute-start(bf16[1,128,512]{2,1,0:T(8,128)(2,1)S(1)} %get-tuple-element.33), channel_id=1, source_target_pairs={{0,22},{1,23},{2,20},{3,21},{4,18},{5,19},{6,16},{7,17},{8,2},{9,3... | collective-permute-start | bytes 393224 | tf_op jit(solution)/shard_map/ppermute | solution.py:412
  21.3 2.4 %collective-permute-done.1.refs_1_ = bf16[1,128,512]{2,1,0:T(8,128)(2,1)S(1)} collective-permute-done((bf16[1,128,512]{2,1,0:T(8,128)(2,1)S(1)}, bf16[1,128,512]{2,1,0:T(8,128)(2,1)S(1)}, u32[]{:S(2)}, u32[]{:S(2)}) %collective-permute-start.1) | collective-permute-done | bytes 131104 | tf_op jit(solution)/shard_map/ppermute | solution.py:412
  23.7 3.0 %collective-permute-start.12 = (bf16[1,128,512]{2,1,0:T(8,128)(2,1)S(1)}, bf16[1,128,512]{2,1,0:T(8,128)(2,1)S(1)}, u32[]{:S(2)}, u32[]{:S(2)}) collective-permute-start(bf16[1,128,512]{2,1,0:T(8,128)(2,1)S(1)} %get-tuple-element.34), channel_id=1, source_target_pairs={{0,6},{1,7},{2,4},{3,5},{4,2},{5,3},{6,0},{7,1},{8,18},{9,19},{10,... | collective-permute-start | bytes 393224 | tf_op jit(solution)/shard_map/ppermute | solution.py:412
  26.7 0.5 collective-permute-done.refs_0_
  27.3 0.0 collective-permute-start.11
  27.3 0.0 collective-permute-done.15.refs_15_
  27.3 5.4 %collective-permute-start.10 = (bf16[1,128,512]{2,1,0:T(8,128)(2,1)S(1)}, bf16[1,128,512]{2,1,0:T(8,128)(2,1)S(1)}, u32[]{:S(2)}, u32[]{:S(2)}) collective-permute-start(bf16[1,128,512]{2,1,0:T(8,128)(2,1)S(1)} %get-tuple-element.36), channel_id=1, source_target_pairs={{0,5},{1,4},{2,7},{3,6},{4,1},{5,0},{6,3},{7,2},{8,17},{9,16},{10,... | collective-permute-start | bytes 393224 | tf_op jit(solution)/shard_map/ppermute | solution.py:412
  32.7 0.0 collective-permute-done.14.refs_14_
  32.7 2.3 %collective-permute-start.9 = (bf16[1,128,512]{2,1,0:T(8,128)(2,1)S(1)}, bf16[1,128,512]{2,1,0:T(8,128)(2,1)S(1)}, u32[]{:S(2)}, u32[]{:S(2)}) collective-permute-start(bf16[1,128,512]{2,1,0:T(8,128)(2,1)S(1)} %get-tuple-element.37), channel_id=1, source_target_pairs={{0,20},{1,21},{2,22},{3,23},{4,16},{5,17},{6,18},{7,19},{8,0},{9,1... | collective-permute-start | bytes 393224 | tf_op jit(solution)/shard_map/ppermute | solution.py:412
  35.0 0.0 collective-permute-done.13.refs_13_
  35.0 1.9 %collective-permute-start.8 = (bf16[1,128,512]{2,1,0:T(8,128)(2,1)S(1)}, bf16[1,128,512]{2,1,0:T(8,128)(2,1)S(1)}, u32[]{:S(2)}, u32[]{:S(2)}) collective-permute-start(bf16[1,128,512]{2,1,0:T(8,128)(2,1)S(1)} %get-tuple-element.38), channel_id=1, source_target_pairs={{0,4},{1,5},{2,6},{3,7},{4,0},{5,1},{6,2},{7,3},{8,16},{9,17},{10,... | collective-permute-start | bytes 393224 | tf_op jit(solution)/shard_map/ppermute | solution.py:412
  36.9 0.0 collective-permute-done.12.refs_12_
  36.9 3.3 %collective-permute-start.7 = (bf16[1,128,512]{2,1,0:T(8,128)(2,1)S(1)}, bf16[1,128,512]{2,1,0:T(8,128)(2,1)S(1)}, u32[]{:S(2)}, u32[]{:S(2)}) collective-permute-start(bf16[1,128,512]{2,1,0:T(8,128)(2,1)S(1)} %get-tuple-element.39), channel_id=1, source_target_pairs={{0,19},{1,18},{2,17},{3,16},{4,23},{5,22},{6,21},{7,20},{8,7},{9,6... | collective-permute-start | bytes 393224 | tf_op jit(solution)/shard_map/ppermute | solution.py:412
  40.2 0.0 collective-permute-done.11.refs_11_
  40.2 1.1 collective-permute-start.6
  41.3 0.0 collective-permute-done.10.refs_10_
  41.3 0.0 collective-permute-done.9.refs_9_
  41.3 2.1 %collective-permute-done.8.refs_8_ = bf16[1,128,512]{2,1,0:T(8,128)(2,1)S(1)} collective-permute-done((bf16[1,128,512]{2,1,0:T(8,128)(2,1)S(1)}, bf16[1,128,512]{2,1,0:T(8,128)(2,1)S(1)}, u32[]{:S(2)}, u32[]{:S(2)}) %collective-permute-start.8) | collective-permute-done | bytes 131104 | tf_op jit(solution)/shard_map/ppermute | solution.py:412
  43.4 4.0 %collective-permute-done.7.refs_7_ = bf16[1,128,512]{2,1,0:T(8,128)(2,1)S(1)} collective-permute-done((bf16[1,128,512]{2,1,0:T(8,128)(2,1)S(1)}, bf16[1,128,512]{2,1,0:T(8,128)(2,1)S(1)}, u32[]{:S(2)}, u32[]{:S(2)}) %collective-permute-start.7) | collective-permute-done | bytes 131104 | tf_op jit(solution)/shard_map/ppermute | solution.py:412
  47.4 1.8 %collective-permute-done.6.refs_6_ = bf16[1,128,512]{2,1,0:T(8,128)(2,1)S(1)} collective-permute-done((bf16[1,128,512]{2,1,0:T(8,128)(2,1)S(1)}, bf16[1,128,512]{2,1,0:T(8,128)(2,1)S(1)}, u32[]{:S(2)}, u32[]{:S(2)}) %collective-permute-start.6) | collective-permute-done | bytes 131104 | tf_op jit(solution)/shard_map/ppermute | solution.py:412
  49.2 0.1 edges.1
  49.4 0.9 collective-permute-start.16
  50.3 0.0 copy-done.2
  50.3 0.1 rev.7
  50.4 0.1 rev.6
  50.5 0.2 band_matrices.1
  50.8 0.7 collective-permute-done.16.refs_16_
  51.5 5.0 %deconvolve_rows.5 = (bf16[128,1024]{1,0:T(8,128)(2,1)S(1)}, bf16[128,1024]{1,0:T(8,128)(2,1)S(1)}) custom-call(s32[16]{0:T(128)S(1)} %copy-done, s32[16]{0:T(128)S(1)} %copy-done.1, bf16[1,128,512]{2,1,0:T(8,128)(2,1)S(1)} %collective-permute-done.refs_0_, bf16[1,128,512]{2,1,0:T(8,128)(2,1)S(1)} %collective-permute-done.1.refs_1_, ...), custom_call_target="tpu_custom_call" | custom-call | tf_op jit(solution)/shard_map/deconvolve_rows/pallas_call | solution.py:293
  56.5 1.3 %collective-permute-start.23 = (bf16[128,1024]{1,0:T(8,128)(2,1)S(1)}, bf16[128,1024]{1,0:T(8,128)(2,1)S(1)}, u32[]{:S(2)}, u32[]{:S(2)}) collective-permute-start(bf16[128,1024]{1,0:T(8,128)(2,1)S(1)} %get-tuple-element.29), channel_id=1, source_target_pairs={{0,2},{1,3},{2,0},{3,1},{4,10},{5,11},{6,8},{7,9},{8,6},{9,7},{10,... | collective-permute-start | bytes 786440 | tf_op jit(solution)/shard_map/ppermute | solution.py:424
  57.8 1.0 collective-permute-start.24
  58.8 5.0 %deconvolve_rows.4 = (bf16[128,1024]{1,0:T(8,128)(2,1)S(1)}, bf16[128,1024]{1,0:T(8,128)(2,1)S(1)}) custom-call(s32[16]{0:T(128)S(1)} %copy-done, s32[16]{0:T(128)S(1)} %copy-done.1, bf16[1,128,512]{2,1,0:T(8,128)(2,1)S(1)} %collective-permute-done.refs_0_, bf16[1,128,512]{2,1,0:T(8,128)(2,1)S(1)} %collective-permute-done.1.refs_1_, ...), custom_call_target="tpu_custom_call" | custom-call | tf_op jit(solution)/shard_map/deconvolve_rows/pallas_call | solution.py:293
  63.8 7.5 %collective-permute-start.21 = (bf16[128,1024]{1,0:T(8,128)(2,1)S(1)}, bf16[128,1024]{1,0:T(8,128)(2,1)S(1)}, u32[]{:S(2)}, u32[]{:S(2)}) collective-permute-start(bf16[128,1024]{1,0:T(8,128)(2,1)S(1)} %get-tuple-element.27), channel_id=1, source_target_pairs={{0,0},{1,1},{2,2},{3,3},{4,8},{5,9},{6,10},{7,11},{8,4},{9,5},{10,... | collective-permute-start | bytes 786440 | tf_op jit(solution)/shard_map/ppermute | solution.py:424
  71.3 0.6 collective-permute-start.22
  71.9 7.4 %deconvolve_rows.3 = (bf16[128,1024]{1,0:T(8,128)(2,1)S(1)}, bf16[128,1024]{1,0:T(8,128)(2,1)S(1)}, bf16[128,1024]{1,0:T(8,128)(2,1)S(1)}, bf16[128,1024]{1,0:T(8,128)(2,1)S(1)}) custom-call(s32[16]{0:T(128)S(1)} %copy-done, s32[16]{0:T(128)S(1)} %copy-done.1, bf16[1,128,512]{2,1,0:T(8,128)(2,1)S(1)} %collective-permute-done.refs_0_, ...), custom_call_target="tpu_custom_call" | custom-call | tf_op jit(solution)/shard_map/deconvolve_rows/pallas_call | solution.py:293
  79.3 0.1 collective-permute-start.18
  79.4 0.0 collective-permute-done.23.refs_2_
  79.4 3.5 %collective-permute-start.19 = (bf16[128,1024]{1,0:T(8,128)(2,1)S(1)}, bf16[128,1024]{1,0:T(8,128)(2,1)S(1)}, u32[]{:S(2)}, u32[]{:S(2)}) collective-permute-start(bf16[128,1024]{1,0:T(8,128)(2,1)S(1)} %get-tuple-element.25), channel_id=1, source_target_pairs={{0,5},{1,4},{2,7},{3,6},{4,13},{5,12},{6,15},{7,14},{8,1},{9,0},{1... | collective-permute-start | bytes 786440 | tf_op jit(solution)/shard_map/ppermute | solution.py:424
  82.9 0.0 collective-permute-done.24.refs_3_
  82.9 0.0 collective-permute-start.20
  82.9 0.0 collective-permute-done.21.refs_0_
  82.9 1.7 %collective-permute-start.17 = (bf16[128,1024]{1,0:T(8,128)(2,1)S(1)}, bf16[128,1024]{1,0:T(8,128)(2,1)S(1)}, u32[]{:S(2)}, u32[]{:S(2)}) collective-permute-start(bf16[128,1024]{1,0:T(8,128)(2,1)S(1)} %get-tuple-element.23), channel_id=1, source_target_pairs={{0,7},{1,6},{2,5},{3,4},{4,15},{5,14},{6,13},{7,12},{8,3},{9,2},{1... | collective-permute-start | bytes 786440 | tf_op jit(solution)/shard_map/ppermute | solution.py:424
  84.7 2.0 %collective-permute-done.22.refs_1_ = bf16[128,1024]{1,0:T(8,128)(2,1)S(1)} collective-permute-done((bf16[128,1024]{1,0:T(8,128)(2,1)S(1)}, bf16[128,1024]{1,0:T(8,128)(2,1)S(1)}, u32[]{:S(2)}, u32[]{:S(2)}) %collective-permute-start.22) | collective-permute-done | bytes 262176 | tf_op jit(solution)/shard_map/ppermute | solution.py:424
  86.7 1.5 %place_pieces.3.refs_3_ = f32[4,128,2048]{2,1,0:T(8,128)} custom-call(bf16[128,1024]{1,0:T(8,128)(2,1)S(1)} %collective-permute-done.21.refs_0_, bf16[128,1024]{1,0:T(8,128)(2,1)S(1)} %collective-permute-done.22.refs_1_, bf16[128,1024]{1,0:T(8,128)(2,1)S(1)} %collective-permute-done.23.refs_2_, bf16[128,1024]{1,0:T(8,128)(2,1)S(1)} %collective-permute-done.24.refs_3_), custom_call_target="tpu_custom_call" | custom-call | tf_op jit(solution)/shard_map/place_pieces/pallas_call | solution.py:372
  88.2 0.0 collective-permute-done.18.refs_0_
  88.2 3.1 %collective-permute-done.19.refs_1_ = bf16[128,1024]{1,0:T(8,128)(2,1)S(1)} collective-permute-done((bf16[128,1024]{1,0:T(8,128)(2,1)S(1)}, bf16[128,1024]{1,0:T(8,128)(2,1)S(1)}, u32[]{:S(2)}, u32[]{:S(2)}) %collective-permute-start.19) | collective-permute-done | bytes 262176 | tf_op jit(solution)/shard_map/ppermute | solution.py:424
  91.2 12.0 %collective-permute-done.20.refs_2_ = bf16[128,1024]{1,0:T(8,128)(2,1)S(1)} collective-permute-done((bf16[128,1024]{1,0:T(8,128)(2,1)S(1)}, bf16[128,1024]{1,0:T(8,128)(2,1)S(1)}, u32[]{:S(2)}, u32[]{:S(2)}) %collective-permute-start.20) | collective-permute-done | bytes 262176 | tf_op jit(solution)/shard_map/ppermute | solution.py:424
  103.2 1.3 %place_pieces.4.refs_1_ = f32[4,128,2048]{2,1,0:T(8,128)} custom-call(bf16[128,1024]{1,0:T(8,128)(2,1)S(1)} %collective-permute-done.18.refs_0_, bf16[128,1024]{1,0:T(8,128)(2,1)S(1)} %collective-permute-done.19.refs_1_, bf16[128,1024]{1,0:T(8,128)(2,1)S(1)} %collective-permute-done.20.refs_2_, ...), custom_call_target="tpu_custom_call", output_to_operand_aliasing={{}: (3, {})} | custom-call | tf_op jit(solution)/shard_map/place_pieces/pallas_call | solution.py:372
  104.6 2.1 %collective-permute-done.17.refs_0_ = bf16[128,1024]{1,0:T(8,128)(2,1)S(1)} collective-permute-done((bf16[128,1024]{1,0:T(8,128)(2,1)S(1)}, bf16[128,1024]{1,0:T(8,128)(2,1)S(1)}, u32[]{:S(2)}, u32[]{:S(2)}) %collective-permute-start.17) | collective-permute-done | bytes 262176 | tf_op jit(solution)/shard_map/ppermute | solution.py:424
  106.7 0.9 place_pieces.5
  (7 shorter events, 0.0 us)
Async XLA Ops:
  0.0 50.3 %copy-start.2 = (f32[65]{0:T(128)S(1)}, f32[65]{0:T(128)}, u32[]{:S(2)}) copy-start(f32[65]{0:T(128)} %param.8) | copy-start | bytes 784
  0.0 50.4 %copy-start.3 = (f32[65]{0:T(128)S(1)}, f32[65]{0:T(128)}, u32[]{:S(2)}) copy-start(f32[65]{0:T(128)} %param.9) | copy-start | bytes 784
  0.0 51.5 %copy-start.1 = (s32[16]{0:T(128)S(1)}, s32[16]{0:T(128)}, u32[]{:S(2)}) copy-start(s32[16]{0:T(128)} %frac_index.5) | copy-start | bytes 196
  0.0 51.5 %copy-start = (s32[16]{0:T(128)S(1)}, s32[16]{0:T(128)}, u32[]{:S(2)}) copy-start(s32[16]{0:T(128)} %row_shift.5) | copy-start | bytes 196
  1.3 8.0 %collective-permute-start.5 = (bf16[1,128,512]{2,1,0:T(8,128)(2,1)S(1)}, bf16[1,128,512]{2,1,0:T(8,128)(2,1)S(1)}, u32[]{:S(2)}, u32[]{:S(2)}) collective-permute-start(bf16[1,128,512]{2,1,0:T(8,128)(2,1)S(1)} %get-tuple-element.41), channel_id=1, source_target_pairs={{0,18},{1,19},{2,16},{3,17},{4,22},{5,23},{6,20},{7,21},{8,6},{9,7... | collective-permute-start | bytes 393224 | tf_op jit(solution)/shard_map/ppermute | solution.py:412
  3.3 13.0 %collective-permute-start.4 = (bf16[1,128,512]{2,1,0:T(8,128)(2,1)S(1)}, bf16[1,128,512]{2,1,0:T(8,128)(2,1)S(1)}, u32[]{:S(2)}, u32[]{:S(2)}) collective-permute-start(bf16[1,128,512]{2,1,0:T(8,128)(2,1)S(1)} %get-tuple-element.42), channel_id=1, source_target_pairs={{0,2},{1,3},{2,0},{3,1},{4,6},{5,7},{6,4},{7,5},{8,22},{9,23},{10,... | collective-permute-start | bytes 393224 | tf_op jit(solution)/shard_map/ppermute | solution.py:412
  5.2 11.1 %collective-permute-start.3 = (bf16[1,128,512]{2,1,0:T(8,128)(2,1)S(1)}, bf16[1,128,512]{2,1,0:T(8,128)(2,1)S(1)}, u32[]{:S(2)}, u32[]{:S(2)}) collective-permute-start(bf16[1,128,512]{2,1,0:T(8,128)(2,1)S(1)} %get-tuple-element.43), channel_id=1, source_target_pairs={{0,17},{1,16},{2,19},{3,18},{4,21},{5,20},{6,23},{7,22},{8,5},{9,4... | collective-permute-start | bytes 393224 | tf_op jit(solution)/shard_map/ppermute | solution.py:412
  8.2 10.9 %collective-permute-start.2 = (bf16[1,128,512]{2,1,0:T(8,128)(2,1)S(1)}, bf16[1,128,512]{2,1,0:T(8,128)(2,1)S(1)}, u32[]{:S(2)}, u32[]{:S(2)}) collective-permute-start(bf16[1,128,512]{2,1,0:T(8,128)(2,1)S(1)} %get-tuple-element.44), channel_id=1, source_target_pairs={{0,1},{1,0},{2,3},{3,2},{4,5},{5,4},{6,7},{7,6},{8,21},{9,20},{10,... | collective-permute-start | bytes 393224 | tf_op jit(solution)/shard_map/ppermute | solution.py:412
  9.3 14.4 %collective-permute-start.1 = (bf16[1,128,512]{2,1,0:T(8,128)(2,1)S(1)}, bf16[1,128,512]{2,1,0:T(8,128)(2,1)S(1)}, u32[]{:S(2)}, u32[]{:S(2)}) collective-permute-start(bf16[1,128,512]{2,1,0:T(8,128)(2,1)S(1)} %get-tuple-element.45), channel_id=1, source_target_pairs={{0,16},{1,17},{2,18},{3,19},{4,20},{5,21},{6,22},{7,23},{8,4},{9,5... | collective-permute-start | bytes 393224 | tf_op jit(solution)/shard_map/ppermute | solution.py:412
  9.3 17.9 %collective-permute-start = (bf16[1,128,512]{2,1,0:T(8,128)(2,1)S(1)}, bf16[1,128,512]{2,1,0:T(8,128)(2,1)S(1)}, u32[]{:S(2)}, u32[]{:S(2)}) collective-permute-start(bf16[1,128,512]{2,1,0:T(8,128)(2,1)S(1)} %get-tuple-element.46), channel_id=1, source_target_pairs={{0,0},{1,1},{2,2},{3,3},{4,4},{5,5},{6,6},{7,7},{8,20},{9,21},{10,... | collective-permute-start | bytes 393224 | tf_op jit(solution)/shard_map/ppermute | solution.py:412
  16.3 11.0 %collective-permute-start.15 = (bf16[1,128,512]{2,1,0:T(8,128)(2,1)S(1)}, bf16[1,128,512]{2,1,0:T(8,128)(2,1)S(1)}, u32[]{:S(2)}, u32[]{:S(2)}) collective-permute-start(bf16[1,128,512]{2,1,0:T(8,128)(2,1)S(1)} %get-tuple-element.31), channel_id=1, source_target_pairs={{0,23},{1,22},{2,21},{3,20},{4,19},{5,18},{6,17},{7,16},{8,3},{9,2... | collective-permute-start | bytes 393224 | tf_op jit(solution)/shard_map/ppermute | solution.py:412
  16.4 16.3 %collective-permute-start.14 = (bf16[1,128,512]{2,1,0:T(8,128)(2,1)S(1)}, bf16[1,128,512]{2,1,0:T(8,128)(2,1)S(1)}, u32[]{:S(2)}, u32[]{:S(2)}) collective-permute-start(bf16[1,128,512]{2,1,0:T(8,128)(2,1)S(1)} %get-tuple-element.32), channel_id=1, source_target_pairs={{0,7},{1,6},{2,5},{3,4},{4,3},{5,2},{6,1},{7,0},{8,19},{9,18},{10,... | collective-permute-start | bytes 393224 | tf_op jit(solution)/shard_map/ppermute | solution.py:412
  19.1 15.9 %collective-permute-start.13 = (bf16[1,128,512]{2,1,0:T(8,128)(2,1)S(1)}, bf16[1,128,512]{2,1,0:T(8,128)(2,1)S(1)}, u32[]{:S(2)}, u32[]{:S(2)}) collective-permute-start(bf16[1,128,512]{2,1,0:T(8,128)(2,1)S(1)} %get-tuple-element.33), channel_id=1, source_target_pairs={{0,22},{1,23},{2,20},{3,21},{4,18},{5,19},{6,16},{7,17},{8,2},{9,3... | collective-permute-start | bytes 393224 | tf_op jit(solution)/shard_map/ppermute | solution.py:412
  23.7 13.2 %collective-permute-start.12 = (bf16[1,128,512]{2,1,0:T(8,128)(2,1)S(1)}, bf16[1,128,512]{2,1,0:T(8,128)(2,1)S(1)}, u32[]{:S(2)}, u32[]{:S(2)}) collective-permute-start(bf16[1,128,512]{2,1,0:T(8,128)(2,1)S(1)} %get-tuple-element.34), channel_id=1, source_target_pairs={{0,6},{1,7},{2,4},{3,5},{4,2},{5,3},{6,0},{7,1},{8,18},{9,19},{10,... | collective-permute-start | bytes 393224 | tf_op jit(solution)/shard_map/ppermute | solution.py:412
  27.3 13.0 %collective-permute-start.11 = (bf16[1,128,512]{2,1,0:T(8,128)(2,1)S(1)}, bf16[1,128,512]{2,1,0:T(8,128)(2,1)S(1)}, u32[]{:S(2)}, u32[]{:S(2)}) collective-permute-start(bf16[1,128,512]{2,1,0:T(8,128)(2,1)S(1)} %get-tuple-element.35), channel_id=1, source_target_pairs={{0,21},{1,20},{2,23},{3,22},{4,17},{5,16},{6,19},{7,18},{8,1},{9,0... | collective-permute-start | bytes 393224 | tf_op jit(solution)/shard_map/ppermute | solution.py:412
  27.3 14.0 %collective-permute-start.10 = (bf16[1,128,512]{2,1,0:T(8,128)(2,1)S(1)}, bf16[1,128,512]{2,1,0:T(8,128)(2,1)S(1)}, u32[]{:S(2)}, u32[]{:S(2)}) collective-permute-start(bf16[1,128,512]{2,1,0:T(8,128)(2,1)S(1)} %get-tuple-element.36), channel_id=1, source_target_pairs={{0,5},{1,4},{2,7},{3,6},{4,1},{5,0},{6,3},{7,2},{8,17},{9,16},{10,... | collective-permute-start | bytes 393224 | tf_op jit(solution)/shard_map/ppermute | solution.py:412
  32.7 8.6 %collective-permute-start.9 = (bf16[1,128,512]{2,1,0:T(8,128)(2,1)S(1)}, bf16[1,128,512]{2,1,0:T(8,128)(2,1)S(1)}, u32[]{:S(2)}, u32[]{:S(2)}) collective-permute-start(bf16[1,128,512]{2,1,0:T(8,128)(2,1)S(1)} %get-tuple-element.37), channel_id=1, source_target_pairs={{0,20},{1,21},{2,22},{3,23},{4,16},{5,17},{6,18},{7,19},{8,0},{9,1... | collective-permute-start | bytes 393224 | tf_op jit(solution)/shard_map/ppermute | solution.py:412
  35.0 8.4 %collective-permute-start.8 = (bf16[1,128,512]{2,1,0:T(8,128)(2,1)S(1)}, bf16[1,128,512]{2,1,0:T(8,128)(2,1)S(1)}, u32[]{:S(2)}, u32[]{:S(2)}) collective-permute-start(bf16[1,128,512]{2,1,0:T(8,128)(2,1)S(1)} %get-tuple-element.38), channel_id=1, source_target_pairs={{0,4},{1,5},{2,6},{3,7},{4,0},{5,1},{6,2},{7,3},{8,16},{9,17},{10,... | collective-permute-start | bytes 393224 | tf_op jit(solution)/shard_map/ppermute | solution.py:412
  36.9 10.5 %collective-permute-start.7 = (bf16[1,128,512]{2,1,0:T(8,128)(2,1)S(1)}, bf16[1,128,512]{2,1,0:T(8,128)(2,1)S(1)}, u32[]{:S(2)}, u32[]{:S(2)}) collective-permute-start(bf16[1,128,512]{2,1,0:T(8,128)(2,1)S(1)} %get-tuple-element.39), channel_id=1, source_target_pairs={{0,19},{1,18},{2,17},{3,16},{4,23},{5,22},{6,21},{7,20},{8,7},{9,6... | collective-permute-start | bytes 393224 | tf_op jit(solution)/shard_map/ppermute | solution.py:412
  40.2 9.0 %collective-permute-start.6 = (bf16[1,128,512]{2,1,0:T(8,128)(2,1)S(1)}, bf16[1,128,512]{2,1,0:T(8,128)(2,1)S(1)}, u32[]{:S(2)}, u32[]{:S(2)}) collective-permute-start(bf16[1,128,512]{2,1,0:T(8,128)(2,1)S(1)} %get-tuple-element.40), channel_id=1, source_target_pairs={{0,3},{1,2},{2,1},{3,0},{4,7},{5,6},{6,5},{7,4},{8,23},{9,22},{10,... | collective-permute-start | bytes 393224 | tf_op jit(solution)/shard_map/ppermute | solution.py:412
  49.4 2.1 %collective-permute-start.16 = (bf16[1024,128]{1,0:T(8,128)(2,1)S(1)}, bf16[1024,128]{1,0:T(8,128)(2,1)S(1)}, u32[]{:S(2)}, u32[]{:S(2)}) collective-permute-start(bf16[1024,128]{1,0:T(8,128)(2,1)S(1)} %edges.1), channel_id=1, source_target_pairs={{0,8},{8,0},{16,24},{24,16},{1,9},{9,1},{17,25},{25,17},{2,10},{10... | collective-permute-start | bytes 786440 | tf_op jit(solution)/shard_map/ppermute | solution.py:413
  56.5 22.9 %collective-permute-start.23 = (bf16[128,1024]{1,0:T(8,128)(2,1)S(1)}, bf16[128,1024]{1,0:T(8,128)(2,1)S(1)}, u32[]{:S(2)}, u32[]{:S(2)}) collective-permute-start(bf16[128,1024]{1,0:T(8,128)(2,1)S(1)} %get-tuple-element.29), channel_id=1, source_target_pairs={{0,2},{1,3},{2,0},{3,1},{4,10},{5,11},{6,8},{7,9},{8,6},{9,7},{10,... | collective-permute-start | bytes 786440 | tf_op jit(solution)/shard_map/ppermute | solution.py:424
  57.8 25.1 %collective-permute-start.24 = (bf16[128,1024]{1,0:T(8,128)(2,1)S(1)}, bf16[128,1024]{1,0:T(8,128)(2,1)S(1)}, u32[]{:S(2)}, u32[]{:S(2)}) collective-permute-start(bf16[128,1024]{1,0:T(8,128)(2,1)S(1)} %get-tuple-element.30), channel_id=1, source_target_pairs={{0,3},{1,2},{2,1},{3,0},{4,11},{5,10},{6,9},{7,8},{8,7},{9,6},{10,... | collective-permute-start | bytes 786440 | tf_op jit(solution)/shard_map/ppermute | solution.py:424
  63.8 19.1 %collective-permute-start.21 = (bf16[128,1024]{1,0:T(8,128)(2,1)S(1)}, bf16[128,1024]{1,0:T(8,128)(2,1)S(1)}, u32[]{:S(2)}, u32[]{:S(2)}) collective-permute-start(bf16[128,1024]{1,0:T(8,128)(2,1)S(1)} %get-tuple-element.27), channel_id=1, source_target_pairs={{0,0},{1,1},{2,2},{3,3},{4,8},{5,9},{6,10},{7,11},{8,4},{9,5},{10,... | collective-permute-start | bytes 786440 | tf_op jit(solution)/shard_map/ppermute | solution.py:424
  71.3 15.4 %collective-permute-start.22 = (bf16[128,1024]{1,0:T(8,128)(2,1)S(1)}, bf16[128,1024]{1,0:T(8,128)(2,1)S(1)}, u32[]{:S(2)}, u32[]{:S(2)}) collective-permute-start(bf16[128,1024]{1,0:T(8,128)(2,1)S(1)} %get-tuple-element.28), channel_id=1, source_target_pairs={{0,1},{1,0},{2,3},{3,2},{4,9},{5,8},{6,11},{7,10},{8,5},{9,4},{10,... | collective-permute-start | bytes 786440 | tf_op jit(solution)/shard_map/ppermute | solution.py:424
  79.3 8.9 %collective-permute-start.18 = (bf16[128,1024]{1,0:T(8,128)(2,1)S(1)}, bf16[128,1024]{1,0:T(8,128)(2,1)S(1)}, u32[]{:S(2)}, u32[]{:S(2)}) collective-permute-start(bf16[128,1024]{1,0:T(8,128)(2,1)S(1)} %get-tuple-element.24), channel_id=1, source_target_pairs={{0,4},{1,5},{2,6},{3,7},{4,12},{5,13},{6,14},{7,15},{8,0},{9,1},{1... | collective-permute-start | bytes 786440 | tf_op jit(solution)/shard_map/ppermute | solution.py:424
  79.4 11.9 %collective-permute-start.19 = (bf16[128,1024]{1,0:T(8,128)(2,1)S(1)}, bf16[128,1024]{1,0:T(8,128)(2,1)S(1)}, u32[]{:S(2)}, u32[]{:S(2)}) collective-permute-start(bf16[128,1024]{1,0:T(8,128)(2,1)S(1)} %get-tuple-element.25), channel_id=1, source_target_pairs={{0,5},{1,4},{2,7},{3,6},{4,13},{5,12},{6,15},{7,14},{8,1},{9,0},{1... | collective-permute-start | bytes 786440 | tf_op jit(solution)/shard_map/ppermute | solution.py:424
  82.9 20.3 %collective-permute-start.20 = (bf16[128,1024]{1,0:T(8,128)(2,1)S(1)}, bf16[128,1024]{1,0:T(8,128)(2,1)S(1)}, u32[]{:S(2)}, u32[]{:S(2)}) collective-permute-start(bf16[128,1024]{1,0:T(8,128)(2,1)S(1)} %get-tuple-element.26), channel_id=1, source_target_pairs={{0,6},{1,7},{2,4},{3,5},{4,14},{5,15},{6,12},{7,13},{8,2},{9,3},{1... | collective-permute-start | bytes 786440 | tf_op jit(solution)/shard_map/ppermute | solution.py:424
  82.9 23.7 %collective-permute-start.17 = (bf16[128,1024]{1,0:T(8,128)(2,1)S(1)}, bf16[128,1024]{1,0:T(8,128)(2,1)S(1)}, u32[]{:S(2)}, u32[]{:S(2)}) collective-permute-start(bf16[128,1024]{1,0:T(8,128)(2,1)S(1)} %get-tuple-element.23), channel_id=1, source_target_pairs={{0,7},{1,6},{2,5},{3,4},{4,15},{5,14},{6,13},{7,12},{8,3},{9,2},{1... | collective-permute-start | bytes 786440 | tf_op jit(solution)/shard_map/ppermute | solution.py:424

commit v7 on v6

--- a/solution.py
+++ b/solution.py
@@ -20,7 +20,7 @@
 TINY = 1e-30
 SHARES = (4, 4, 2)
 CHUNKS = 1
-PLACED = ((0, 4), (4, 7), (7, 8))
+PLACED = ((0, 7), (7, 8))
 VMEM_BYTES = 24 * 2**20
 FIRST_STEPS = 6
 

time: 108 us -> 108 us (level)
  waiting for transfers between devices: 30.7 us -> 32.3 us
  Pallas kernels: 21.5 us -> 20.3 us
    pallas_call x3 -> x2, Pallas kernels: 3.74 us -> 2.98 us  [place_pieces(): pl.pallas_call(functools.partial(place_kernel, first, count), in_specs=[p...]
  transfers between devices with their start and end apart: 25 -> 25, of which waited for: 10 -> 10; matrix products, arithmetic and copies ran while one was open for 2% -> 2% of each run, Pallas kernels for 14% -> 13%
where the time goes in v7:
time: 108 us
  starting transfers between devices  51.6 us (48%)
  waiting for transfers between devices  32.3 us (30%)
  Pallas kernels  20.3 us (19%)
  local copies, waits for them, and re-layouts  3 us (3%)
    ppermute x16, starting transfers between devices, by_planes(): pieces.append(lax.ppermute(piece, ('scan', 'ybrick'), route))  34.6 us
    ppermute x8, waiting for transfers between devices, by_planes(): arrived.append(lax.ppermute(piece, ('scan', 'ybrick'), route))  20.2 us
    pallas_call x3, Pallas kernels, deconvolve_rows(): pl.pallas_call(functools.partial(rows_kernel, bricks, first_k, count), ou...  16.9 us
    ppermute x8, starting transfers between devices, by_planes(): arrived.append(lax.ppermute(piece, ('scan', 'ybrick'), route))  15.9 us
    ppermute x16, waiting for transfers between devices, by_planes(): pieces.append(lax.ppermute(piece, ('scan', 'ybrick'), route))  11.5 us
    pallas_call x2, Pallas kernels, place_pieces(): pl.pallas_call(functools.partial(place_kernel, first, count), in_specs=[p...  2.98 us
    dynamic_slice x2, local copies, waits for them, and re-layouts, by_planes(): piece = lax.dynamic_slice_in_dim(raw, plane, 1, 0)  2.79 us
  transfers between devices with their start and end apart: 25, of which 10 were waited for; matrix products, arithmetic and copies ran while one was open for 2% of the time, Pallas kernels for 13%

profile of v7, /device:TPU:9, one launch (start us, length us, event | category | flops | bytes accessed | tf_op | source)
XLA Modules:
  0.0 107.6 jit_solution(7317846214506736458)
XLA Ops:
  0.0 1.3 %constant_dynamic-slice_fusion.10 = (bf16[1,128,512]{2,1,0:T(8,128)(2,1)S(1)}, bf16[1,128,512]{2,1,0:T(8,128)(2,1)S(1)}, bf16[1,128,512]{2,1,0:T(8,128)(2,1)S(1)...) fusion(bf16[16,128,512]{2,1,0:T(8,128)(2,1)} %param.5, ...), kind=kLoop, calls=%fused_computation.10 | loop fusion | bytes 1572888 | tf_op jit(solution)/shard_map/dynamic_slice | solution.py:405
  1.3 1.9 %collective-permute-start.5 = (bf16[1,128,512]{2,1,0:T(8,128)(2,1)S(1)}, bf16[1,128,512]{2,1,0:T(8,128)(2,1)S(1)}, u32[]{:S(2)}, u32[]{:S(2)}) collective-permute-start(bf16[1,128,512]{2,1,0:T(8,128)(2,1)S(1)} %get-tuple-element.41), channel_id=1, source_target_pairs={{0,18},{1,19},{2,16},{3,17},{4,22},{5,23},{6,20},{7,21},{8,6},{9,7... | collective-permute-start | bytes 393224 | tf_op jit(solution)/shard_map/ppermute | solution.py:412
  3.2 2.0 %collective-permute-start.4 = (bf16[1,128,512]{2,1,0:T(8,128)(2,1)S(1)}, bf16[1,128,512]{2,1,0:T(8,128)(2,1)S(1)}, u32[]{:S(2)}, u32[]{:S(2)}) collective-permute-start(bf16[1,128,512]{2,1,0:T(8,128)(2,1)S(1)} %get-tuple-element.42), channel_id=1, source_target_pairs={{0,2},{1,3},{2,0},{3,1},{4,6},{5,7},{6,4},{7,5},{8,22},{9,23},{10,... | collective-permute-start | bytes 393224 | tf_op jit(solution)/shard_map/ppermute | solution.py:412
  5.2 3.0 %collective-permute-start.3 = (bf16[1,128,512]{2,1,0:T(8,128)(2,1)S(1)}, bf16[1,128,512]{2,1,0:T(8,128)(2,1)S(1)}, u32[]{:S(2)}, u32[]{:S(2)}) collective-permute-start(bf16[1,128,512]{2,1,0:T(8,128)(2,1)S(1)} %get-tuple-element.43), channel_id=1, source_target_pairs={{0,17},{1,16},{2,19},{3,18},{4,21},{5,20},{6,23},{7,22},{8,5},{9,4... | collective-permute-start | bytes 393224 | tf_op jit(solution)/shard_map/ppermute | solution.py:412
  8.1 1.2 %collective-permute-start.2 = (bf16[1,128,512]{2,1,0:T(8,128)(2,1)S(1)}, bf16[1,128,512]{2,1,0:T(8,128)(2,1)S(1)}, u32[]{:S(2)}, u32[]{:S(2)}) collective-permute-start(bf16[1,128,512]{2,1,0:T(8,128)(2,1)S(1)} %get-tuple-element.44), channel_id=1, source_target_pairs={{0,1},{1,0},{2,3},{3,2},{4,5},{5,4},{6,7},{7,6},{8,21},{9,20},{10,... | collective-permute-start | bytes 393224 | tf_op jit(solution)/shard_map/ppermute | solution.py:412
  9.3 0.0 collective-permute-start.1
  9.3 0.0 copy-start.1
  9.3 0.0 collective-permute-done.5.refs_5_
  9.3 5.4 %collective-permute-start = (bf16[1,128,512]{2,1,0:T(8,128)(2,1)S(1)}, bf16[1,128,512]{2,1,0:T(8,128)(2,1)S(1)}, u32[]{:S(2)}, u32[]{:S(2)}) collective-permute-start(bf16[1,128,512]{2,1,0:T(8,128)(2,1)S(1)} %get-tuple-element.46), channel_id=1, source_target_pairs={{0,0},{1,1},{2,2},{3,3},{4,4},{5,5},{6,6},{7,7},{8,20},{9,21},{10,... | collective-permute-start | bytes 393224 | tf_op jit(solution)/shard_map/ppermute | solution.py:412
  14.7 1.5 %constant_dynamic-slice_fusion = (bf16[1,128,512]{2,1,0:T(8,128)(2,1)S(1)}, bf16[1,128,512]{2,1,0:T(8,128)(2,1)S(1)}, bf16[1,128,512]{2,1,0:T(8,128)(2,1)S(1)}, ...) fusion(bf16[16,128,512]{2,1,0:T(8,128)(2,1)} %param.5, ...), kind=kLoop, calls=%fused_computation | loop fusion | bytes 2621480 | tf_op jit(solution)/shard_map/dynamic_slice | solution.py:405
  16.2 0.0 collective-permute-done.4.refs_4_
  16.2 0.1 collective-permute-start.15
  16.3 0.0 collective-permute-done.3.refs_3_
  16.3 2.9 %collective-permute-start.14 = (bf16[1,128,512]{2,1,0:T(8,128)(2,1)S(1)}, bf16[1,128,512]{2,1,0:T(8,128)(2,1)S(1)}, u32[]{:S(2)}, u32[]{:S(2)}) collective-permute-start(bf16[1,128,512]{2,1,0:T(8,128)(2,1)S(1)} %get-tuple-element.32), channel_id=1, source_target_pairs={{0,7},{1,6},{2,5},{3,4},{4,3},{5,2},{6,1},{7,0},{8,19},{9,18},{10,... | collective-permute-start | bytes 393224 | tf_op jit(solution)/shard_map/ppermute | solution.py:412
  19.2 0.0 collective-permute-done.2.refs_2_
  19.2 2.1 %collective-permute-start.13 = (bf16[1,128,512]{2,1,0:T(8,128)(2,1)S(1)}, bf16[1,128,512]{2,1,0:T(8,128)(2,1)S(1)}, u32[]{:S(2)}, u32[]{:S(2)}) collective-permute-start(bf16[1,128,512]{2,1,0:T(8,128)(2,1)S(1)} %get-tuple-element.33), channel_id=1, source_target_pairs={{0,22},{1,23},{2,20},{3,21},{4,18},{5,19},{6,16},{7,17},{8,2},{9,3... | collective-permute-start | bytes 393224 | tf_op jit(solution)/shard_map/ppermute | solution.py:412
  21.3 2.4 %collective-permute-done.1.refs_1_ = bf16[1,128,512]{2,1,0:T(8,128)(2,1)S(1)} collective-permute-done((bf16[1,128,512]{2,1,0:T(8,128)(2,1)S(1)}, bf16[1,128,512]{2,1,0:T(8,128)(2,1)S(1)}, u32[]{:S(2)}, u32[]{:S(2)}) %collective-permute-start.1) | collective-permute-done | bytes 131104 | tf_op jit(solution)/shard_map/ppermute | solution.py:412
  23.6 2.4 %collective-permute-start.12 = (bf16[1,128,512]{2,1,0:T(8,128)(2,1)S(1)}, bf16[1,128,512]{2,1,0:T(8,128)(2,1)S(1)}, u32[]{:S(2)}, u32[]{:S(2)}) collective-permute-start(bf16[1,128,512]{2,1,0:T(8,128)(2,1)S(1)} %get-tuple-element.34), channel_id=1, source_target_pairs={{0,6},{1,7},{2,4},{3,5},{4,2},{5,3},{6,0},{7,1},{8,18},{9,19},{10,... | collective-permute-start | bytes 393224 | tf_op jit(solution)/shard_map/ppermute | solution.py:412
  26.1 1.1 %collective-permute-done.refs_0_ = bf16[1,128,512]{2,1,0:T(8,128)(2,1)S(1)} collective-permute-done((bf16[1,128,512]{2,1,0:T(8,128)(2,1)S(1)}, bf16[1,128,512]{2,1,0:T(8,128)(2,1)S(1)}, u32[]{:S(2)}, u32[]{:S(2)}) %collective-permute-start) | collective-permute-done | bytes 131104 | tf_op jit(solution)/shard_map/ppermute | solution.py:412
  27.2 0.0 collective-permute-start.11
  27.2 0.0 collective-permute-done.15.refs_15_
  27.2 5.7 %collective-permute-start.10 = (bf16[1,128,512]{2,1,0:T(8,128)(2,1)S(1)}, bf16[1,128,512]{2,1,0:T(8,128)(2,1)S(1)}, u32[]{:S(2)}, u32[]{:S(2)}) collective-permute-start(bf16[1,128,512]{2,1,0:T(8,128)(2,1)S(1)} %get-tuple-element.36), channel_id=1, source_target_pairs={{0,5},{1,4},{2,7},{3,6},{4,1},{5,0},{6,3},{7,2},{8,17},{9,16},{10,... | collective-permute-start | bytes 393224 | tf_op jit(solution)/shard_map/ppermute | solution.py:412
  32.9 0.0 collective-permute-done.14.refs_14_
  32.9 2.0 %collective-permute-start.9 = (bf16[1,128,512]{2,1,0:T(8,128)(2,1)S(1)}, bf16[1,128,512]{2,1,0:T(8,128)(2,1)S(1)}, u32[]{:S(2)}, u32[]{:S(2)}) collective-permute-start(bf16[1,128,512]{2,1,0:T(8,128)(2,1)S(1)} %get-tuple-element.37), channel_id=1, source_target_pairs={{0,20},{1,21},{2,22},{3,23},{4,16},{5,17},{6,18},{7,19},{8,0},{9,1... | collective-permute-start | bytes 393224 | tf_op jit(solution)/shard_map/ppermute | solution.py:412
  34.9 0.0 collective-permute-done.13.refs_13_
  34.9 1.9 %collective-permute-start.8 = (bf16[1,128,512]{2,1,0:T(8,128)(2,1)S(1)}, bf16[1,128,512]{2,1,0:T(8,128)(2,1)S(1)}, u32[]{:S(2)}, u32[]{:S(2)}) collective-permute-start(bf16[1,128,512]{2,1,0:T(8,128)(2,1)S(1)} %get-tuple-element.38), channel_id=1, source_target_pairs={{0,4},{1,5},{2,6},{3,7},{4,0},{5,1},{6,2},{7,3},{8,16},{9,17},{10,... | collective-permute-start | bytes 393224 | tf_op jit(solution)/shard_map/ppermute | solution.py:412
  36.8 0.0 collective-permute-done.12.refs_12_
  36.8 3.2 %collective-permute-start.7 = (bf16[1,128,512]{2,1,0:T(8,128)(2,1)S(1)}, bf16[1,128,512]{2,1,0:T(8,128)(2,1)S(1)}, u32[]{:S(2)}, u32[]{:S(2)}) collective-permute-start(bf16[1,128,512]{2,1,0:T(8,128)(2,1)S(1)} %get-tuple-element.39), channel_id=1, source_target_pairs={{0,19},{1,18},{2,17},{3,16},{4,23},{5,22},{6,21},{7,20},{8,7},{9,6... | collective-permute-start | bytes 393224 | tf_op jit(solution)/shard_map/ppermute | solution.py:412
  40.0 0.0 collective-permute-done.11.refs_11_
  40.0 1.1 collective-permute-start.6
  41.1 0.0 collective-permute-done.10.refs_10_
  41.1 0.0 collective-permute-done.9.refs_9_
  41.1 2.5 %collective-permute-done.8.refs_8_ = bf16[1,128,512]{2,1,0:T(8,128)(2,1)S(1)} collective-permute-done((bf16[1,128,512]{2,1,0:T(8,128)(2,1)S(1)}, bf16[1,128,512]{2,1,0:T(8,128)(2,1)S(1)}, u32[]{:S(2)}, u32[]{:S(2)}) %collective-permute-start.8) | collective-permute-done | bytes 131104 | tf_op jit(solution)/shard_map/ppermute | solution.py:412
  43.5 3.8 %collective-permute-done.7.refs_7_ = bf16[1,128,512]{2,1,0:T(8,128)(2,1)S(1)} collective-permute-done((bf16[1,128,512]{2,1,0:T(8,128)(2,1)S(1)}, bf16[1,128,512]{2,1,0:T(8,128)(2,1)S(1)}, u32[]{:S(2)}, u32[]{:S(2)}) %collective-permute-start.7) | collective-permute-done | bytes 131104 | tf_op jit(solution)/shard_map/ppermute | solution.py:412
  47.3 1.7 %collective-permute-done.6.refs_6_ = bf16[1,128,512]{2,1,0:T(8,128)(2,1)S(1)} collective-permute-done((bf16[1,128,512]{2,1,0:T(8,128)(2,1)S(1)}, bf16[1,128,512]{2,1,0:T(8,128)(2,1)S(1)}, u32[]{:S(2)}, u32[]{:S(2)}) %collective-permute-start.6) | collective-permute-done | bytes 131104 | tf_op jit(solution)/shard_map/ppermute | solution.py:412
  49.0 0.1 edges.1
  49.1 1.1 %collective-permute-start.16 = (bf16[1024,128]{1,0:T(8,128)(2,1)S(1)}, bf16[1024,128]{1,0:T(8,128)(2,1)S(1)}, u32[]{:S(2)}, u32[]{:S(2)}) collective-permute-start(bf16[1024,128]{1,0:T(8,128)(2,1)S(1)} %edges.1), channel_id=1, source_target_pairs={{0,8},{8,0},{16,24},{24,16},{1,9},{9,1},{17,25},{25,17},{2,10},{10... | collective-permute-start | bytes 786440 | tf_op jit(solution)/shard_map/ppermute | solution.py:413
  50.3 0.0 copy-done.2
  50.3 0.1 rev.7
  50.4 0.1 rev.6
  50.5 0.2 band_matrices.1
  50.7 0.7 collective-permute-done.16.refs_16_
  51.4 0.0 copy-done.1
  51.4 4.9 %deconvolve_rows.5 = (bf16[128,1024]{1,0:T(8,128)(2,1)S(1)}, bf16[128,1024]{1,0:T(8,128)(2,1)S(1)}) custom-call(s32[16]{0:T(128)S(1)} %copy-done, s32[16]{0:T(128)S(1)} %copy-done.1, bf16[1,128,512]{2,1,0:T(8,128)(2,1)S(1)} %collective-permute-done.refs_0_, bf16[1,128,512]{2,1,0:T(8,128)(2,1)S(1)} %collective-permute-done.1.refs_1_, ...), custom_call_target="tpu_custom_call" | custom-call | tf_op jit(solution)/shard_map/deconvolve_rows/pallas_call | solution.py:293
  56.3 1.3 %collective-permute-start.20 = (bf16[128,1024]{1,0:T(8,128)(2,1)S(1)}, bf16[128,1024]{1,0:T(8,128)(2,1)S(1)}, u32[]{:S(2)}, u32[]{:S(2)}) collective-permute-start(bf16[128,1024]{1,0:T(8,128)(2,1)S(1)} %get-tuple-element.26), channel_id=1, source_target_pairs={{0,2},{1,3},{2,0},{3,1},{4,10},{5,11},{6,8},{7,9},{8,6},{9,7},{10,... | collective-permute-start | bytes 786440 | tf_op jit(solution)/shard_map/ppermute | solution.py:424
  57.7 1.1 collective-permute-start.21
  58.7 4.9 %deconvolve_rows.4 = (bf16[128,1024]{1,0:T(8,128)(2,1)S(1)}, bf16[128,1024]{1,0:T(8,128)(2,1)S(1)}) custom-call(s32[16]{0:T(128)S(1)} %copy-done, s32[16]{0:T(128)S(1)} %copy-done.1, bf16[1,128,512]{2,1,0:T(8,128)(2,1)S(1)} %collective-permute-done.refs_0_, bf16[1,128,512]{2,1,0:T(8,128)(2,1)S(1)} %collective-permute-done.1.refs_1_, ...), custom_call_target="tpu_custom_call" | custom-call | tf_op jit(solution)/shard_map/deconvolve_rows/pallas_call | solution.py:293
  63.6 7.2 %collective-permute-start.18 = (bf16[128,1024]{1,0:T(8,128)(2,1)S(1)}, bf16[128,1024]{1,0:T(8,128)(2,1)S(1)}, u32[]{:S(2)}, u32[]{:S(2)}) collective-permute-start(bf16[128,1024]{1,0:T(8,128)(2,1)S(1)} %get-tuple-element.24), channel_id=1, source_target_pairs={{0,0},{1,1},{2,2},{3,3},{4,8},{5,9},{6,10},{7,11},{8,4},{9,5},{10,... | collective-permute-start | bytes 786440 | tf_op jit(solution)/shard_map/ppermute | solution.py:424
  70.8 0.9 collective-permute-start.19
  71.8 7.2 %deconvolve_rows.3 = (bf16[128,1024]{1,0:T(8,128)(2,1)S(1)}, bf16[128,1024]{1,0:T(8,128)(2,1)S(1)}, bf16[128,1024]{1,0:T(8,128)(2,1)S(1)}, bf16[128,1024]{1,0:T(8,128)(2,1)S(1)}) custom-call(s32[16]{0:T(128)S(1)} %copy-done, s32[16]{0:T(128)S(1)} %copy-done.1, bf16[1,128,512]{2,1,0:T(8,128)(2,1)S(1)} %collective-permute-done.refs_0_, ...), custom_call_target="tpu_custom_call" | custom-call | tf_op jit(solution)/shard_map/deconvolve_rows/pallas_call | solution.py:293
  78.9 0.1 collective-permute-start.22
  79.0 0.0 collective-permute-done.20.refs_2_
  79.0 3.2 %collective-permute-start.23 = (bf16[128,1024]{1,0:T(8,128)(2,1)S(1)}, bf16[128,1024]{1,0:T(8,128)(2,1)S(1)}, u32[]{:S(2)}, u32[]{:S(2)}) collective-permute-start(bf16[128,1024]{1,0:T(8,128)(2,1)S(1)} %get-tuple-element.29), channel_id=1, source_target_pairs={{0,5},{1,4},{2,7},{3,6},{4,13},{5,12},{6,15},{7,14},{8,1},{9,0},{1... | collective-permute-start | bytes 786440 | tf_op jit(solution)/shard_map/ppermute | solution.py:424
  82.2 0.0 collective-permute-done.21.refs_3_
  82.2 0.0 collective-permute-start.24
  82.2 0.0 collective-permute-done.18.refs_0_
  82.3 2.0 %collective-permute-start.17 = (bf16[128,1024]{1,0:T(8,128)(2,1)S(1)}, bf16[128,1024]{1,0:T(8,128)(2,1)S(1)}, u32[]{:S(2)}, u32[]{:S(2)}) collective-permute-start(bf16[128,1024]{1,0:T(8,128)(2,1)S(1)} %get-tuple-element.23), channel_id=1, source_target_pairs={{0,7},{1,6},{2,5},{3,4},{4,15},{5,14},{6,13},{7,12},{8,3},{9,2},{1... | collective-permute-start | bytes 786440 | tf_op jit(solution)/shard_map/ppermute | solution.py:424
  84.3 2.7 %collective-permute-done.19.refs_1_ = bf16[128,1024]{1,0:T(8,128)(2,1)S(1)} collective-permute-done((bf16[128,1024]{1,0:T(8,128)(2,1)S(1)}, bf16[128,1024]{1,0:T(8,128)(2,1)S(1)}, u32[]{:S(2)}, u32[]{:S(2)}) %collective-permute-start.19) | collective-permute-done | bytes 262176 | tf_op jit(solution)/shard_map/ppermute | solution.py:424
  87.0 0.0 collective-permute-done.22.refs_4_
  87.0 3.6 %collective-permute-done.23.refs_5_ = bf16[128,1024]{1,0:T(8,128)(2,1)S(1)} collective-permute-done((bf16[128,1024]{1,0:T(8,128)(2,1)S(1)}, bf16[128,1024]{1,0:T(8,128)(2,1)S(1)}, u32[]{:S(2)}, u32[]{:S(2)}) %collective-permute-start.23) | collective-permute-done | bytes 262176 | tf_op jit(solution)/shard_map/ppermute | solution.py:424
  90.6 12.6 %collective-permute-done.24.refs_6_ = bf16[128,1024]{1,0:T(8,128)(2,1)S(1)} collective-permute-done((bf16[128,1024]{1,0:T(8,128)(2,1)S(1)}, bf16[128,1024]{1,0:T(8,128)(2,1)S(1)}, u32[]{:S(2)}, u32[]{:S(2)}) %collective-permute-start.24) | collective-permute-done | bytes 262176 | tf_op jit(solution)/shard_map/ppermute | solution.py:424
  103.2 2.0 %place_pieces.2.refs_1_ = f32[4,128,2048]{2,1,0:T(8,128)} custom-call(bf16[128,1024]{1,0:T(8,128)(2,1)S(1)} %collective-permute-done.18.refs_0_, bf16[128,1024]{1,0:T(8,128)(2,1)S(1)} %collective-permute-done.19.refs_1_, bf16[128,1024]{1,0:T(8,128)(2,1)S(1)} %collective-permute-done.20.refs_2_, bf16[128,1024]{1,0:T(8,128)(2,1)S(1)} %collective-permute-done.21.refs_3_, ...), custom_call_target="tpu_custom_call" | custom-call | tf_op jit(solution)/shard_map/place_pieces/pallas_call | solution.py:372
  105.3 1.2 %collective-permute-done.17.refs_0_ = bf16[128,1024]{1,0:T(8,128)(2,1)S(1)} collective-permute-done((bf16[128,1024]{1,0:T(8,128)(2,1)S(1)}, bf16[128,1024]{1,0:T(8,128)(2,1)S(1)}, u32[]{:S(2)}, u32[]{:S(2)}) %collective-permute-start.17) | collective-permute-done | bytes 262176 | tf_op jit(solution)/shard_map/ppermute | solution.py:424
  106.5 0.9 place_pieces.3
  (6 shorter events, 0.0 us)
Async XLA Ops:
  1.3 8.0 %collective-permute-start.5 = (bf16[1,128,512]{2,1,0:T(8,128)(2,1)S(1)}, bf16[1,128,512]{2,1,0:T(8,128)(2,1)S(1)}, u32[]{:S(2)}, u32[]{:S(2)}) collective-permute-start(bf16[1,128,512]{2,1,0:T(8,128)(2,1)S(1)} %get-tuple-element.41), channel_id=1, source_target_pairs={{0,18},{1,19},{2,16},{3,17},{4,22},{5,23},{6,20},{7,21},{8,6},{9,7... | collective-permute-start | bytes 393224 | tf_op jit(solution)/shard_map/ppermute | solution.py:412
  3.2 13.0 %collective-permute-start.4 = (bf16[1,128,512]{2,1,0:T(8,128)(2,1)S(1)}, bf16[1,128,512]{2,1,0:T(8,128)(2,1)S(1)}, u32[]{:S(2)}, u32[]{:S(2)}) collective-permute-start(bf16[1,128,512]{2,1,0:T(8,128)(2,1)S(1)} %get-tuple-element.42), channel_id=1, source_target_pairs={{0,2},{1,3},{2,0},{3,1},{4,6},{5,7},{6,4},{7,5},{8,22},{9,23},{10,... | collective-permute-start | bytes 393224 | tf_op jit(solution)/shard_map/ppermute | solution.py:412
  5.2 11.1 %collective-permute-start.3 = (bf16[1,128,512]{2,1,0:T(8,128)(2,1)S(1)}, bf16[1,128,512]{2,1,0:T(8,128)(2,1)S(1)}, u32[]{:S(2)}, u32[]{:S(2)}) collective-permute-start(bf16[1,128,512]{2,1,0:T(8,128)(2,1)S(1)} %get-tuple-element.43), channel_id=1, source_target_pairs={{0,17},{1,16},{2,19},{3,18},{4,21},{5,20},{6,23},{7,22},{8,5},{9,4... | collective-permute-start | bytes 393224 | tf_op jit(solution)/shard_map/ppermute | solution.py:412
  8.1 11.0 %collective-permute-start.2 = (bf16[1,128,512]{2,1,0:T(8,128)(2,1)S(1)}, bf16[1,128,512]{2,1,0:T(8,128)(2,1)S(1)}, u32[]{:S(2)}, u32[]{:S(2)}) collective-permute-start(bf16[1,128,512]{2,1,0:T(8,128)(2,1)S(1)} %get-tuple-element.44), channel_id=1, source_target_pairs={{0,1},{1,0},{2,3},{3,2},{4,5},{5,4},{6,7},{7,6},{8,21},{9,20},{10,... | collective-permute-start | bytes 393224 | tf_op jit(solution)/shard_map/ppermute | solution.py:412
  9.3 14.4 %collective-permute-start.1 = (bf16[1,128,512]{2,1,0:T(8,128)(2,1)S(1)}, bf16[1,128,512]{2,1,0:T(8,128)(2,1)S(1)}, u32[]{:S(2)}, u32[]{:S(2)}) collective-permute-start(bf16[1,128,512]{2,1,0:T(8,128)(2,1)S(1)} %get-tuple-element.45), channel_id=1, source_target_pairs={{0,16},{1,17},{2,18},{3,19},{4,20},{5,21},{6,22},{7,23},{8,4},{9,5... | collective-permute-start | bytes 393224 | tf_op jit(solution)/shard_map/ppermute | solution.py:412
  9.3 41.0 %copy-start.2 = (f32[65]{0:T(128)S(1)}, f32[65]{0:T(128)}, u32[]{:S(2)}) copy-start(f32[65]{0:T(128)} %param.8) | copy-start | bytes 784
  9.3 41.1 %copy-start.3 = (f32[65]{0:T(128)S(1)}, f32[65]{0:T(128)}, u32[]{:S(2)}) copy-start(f32[65]{0:T(128)} %param.9) | copy-start | bytes 784
  9.3 42.1 %copy-start = (s32[16]{0:T(128)S(1)}, s32[16]{0:T(128)}, u32[]{:S(2)}) copy-start(s32[16]{0:T(128)} %row_shift.5) | copy-start | bytes 196
  9.3 42.1 %copy-start.1 = (s32[16]{0:T(128)S(1)}, s32[16]{0:T(128)}, u32[]{:S(2)}) copy-start(s32[16]{0:T(128)} %frac_index.5) | copy-start | bytes 196
  9.3 17.9 %collective-permute-start = (bf16[1,128,512]{2,1,0:T(8,128)(2,1)S(1)}, bf16[1,128,512]{2,1,0:T(8,128)(2,1)S(1)}, u32[]{:S(2)}, u32[]{:S(2)}) collective-permute-start(bf16[1,128,512]{2,1,0:T(8,128)(2,1)S(1)} %get-tuple-element.46), channel_id=1, source_target_pairs={{0,0},{1,1},{2,2},{3,3},{4,4},{5,5},{6,6},{7,7},{8,20},{9,21},{10,... | collective-permute-start | bytes 393224 | tf_op jit(solution)/shard_map/ppermute | solution.py:412
  16.2 11.0 %collective-permute-start.15 = (bf16[1,128,512]{2,1,0:T(8,128)(2,1)S(1)}, bf16[1,128,512]{2,1,0:T(8,128)(2,1)S(1)}, u32[]{:S(2)}, u32[]{:S(2)}) collective-permute-start(bf16[1,128,512]{2,1,0:T(8,128)(2,1)S(1)} %get-tuple-element.31), channel_id=1, source_target_pairs={{0,23},{1,22},{2,21},{3,20},{4,19},{5,18},{6,17},{7,16},{8,3},{9,2... | collective-permute-start | bytes 393224 | tf_op jit(solution)/shard_map/ppermute | solution.py:412
  16.3 16.6 %collective-permute-start.14 = (bf16[1,128,512]{2,1,0:T(8,128)(2,1)S(1)}, bf16[1,128,512]{2,1,0:T(8,128)(2,1)S(1)}, u32[]{:S(2)}, u32[]{:S(2)}) collective-permute-start(bf16[1,128,512]{2,1,0:T(8,128)(2,1)S(1)} %get-tuple-element.32), channel_id=1, source_target_pairs={{0,7},{1,6},{2,5},{3,4},{4,3},{5,2},{6,1},{7,0},{8,19},{9,18},{10,... | collective-permute-start | bytes 393224 | tf_op jit(solution)/shard_map/ppermute | solution.py:412
  19.2 15.7 %collective-permute-start.13 = (bf16[1,128,512]{2,1,0:T(8,128)(2,1)S(1)}, bf16[1,128,512]{2,1,0:T(8,128)(2,1)S(1)}, u32[]{:S(2)}, u32[]{:S(2)}) collective-permute-start(bf16[1,128,512]{2,1,0:T(8,128)(2,1)S(1)} %get-tuple-element.33), channel_id=1, source_target_pairs={{0,22},{1,23},{2,20},{3,21},{4,18},{5,19},{6,16},{7,17},{8,2},{9,3... | collective-permute-start | bytes 393224 | tf_op jit(solution)/shard_map/ppermute | solution.py:412
  23.6 13.2 %collective-permute-start.12 = (bf16[1,128,512]{2,1,0:T(8,128)(2,1)S(1)}, bf16[1,128,512]{2,1,0:T(8,128)(2,1)S(1)}, u32[]{:S(2)}, u32[]{:S(2)}) collective-permute-start(bf16[1,128,512]{2,1,0:T(8,128)(2,1)S(1)} %get-tuple-element.34), channel_id=1, source_target_pairs={{0,6},{1,7},{2,4},{3,5},{4,2},{5,3},{6,0},{7,1},{8,18},{9,19},{10,... | collective-permute-start | bytes 393224 | tf_op jit(solution)/shard_map/ppermute | solution.py:412
  27.2 12.8 %collective-permute-start.11 = (bf16[1,128,512]{2,1,0:T(8,128)(2,1)S(1)}, bf16[1,128,512]{2,1,0:T(8,128)(2,1)S(1)}, u32[]{:S(2)}, u32[]{:S(2)}) collective-permute-start(bf16[1,128,512]{2,1,0:T(8,128)(2,1)S(1)} %get-tuple-element.35), channel_id=1, source_target_pairs={{0,21},{1,20},{2,23},{3,22},{4,17},{5,16},{6,19},{7,18},{8,1},{9,0... | collective-permute-start | bytes 393224 | tf_op jit(solution)/shard_map/ppermute | solution.py:412
  27.2 13.8 %collective-permute-start.10 = (bf16[1,128,512]{2,1,0:T(8,128)(2,1)S(1)}, bf16[1,128,512]{2,1,0:T(8,128)(2,1)S(1)}, u32[]{:S(2)}, u32[]{:S(2)}) collective-permute-start(bf16[1,128,512]{2,1,0:T(8,128)(2,1)S(1)} %get-tuple-element.36), channel_id=1, source_target_pairs={{0,5},{1,4},{2,7},{3,6},{4,1},{5,0},{6,3},{7,2},{8,17},{9,16},{10,... | collective-permute-start | bytes 393224 | tf_op jit(solution)/shard_map/ppermute | solution.py:412
  32.9 8.1 %collective-permute-start.9 = (bf16[1,128,512]{2,1,0:T(8,128)(2,1)S(1)}, bf16[1,128,512]{2,1,0:T(8,128)(2,1)S(1)}, u32[]{:S(2)}, u32[]{:S(2)}) collective-permute-start(bf16[1,128,512]{2,1,0:T(8,128)(2,1)S(1)} %get-tuple-element.37), channel_id=1, source_target_pairs={{0,20},{1,21},{2,22},{3,23},{4,16},{5,17},{6,18},{7,19},{8,0},{9,1... | collective-permute-start | bytes 393224 | tf_op jit(solution)/shard_map/ppermute | solution.py:412
  34.9 8.6 %collective-permute-start.8 = (bf16[1,128,512]{2,1,0:T(8,128)(2,1)S(1)}, bf16[1,128,512]{2,1,0:T(8,128)(2,1)S(1)}, u32[]{:S(2)}, u32[]{:S(2)}) collective-permute-start(bf16[1,128,512]{2,1,0:T(8,128)(2,1)S(1)} %get-tuple-element.38), channel_id=1, source_target_pairs={{0,4},{1,5},{2,6},{3,7},{4,0},{5,1},{6,2},{7,3},{8,16},{9,17},{10,... | collective-permute-start | bytes 393224 | tf_op jit(solution)/shard_map/ppermute | solution.py:412
  36.8 10.5 %collective-permute-start.7 = (bf16[1,128,512]{2,1,0:T(8,128)(2,1)S(1)}, bf16[1,128,512]{2,1,0:T(8,128)(2,1)S(1)}, u32[]{:S(2)}, u32[]{:S(2)}) collective-permute-start(bf16[1,128,512]{2,1,0:T(8,128)(2,1)S(1)} %get-tuple-element.39), channel_id=1, source_target_pairs={{0,19},{1,18},{2,17},{3,16},{4,23},{5,22},{6,21},{7,20},{8,7},{9,6... | collective-permute-start | bytes 393224 | tf_op jit(solution)/shard_map/ppermute | solution.py:412
  40.0 9.0 %collective-permute-start.6 = (bf16[1,128,512]{2,1,0:T(8,128)(2,1)S(1)}, bf16[1,128,512]{2,1,0:T(8,128)(2,1)S(1)}, u32[]{:S(2)}, u32[]{:S(2)}) collective-permute-start(bf16[1,128,512]{2,1,0:T(8,128)(2,1)S(1)} %get-tuple-element.40), channel_id=1, source_target_pairs={{0,3},{1,2},{2,1},{3,0},{4,7},{5,6},{6,5},{7,4},{8,23},{9,22},{10,... | collective-permute-start | bytes 393224 | tf_op jit(solution)/shard_map/ppermute | solution.py:412
  49.1 2.3 %collective-permute-start.16 = (bf16[1024,128]{1,0:T(8,128)(2,1)S(1)}, bf16[1024,128]{1,0:T(8,128)(2,1)S(1)}, u32[]{:S(2)}, u32[]{:S(2)}) collective-permute-start(bf16[1024,128]{1,0:T(8,128)(2,1)S(1)} %edges.1), channel_id=1, source_target_pairs={{0,8},{8,0},{16,24},{24,16},{1,9},{9,1},{17,25},{25,17},{2,10},{10... | collective-permute-start | bytes 786440 | tf_op jit(solution)/shard_map/ppermute | solution.py:413
  56.3 22.7 %collective-permute-start.20 = (bf16[128,1024]{1,0:T(8,128)(2,1)S(1)}, bf16[128,1024]{1,0:T(8,128)(2,1)S(1)}, u32[]{:S(2)}, u32[]{:S(2)}) collective-permute-start(bf16[128,1024]{1,0:T(8,128)(2,1)S(1)} %get-tuple-element.26), channel_id=1, source_target_pairs={{0,2},{1,3},{2,0},{3,1},{4,10},{5,11},{6,8},{7,9},{8,6},{9,7},{10,... | collective-permute-start | bytes 786440 | tf_op jit(solution)/shard_map/ppermute | solution.py:424
  57.7 24.6 %collective-permute-start.21 = (bf16[128,1024]{1,0:T(8,128)(2,1)S(1)}, bf16[128,1024]{1,0:T(8,128)(2,1)S(1)}, u32[]{:S(2)}, u32[]{:S(2)}) collective-permute-start(bf16[128,1024]{1,0:T(8,128)(2,1)S(1)} %get-tuple-element.27), channel_id=1, source_target_pairs={{0,3},{1,2},{2,1},{3,0},{4,11},{5,10},{6,9},{7,8},{8,7},{9,6},{10,... | collective-permute-start | bytes 786440 | tf_op jit(solution)/shard_map/ppermute | solution.py:424
  63.6 18.6 %collective-permute-start.18 = (bf16[128,1024]{1,0:T(8,128)(2,1)S(1)}, bf16[128,1024]{1,0:T(8,128)(2,1)S(1)}, u32[]{:S(2)}, u32[]{:S(2)}) collective-permute-start(bf16[128,1024]{1,0:T(8,128)(2,1)S(1)} %get-tuple-element.24), channel_id=1, source_target_pairs={{0,0},{1,1},{2,2},{3,3},{4,8},{5,9},{6,10},{7,11},{8,4},{9,5},{10,... | collective-permute-start | bytes 786440 | tf_op jit(solution)/shard_map/ppermute | solution.py:424
  70.8 16.2 %collective-permute-start.19 = (bf16[128,1024]{1,0:T(8,128)(2,1)S(1)}, bf16[128,1024]{1,0:T(8,128)(2,1)S(1)}, u32[]{:S(2)}, u32[]{:S(2)}) collective-permute-start(bf16[128,1024]{1,0:T(8,128)(2,1)S(1)} %get-tuple-element.25), channel_id=1, source_target_pairs={{0,1},{1,0},{2,3},{3,2},{4,9},{5,8},{6,11},{7,10},{8,5},{9,4},{10,... | collective-permute-start | bytes 786440 | tf_op jit(solution)/shard_map/ppermute | solution.py:424
  78.9 8.1 %collective-permute-start.22 = (bf16[128,1024]{1,0:T(8,128)(2,1)S(1)}, bf16[128,1024]{1,0:T(8,128)(2,1)S(1)}, u32[]{:S(2)}, u32[]{:S(2)}) collective-permute-start(bf16[128,1024]{1,0:T(8,128)(2,1)S(1)} %get-tuple-element.28), channel_id=1, source_target_pairs={{0,4},{1,5},{2,6},{3,7},{4,12},{5,13},{6,14},{7,15},{8,0},{9,1},{1... | collective-permute-start | bytes 786440 | tf_op jit(solution)/shard_map/ppermute | solution.py:424
  79.0 11.6 %collective-permute-start.23 = (bf16[128,1024]{1,0:T(8,128)(2,1)S(1)}, bf16[128,1024]{1,0:T(8,128)(2,1)S(1)}, u32[]{:S(2)}, u32[]{:S(2)}) collective-permute-start(bf16[128,1024]{1,0:T(8,128)(2,1)S(1)} %get-tuple-element.29), channel_id=1, source_target_pairs={{0,5},{1,4},{2,7},{3,6},{4,13},{5,12},{6,15},{7,14},{8,1},{9,0},{1... | collective-permute-start | bytes 786440 | tf_op jit(solution)/shard_map/ppermute | solution.py:424
  82.2 21.0 %collective-permute-start.24 = (bf16[128,1024]{1,0:T(8,128)(2,1)S(1)}, bf16[128,1024]{1,0:T(8,128)(2,1)S(1)}, u32[]{:S(2)}, u32[]{:S(2)}) collective-permute-start(bf16[128,1024]{1,0:T(8,128)(2,1)S(1)} %get-tuple-element.30), channel_id=1, source_target_pairs={{0,6},{1,7},{2,4},{3,5},{4,14},{5,15},{6,12},{7,13},{8,2},{9,3},{1... | collective-permute-start | bytes 786440 | tf_op jit(solution)/shard_map/ppermute | solution.py:424
  82.3 24.2 %collective-permute-start.17 = (bf16[128,1024]{1,0:T(8,128)(2,1)S(1)}, bf16[128,1024]{1,0:T(8,128)(2,1)S(1)}, u32[]{:S(2)}, u32[]{:S(2)}) collective-permute-start(bf16[128,1024]{1,0:T(8,128)(2,1)S(1)} %get-tuple-element.23), channel_id=1, source_target_pairs={{0,7},{1,6},{2,5},{3,4},{4,15},{5,14},{6,13},{7,12},{8,3},{9,2},{1... | collective-permute-start | bytes 786440 | tf_op jit(solution)/shard_map/ppermute | solution.py:424
